TPU v7x, 32 devices: a whole 2x2x4 slice. The times are simulated.
32 devices in a mesh: lon: 8 (over z, y), lev: 4 (over x, core).
Axes of the slice: x: 2, y: 2, z: 4, core: 2. Of those that a mesh axis runs over, the one named last changes fastest.
Arguments:
- current_vector: float32 [16, 256, 512], P('lev', 'lon'), may hold values from -6 to 6
- previous_vector: float32 [16, 256, 512], P('lev', 'lon')
- beta_previous: float32 [], replicated, may hold values from 0.5 to 1.5
- stored_vectors: float32 [16, 16, 256, 512], P(None, 'lev', 'lon')
- velocity: float32 [2, 3, 16, 256, 512], P(None, None, 'lev', 'lon'), may hold values from -0.6 to 0.6
- level_weight: float32 [16], P('lev'), may hold values from 0.3 to 3
- box_owner: int32 [256, 512], P('lon'), may hold values from 0 to 5, as said below
Outputs:
- next_vector: float32 [16, 256, 512], P('lev', 'lon')
- lanczos_coefficients: float32 [18], replicated
Inputs may be any that keep to these rules, and one draw needn't show every extreme that they name: `box_owner`: each box is a rectangle in longitude (possibly across the date line) and latitude; a later box overwrites an earlier one where they meet; box 5 is present in every draw and spans more than half of the 256 longitude columns.
All inputs are finite; a program needn't handle non-finite values.
Results may differ from a plain program's by a relative error of at most 0.000076.
Values sent between devices are 32-bit elements; how exact they have to be, the bound alone decides.
No kernel may reach another device: no remote copies, remote signals or barrier semaphores. Data moves between devices by JAX's collectives and lax.ppermute only.
A program may use at most 64 MiB of HBM per device.

v0:
```python
import jax
import jax.numpy as jnp
from jax import lax
from jax.sharding import PartitionSpec as P

NBOX = 5


kappa_mix = 0.1
centre_coef = 1.0 - 6.0 * kappa_mix
highest = lax.Precision.HIGHEST


def extended(cells, sides, width, closed):
    for axis, dim in sides:
        count = lax.axis_size(axis)
        ends = count if closed else count - 1
        head = lax.slice_in_dim(cells, 0, width, axis=dim)
        tail = lax.slice_in_dim(cells, cells.shape[dim] - width, cells.shape[dim], axis=dim)
        cells = jnp.concatenate(
            [
                lax.ppermute(tail, axis, [(i, (i + 1) % count) for i in range(ends)]),
                cells,
                lax.ppermute(head, axis, [((i + 1) % count, i) for i in range(ends)]),
            ],
            axis=dim,
        )
    return cells


def coefficients(flow):
    return (
        kappa_mix - 0.5 * flow[0],
        kappa_mix + 0.5 * flow[0],
        kappa_mix - 0.5 * flow[1],
        kappa_mix + 0.5 * flow[1],
        kappa_mix - 0.5 * flow[2],
        kappa_mix + 0.5 * flow[2],
    )


def neighbours(stacked):
    zonal_padded = extended(stacked, (("lon", 2),), 1, True)
    layered = extended(stacked, (("lev", 1),), 1, False)
    return (zonal_padded[:, :, 2:], zonal_padded[:, :, :-2], layered[:, 2:], layered[:, :-2])


def meridional_adjoint(stencil, values):
    result = jnp.pad((stencil[2] * values)[:, :, :-1], ((0, 0), (0, 0), (1, 0)))
    return result + jnp.pad((stencil[3] * values)[:, :, 1:], ((0, 0), (0, 0), (0, 1)))


def tangent(values, flow):
    stencil = coefficients(flow)
    eastern, western, level_above, level_below = neighbours(values[None])
    northern = jnp.pad(values[:, :, 1:], ((0, 0), (0, 0), (0, 1)))
    southern = jnp.pad(values[:, :, :-1], ((0, 0), (0, 0), (1, 0)))
    return (
        centre_coef * values
        + stencil[0] * eastern[0]
        + stencil[1] * western[0]
        + stencil[2] * northern
        + stencil[3] * southern
        + stencil[4] * level_above[0]
        + stencil[5] * level_below[0]
    )


def adjoint_products(values, flow):
    stencil = coefficients(flow)
    stacked = jnp.stack(
        [stencil[0] * values, stencil[1] * values, stencil[4] * values, stencil[5] * values]
    )
    eastern, western, level_above, level_below = neighbours(stacked)
    result = centre_coef * values + western[0] + eastern[1] + level_below[2] + level_above[3]
    return result + meridional_adjoint(stencil, values)


def body(
    current_vector,
    previous_vector,
    beta_previous,
    stored_vectors,
    velocity,
    level_weight,
    box_owner,
):
    lon_count = lax.axis_size("lon")
    lev_count = lax.axis_size("lev")
    cells = float(current_vector.size * lon_count * lev_count)
    columns = float(box_owner.size * lon_count)
    boxes = jnp.arange(1, NBOX + 1, dtype=jnp.int32)
    owner_hot = (box_owner[None] == boxes[:, None, None]).astype(jnp.float32)
    counts = lax.psum(jnp.sum(owner_hot, axis=(1, 2)), "lon")
    scales = columns / (NBOX * jnp.maximum(counts, 1.0))
    factor = jnp.sum(owner_hot * scales[:, None, None], axis=0)
    first = tangent(current_vector, velocity[0])
    second = tangent(first, velocity[1])
    weighted = level_weight[:, None, None] * factor[None] * second
    back = adjoint_products(adjoint_products(weighted, velocity[1]), velocity[0])
    applied = back - beta_previous * previous_vector
    basis = stored_vectors.reshape(stored_vectors.shape[0], -1)
    alpha_term = lax.psum(jnp.sum(applied * current_vector), ("lon", "lev")) / cells
    lanczos = applied - alpha_term * current_vector
    partial_value = jnp.dot(basis, lanczos.reshape(-1), precision=highest)
    projections = lax.psum(partial_value, ("lon", "lev")) / cells
    orthogonal = lanczos - jnp.dot(projections, basis, precision=highest).reshape(lanczos.shape)
    square = lax.psum(jnp.sum(orthogonal * orthogonal), ("lon", "lev")) / cells
    beta_norm = jnp.sqrt(square + 1e-12)
    return (
        orthogonal / beta_norm,
        jnp.concatenate([alpha_term[None], beta_norm[None], projections]),
    )


def solution(mesh):
    placed = (
        P("lev", "lon", None),
        P("lev", "lon", None),
        P(),
        P(None, "lev", "lon", None),
        P(None, None, "lev", "lon", None),
        P("lev"),
        P("lon", None),
    )
    return jax.shard_map(
        body, mesh=mesh, in_specs=placed, out_specs=(P("lev", "lon", None), P()), check_vma=False
    )
```

profile of v0, /device:TPU:0, one launch (start us, length us, event | category | flops | bytes accessed | tf_op | source)
XLA Modules:
  0.0 218.3 jit_solution(6118552443733960788)
XLA Ops:
  0.7 1.0 fusion.75
  1.7 1.3 collective-permute-start.2
  3.0 3.0 %collective-permute-start.3 = (f32[1,1,32,512]{3,2,1,0:T(8,128)S(1)}, f32[1,1,32,512]{3,2,1,0:T(8,128)S(1)}, u32[]{:S(2)}, u32[]{:S(2)}) collective-permute-start(f32[1,1,32,512]{3,2,1,0:T(8,128)S(1)} %get-tuple-element.41), channel_id=1, source_target_pairs={{0,1},{1,2},{2,3},{4,5},{5,6},{6,7},{8,9},{9,10},{10,11},{12,13},{... | collective-permute-start | bytes 196616 | tf_op jit(solution)/shard_map/ppermute | solution.py:22
  6.0 0.9 fusion.74
  6.9 6.1 %collective-permute-start = (f32[1,4,1,512]{3,2,1,0:T(1,128)S(1)}, f32[1,4,1,512]{3,2,1,0:T(1,128)S(1)}, u32[]{:S(2)}, u32[]{:S(2)}) collective-permute-start(f32[1,4,1,512]{3,2,1,0:T(1,128)S(1)} %get-tuple-element.38), channel_id=1, source_target_pairs={{4,0},{8,4},{12,8},{16,12},{20,16},{24,20},{28,24},{0,28},{5,1},{9... | collective-permute-start | bytes 24584 | tf_op jit(solution)/shard_map/ppermute | solution.py:24
  12.9 1.0 fusion.7
  14.0 1.2 fusion.73
  15.2 21.8 %psum.28 = f32[5]{0:T(128)S(1)} all-reduce(f32[5]{0:T(128)S(1)} %fusion.7), channel_id=1, replica_groups=mesh['lon'=8,'lev'=4] {'lon'}, use_global_device_ids=true, to_apply=%region_1.0 | all-reduce | flops 5 | bytes 40 | tf_op jit(solution)/shard_map/psum | solution.py:94
  37.0 1.2 subtract_bitcast_fusion.1
  38.2 0.9 fusion.8
  39.8 1.9 fusion.45
  41.8 1.3 collective-permute-start.6
  43.1 3.0 %collective-permute-start.7 = (f32[1,1,32,512]{3,2,1,0:T(8,128)S(1)}, f32[1,1,32,512]{3,2,1,0:T(8,128)S(1)}, u32[]{:S(2)}, u32[]{:S(2)}) collective-permute-start(f32[1,1,32,512]{3,2,1,0:T(8,128)S(1)} %get-tuple-element.35), channel_id=1, source_target_pairs={{0,1},{1,2},{2,3},{4,5},{5,6},{6,7},{8,9},{9,10},{10,11},{12,13},{... | collective-permute-start | bytes 196616 | tf_op jit(solution)/shard_map/ppermute | solution.py:22
  46.2 2.0 collective-permute-start.5
  48.4 1.5 collective-permute-done.4
  49.9 2.8 %collective-permute-done.5 = f32[1,4,1,512]{3,2,1,0:T(1,128)S(1)} collective-permute-done((f32[1,4,1,512]{3,2,1,0:T(1,128)S(1)}, f32[1,4,1,512]{3,2,1,0:T(1,128)S(1)}, u32[]{:S(2)}, u32[]{:S(2)}) %collective-permute-start.5) | collective-permute-done | bytes 8224 | tf_op jit(solution)/shard_map/ppermute | solution.py:22
  53.1 2.0 collective-permute-start.10
  55.2 1.3 collective-permute-start.11
  56.6 4.7 %collective-permute-start.9 = (f32[4,4,1,512]{3,2,1,0:T(1,128)S(1)}, f32[4,4,1,512]{3,2,1,0:T(1,128)S(1)}, u32[]{:S(2)}, u32[]{:S(2)}) collective-permute-start(f32[4,4,1,512]{3,2,1,0:T(1,128)S(1)} %get-tuple-element.23), channel_id=1, source_target_pairs={{4,0},{8,4},{12,8},{16,12},{20,16},{24,20},{28,24},{0,28},{5,1},{9... | collective-permute-start | bytes 98312 | tf_op jit(solution)/shard_map/ppermute | solution.py:24
  61.5 1.7 collective-permute-done.8
  63.6 3.0 %collective-permute-start.14 = (f32[4,1,32,512]{3,2,1,0:T(8,128)S(1)}, f32[4,1,32,512]{3,2,1,0:T(8,128)S(1)}, u32[]{:S(2)}, u32[]{:S(2)}) collective-permute-start(f32[4,1,32,512]{3,2,1,0:T(8,128)S(1)} %get-tuple-element.20), channel_id=1, source_target_pairs={{0,1},{1,2},{2,3},{4,5},{5,6},{6,7},{8,9},{9,10},{10,11},{12,13},{... | collective-permute-start | bytes 786440 | tf_op jit(solution)/shard_map/ppermute | solution.py:22
  66.7 1.3 collective-permute-start.15
  68.1 4.7 %collective-permute-start.13 = (f32[4,4,1,512]{3,2,1,0:T(1,128)S(1)}, f32[4,4,1,512]{3,2,1,0:T(1,128)S(1)}, u32[]{:S(2)}, u32[]{:S(2)}) collective-permute-start(f32[4,4,1,512]{3,2,1,0:T(1,128)S(1)} %get-tuple-element.19), channel_id=1, source_target_pairs={{4,0},{8,4},{12,8},{16,12},{20,16},{24,20},{28,24},{0,28},{5,1},{9... | collective-permute-start | bytes 98312 | tf_op jit(solution)/shard_map/ppermute | solution.py:24
  73.0 1.8 collective-permute-done.12
  74.8 0.8 multiply_reduce_fusion.1
  75.7 43.7 %psum.29 = f32[]{:T(128)} all-reduce(f32[]{:T(128)} %get-tuple-element.2), channel_id=1, replica_groups=mesh['lon'=8,'lev'=4] {'lon','lev'}, use_global_device_ids=true, to_apply=%region_4.5 | all-reduce | flops 1 | bytes 8 | tf_op jit(solution)/shard_map/psum | solution.py:103
  120.0 8.6 %fusion.4 = f32[16]{0:T(128)S(1)} fusion(f32[16,4,32,512]{3,2,1,0:T(8,128)} %param.10, f32[4,32,512,1]{2,1,0,3:T(8,128)S(1)} %bitcast.248), kind=kOutput, calls=%fused_computation.4 | convolution fusion | flops 12582912 | bytes 4456512 | tf_op jit(solution)/shard_map/dot_general | solution.py:105
  128.7 40.7 %psum.30 = f32[16]{0:T(128)S(1)} all-reduce(f32[16]{0:T(128)S(1)} %fusion.4), channel_id=1, replica_groups=mesh['lon'=8,'lev'=4] {'lon','lev'}, use_global_device_ids=true, to_apply=%region_5.6 | all-reduce | flops 16 | bytes 128 | tf_op jit(solution)/shard_map/psum | solution.py:106
  169.3 6.4 %fusion = f32[1,4,32,512]{3,0,2,1:T(1,128)S(1)} fusion(f32[4,32,512,16]{2,1,0,3:T(8,128)} %bitcast.241, f32[16]{0:T(128)S(1)} %psum.30), kind=kOutput, calls=%fused_computation | convolution fusion | flops 12582928 | bytes 4456512 | tf_op jit(solution)/shard_map/dot_general | solution.py:107
  175.7 0.7 multiply_reduce_fusion
  176.4 39.9 %psum.31 = f32[]{:T(128)} all-reduce(f32[]{:T(128)} %multiply_reduce_fusion), channel_id=1, replica_groups=mesh['lon'=8,'lev'=4] {'lon','lev'}, use_global_device_ids=true, to_apply=%region_7.8 | all-reduce | flops 1 | bytes 8 | tf_op jit(solution)/shard_map/psum | solution.py:108
  217.0 0.7 broadcast_divide_fusion
  (42 shorter events, 2.4 us)
Async XLA Ops:
  0.6 52.0 %copy-start.1 = (f32[2,3,4,32,512]{4,3,2,1,0:T(8,128)S(1)}, f32[2,3,4,32,512]{4,3,2,1,0:T(8,128)}, u32[]{:S(2)}) copy-start(f32[2,3,4,32,512]{4,3,2,1,0:T(8,128)} %param.11) | copy-start | bytes 4718596
  0.6 52.0 %copy-start.3 = (f32[4]{0:T(128)S(1)}, f32[4]{0:T(128)}, u32[]{:S(2)}) copy-start(f32[4]{0:T(128)} %param.12) | copy-start | bytes 52
  1.7 38.2 %collective-permute-start.2 = (f32[1,1,32,512]{3,2,1,0:T(8,128)S(1)}, f32[1,1,32,512]{3,2,1,0:T(8,128)S(1)}, u32[]{:S(2)}, u32[]{:S(2)}) collective-permute-start(f32[1,1,32,512]{3,2,1,0:T(8,128)S(1)} %get-tuple-element.40), channel_id=1, source_target_pairs={{1,0},{2,1},{3,2},{5,4},{6,5},{7,6},{9,8},{10,9},{11,10},{13,12},{... | collective-permute-start | bytes 196616 | tf_op jit(solution)/shard_map/ppermute | solution.py:24
  3.0 36.9 %collective-permute-start.3 = (f32[1,1,32,512]{3,2,1,0:T(8,128)S(1)}, f32[1,1,32,512]{3,2,1,0:T(8,128)S(1)}, u32[]{:S(2)}, u32[]{:S(2)}) collective-permute-start(f32[1,1,32,512]{3,2,1,0:T(8,128)S(1)} %get-tuple-element.41), channel_id=1, source_target_pairs={{0,1},{1,2},{2,3},{4,5},{5,6},{6,7},{8,9},{9,10},{10,11},{12,13},{... | collective-permute-start | bytes 196616 | tf_op jit(solution)/shard_map/ppermute | solution.py:22
  6.9 32.9 %collective-permute-start = (f32[1,4,1,512]{3,2,1,0:T(1,128)S(1)}, f32[1,4,1,512]{3,2,1,0:T(1,128)S(1)}, u32[]{:S(2)}, u32[]{:S(2)}) collective-permute-start(f32[1,4,1,512]{3,2,1,0:T(1,128)S(1)} %get-tuple-element.38), channel_id=1, source_target_pairs={{4,0},{8,4},{12,8},{16,12},{20,16},{24,20},{28,24},{0,28},{5,1},{9... | collective-permute-start | bytes 24584 | tf_op jit(solution)/shard_map/ppermute | solution.py:24
  12.9 26.9 %collective-permute-start.1 = (f32[1,4,1,512]{3,2,1,0:T(1,128)S(1)}, f32[1,4,1,512]{3,2,1,0:T(1,128)S(1)}, u32[]{:S(2)}, u32[]{:S(2)}) collective-permute-start(f32[1,4,1,512]{3,2,1,0:T(1,128)S(1)} %get-tuple-element.39), channel_id=1, source_target_pairs={{0,4},{4,8},{8,12},{12,16},{16,20},{20,24},{24,28},{28,0},{1,5},{5... | collective-permute-start | bytes 24584 | tf_op jit(solution)/shard_map/ppermute | solution.py:22
  41.8 10.8 %collective-permute-start.6 = (f32[1,1,32,512]{3,2,1,0:T(8,128)S(1)}, f32[1,1,32,512]{3,2,1,0:T(8,128)S(1)}, u32[]{:S(2)}, u32[]{:S(2)}) collective-permute-start(f32[1,1,32,512]{3,2,1,0:T(8,128)S(1)} %get-tuple-element.34), channel_id=1, source_target_pairs={{1,0},{2,1},{3,2},{5,4},{6,5},{7,6},{9,8},{10,9},{11,10},{13,12},{... | collective-permute-start | bytes 196616 | tf_op jit(solution)/shard_map/ppermute | solution.py:24
  43.1 9.5 %collective-permute-start.7 = (f32[1,1,32,512]{3,2,1,0:T(8,128)S(1)}, f32[1,1,32,512]{3,2,1,0:T(8,128)S(1)}, u32[]{:S(2)}, u32[]{:S(2)}) collective-permute-start(f32[1,1,32,512]{3,2,1,0:T(8,128)S(1)} %get-tuple-element.35), channel_id=1, source_target_pairs={{0,1},{1,2},{2,3},{4,5},{5,6},{6,7},{8,9},{9,10},{10,11},{12,13},{... | collective-permute-start | bytes 196616 | tf_op jit(solution)/shard_map/ppermute | solution.py:22
  46.2 3.7 %collective-permute-start.4 = (f32[1,4,1,512]{3,2,1,0:T(1,128)S(1)}, f32[1,4,1,512]{3,2,1,0:T(1,128)S(1)}, u32[]{:S(2)}, u32[]{:S(2)}) collective-permute-start(f32[1,4,1,512]{3,2,1,0:T(1,128)S(1)} %get-tuple-element.30), channel_id=1, source_target_pairs={{4,0},{8,4},{12,8},{16,12},{20,16},{24,20},{28,24},{0,28},{5,1},{9... | collective-permute-start | bytes 24584 | tf_op jit(solution)/shard_map/ppermute | solution.py:24
  46.2 6.4 %collective-permute-start.5 = (f32[1,4,1,512]{3,2,1,0:T(1,128)S(1)}, f32[1,4,1,512]{3,2,1,0:T(1,128)S(1)}, u32[]{:S(2)}, u32[]{:S(2)}) collective-permute-start(f32[1,4,1,512]{3,2,1,0:T(1,128)S(1)} %get-tuple-element.31), channel_id=1, source_target_pairs={{0,4},{4,8},{8,12},{12,16},{16,20},{20,24},{24,28},{28,0},{1,5},{5... | collective-permute-start | bytes 24584 | tf_op jit(solution)/shard_map/ppermute | solution.py:22
  53.1 10.1 %collective-permute-start.10 = (f32[4,1,32,512]{3,2,1,0:T(8,128)S(1)}, f32[4,1,32,512]{3,2,1,0:T(8,128)S(1)}, u32[]{:S(2)}, u32[]{:S(2)}) collective-permute-start(f32[4,1,32,512]{3,2,1,0:T(8,128)S(1)} %get-tuple-element.24), channel_id=1, source_target_pairs={{0,1},{1,2},{2,3},{4,5},{5,6},{6,7},{8,9},{9,10},{10,11},{12,13},{... | collective-permute-start | bytes 786440 | tf_op jit(solution)/shard_map/ppermute | solution.py:22
  55.2 8.0 %collective-permute-start.11 = (f32[4,1,32,512]{3,2,1,0:T(8,128)S(1)}, f32[4,1,32,512]{3,2,1,0:T(8,128)S(1)}, u32[]{:S(2)}, u32[]{:S(2)}) collective-permute-start(f32[4,1,32,512]{3,2,1,0:T(8,128)S(1)} %get-tuple-element.25), channel_id=1, source_target_pairs={{1,0},{2,1},{3,2},{5,4},{6,5},{7,6},{9,8},{10,9},{11,10},{13,12},{... | collective-permute-start | bytes 786440 | tf_op jit(solution)/shard_map/ppermute | solution.py:24
  56.5 6.7 %collective-permute-start.8 = (f32[4,4,1,512]{3,2,1,0:T(1,128)S(1)}, f32[4,4,1,512]{3,2,1,0:T(1,128)S(1)}, u32[]{:S(2)}, u32[]{:S(2)}) collective-permute-start(f32[4,4,1,512]{3,2,1,0:T(1,128)S(1)} %get-tuple-element.22), channel_id=1, source_target_pairs={{0,4},{4,8},{8,12},{12,16},{16,20},{20,24},{24,28},{28,0},{1,5},{5... | collective-permute-start | bytes 98312 | tf_op jit(solution)/shard_map/ppermute | solution.py:22
  56.6 6.6 %collective-permute-start.9 = (f32[4,4,1,512]{3,2,1,0:T(1,128)S(1)}, f32[4,4,1,512]{3,2,1,0:T(1,128)S(1)}, u32[]{:S(2)}, u32[]{:S(2)}) collective-permute-start(f32[4,4,1,512]{3,2,1,0:T(1,128)S(1)} %get-tuple-element.23), channel_id=1, source_target_pairs={{4,0},{8,4},{12,8},{16,12},{20,16},{24,20},{28,24},{0,28},{5,1},{9... | collective-permute-start | bytes 98312 | tf_op jit(solution)/shard_map/ppermute | solution.py:24
  63.2 11.6 %copy-start = (f32[4,32,512]{2,1,0:T(8,128)S(1)}, f32[4,32,512]{2,1,0:T(8,128)}, u32[]{:S(2)}) copy-start(f32[4,32,512]{2,1,0:T(8,128)} %param.7) | copy-start | bytes 786436
  63.2 11.6 %copy-start.2 = (f32[4,32,512]{2,1,0:T(8,128)S(1)}, f32[4,32,512]{2,1,0:T(8,128)}, u32[]{:S(2)}) copy-start(f32[4,32,512]{2,1,0:T(8,128)} %param.8) | copy-start | bytes 786436
  63.6 11.2 %collective-permute-start.14 = (f32[4,1,32,512]{3,2,1,0:T(8,128)S(1)}, f32[4,1,32,512]{3,2,1,0:T(8,128)S(1)}, u32[]{:S(2)}, u32[]{:S(2)}) collective-permute-start(f32[4,1,32,512]{3,2,1,0:T(8,128)S(1)} %get-tuple-element.20), channel_id=1, source_target_pairs={{0,1},{1,2},{2,3},{4,5},{5,6},{6,7},{8,9},{9,10},{10,11},{12,13},{... | collective-permute-start | bytes 786440 | tf_op jit(solution)/shard_map/ppermute | solution.py:22
  66.7 8.1 %collective-permute-start.15 = (f32[4,1,32,512]{3,2,1,0:T(8,128)S(1)}, f32[4,1,32,512]{3,2,1,0:T(8,128)S(1)}, u32[]{:S(2)}, u32[]{:S(2)}) collective-permute-start(f32[4,1,32,512]{3,2,1,0:T(8,128)S(1)} %get-tuple-element.21), channel_id=1, source_target_pairs={{1,0},{2,1},{3,2},{5,4},{6,5},{7,6},{9,8},{10,9},{11,10},{13,12},{... | collective-permute-start | bytes 786440 | tf_op jit(solution)/shard_map/ppermute | solution.py:24
  68.0 6.8 %collective-permute-start.12 = (f32[4,4,1,512]{3,2,1,0:T(1,128)S(1)}, f32[4,4,1,512]{3,2,1,0:T(1,128)S(1)}, u32[]{:S(2)}, u32[]{:S(2)}) collective-permute-start(f32[4,4,1,512]{3,2,1,0:T(1,128)S(1)} %get-tuple-element.18), channel_id=1, source_target_pairs={{0,4},{4,8},{8,12},{12,16},{16,20},{20,24},{24,28},{28,0},{1,5},{5... | collective-permute-start | bytes 98312 | tf_op jit(solution)/shard_map/ppermute | solution.py:22
  68.1 6.7 %collective-permute-start.13 = (f32[4,4,1,512]{3,2,1,0:T(1,128)S(1)}, f32[4,4,1,512]{3,2,1,0:T(1,128)S(1)}, u32[]{:S(2)}, u32[]{:S(2)}) collective-permute-start(f32[4,4,1,512]{3,2,1,0:T(1,128)S(1)} %get-tuple-element.19), channel_id=1, source_target_pairs={{4,0},{8,4},{12,8},{16,12},{20,16},{24,20},{28,24},{0,28},{5,1},{9... | collective-permute-start | bytes 98312 | tf_op jit(solution)/shard_map/ppermute | solution.py:24
where the time goes:
time: 219 us; the launch traced here: 218 us
  blocking collectives  146 us (67%)
  starting transfers between devices  34 us (16%)
  matrix products  15 us (7%)
  other arithmetic  9.36 us (4%)
  waiting for transfers between devices  7.72 us (4%)
  local copies, waits for them, and re-layouts  3.22 us (1%)
  between operations  2.96 us (1%)
    psum x1, blocking collectives, body(): lax.psum(jnp.sum(applied * current_vector), ('lon', 'lev')) / cells  43.7 us
    psum x1, blocking collectives, body(): projections = lax.psum(partial_value, ('lon', 'lev')) / cells  40.7 us
    psum x1, blocking collectives, body(): square = lax.psum(jnp.sum(orthogonal * orthogonal), ('lon', 'lev')) / cells  39.9 us
    psum x1, blocking collectives, body(): counts = lax.psum(jnp.sum(owner_hot, axis=(1, 2)), 'lon')  21.8 us
    ppermute x8, starting transfers between devices, extended(): lax.ppermute(head, axis, [((i + 1) % count, i) for i in range(ends)])  20.7 us
    ppermute x8, starting transfers between devices, extended(): lax.ppermute(tail, axis, [(i, (i + 1) % count) for i in range(ends)])  13.3 us
    dot_general x1, matrix products, body(): partial_value = jnp.dot(basis, lanczos.reshape(-1), precision=highest)  8.61 us
    dot_general x1, matrix products, body(): jnp.dot(projections, basis, precision=highest).reshape(lanczos.shape)  6.42 us
  transfers between devices with their start and end apart: 16, of which 4 were waited for; matrix products, arithmetic and copies ran while one was open for 3% of the time, Pallas kernels for 0%

commit v1 on v0

v1 whole, which is shorter than its diff:
```python
import functools

import jax
import jax.numpy as jnp
from jax import lax
from jax.experimental import pallas as pl
from jax.experimental.pallas import tpu as pltpu
from jax.sharding import PartitionSpec as P

NBOX = 5
kappa = 0.1
centre = 1.0 - 6.0 * kappa
f32 = jnp.float32

VM = pl.BlockSpec(memory_space=pltpu.VMEM)
SM = pl.BlockSpec(memory_space=pltpu.SMEM)
CHUNK = 8
WIDE = 4
SECOND = 2
V_ROWS, A_ROWS, B_ROWS = 4, 3, 2
LEVEL_ROWS = V_ROWS + 3 * A_ROWS


def sds(*shape):
    return jax.ShapeDtypeStruct(shape, f32)


def call(kernel, outs, operands, specs=None, scratch=(), flops=0):
    nbytes = sum(4 * x.size for x in operands)
    return pl.pallas_call(
        kernel,
        out_shape=outs,
        in_specs=specs or [VM] * len(operands),
        out_specs=jax.tree.map(lambda _: VM, outs),
        scratch_shapes=list(scratch),
        compiler_params=pltpu.CompilerParams(vmem_limit_bytes=40 << 20),
        cost_estimate=pl.CostEstimate(flops=flops, bytes_accessed=nbytes, transcendentals=0),
    )(*operands)


def lane_iota(shape):
    return lax.broadcasted_iota(jnp.int32, shape, len(shape) - 1)


def even_level():
    return lax.rem(lax.axis_index("lev"), 2) == 0


def pack_kernel(levels, cols, v, vel, owner, lo_a, lo_b, hi_a, hi_b, lev_a, lev_b, counts):
    for msg_a, msg_b, low in ((lo_a, lo_b, True), (hi_a, hi_b, False)):

        def edge(n):
            return slice(0, n) if low else slice(cols - n, cols)

        for lev in range(levels):
            base = lev * LEVEL_ROWS
            msg_a[base : base + V_ROWS] = v[lev, edge(V_ROWS)]
            for comp in range(3):
                at = base + V_ROWS + comp * A_ROWS
                msg_a[at : at + A_ROWS] = vel[0, comp, lev, edge(A_ROWS)]
                at = (lev * 3 + comp) * B_ROWS
                msg_b[at : at + B_ROWS] = vel[1, comp, lev, edge(B_ROWS)]
        at = levels * LEVEL_ROWS
        msg_a[at : at + B_ROWS] = owner[edge(B_ROWS)].astype(f32)
    even = even_level()
    for msg, top in ((lev_a, even), (lev_b, jnp.logical_not(even))):
        near = jnp.where(top, levels - 1, 0)
        msg[0] = v[near]
        msg[1] = v[jnp.where(top, levels - 2, 1)]
        for comp in range(3):
            msg[2 + comp] = vel[0, comp, near]
    lanes = lane_iota((1, 128))
    row = jnp.zeros((1, 128), f32)
    held = owner[...]
    for box in range(1, NBOX + 1):
        hot = jnp.sum((held == box).astype(f32), axis=0, keepdims=True)
        row = jnp.where(lanes == box - 1, jnp.sum(hot, axis=1, keepdims=True), row)
    counts[...] = row


def corner_kernel(levels, n_counts, west, east, *refs):
    count_refs, (halo_v, halo_a, corner_a, corner_b, counts) = refs[:n_counts], refs[n_counts:]
    halo_a[...] = jnp.zeros(halo_a.shape, f32)
    for lev in range(levels):
        base = lev * LEVEL_ROWS
        halo_v[lev, 0:V_ROWS] = east[base : base + V_ROWS]
        halo_v[lev, CHUNK - V_ROWS : CHUNK] = west[base : base + V_ROWS]
        for comp in range(3):
            at = base + V_ROWS + comp * A_ROWS
            halo_a[comp, lev, 0:A_ROWS] = east[at : at + A_ROWS]
            halo_a[comp, lev, CHUNK - A_ROWS : CHUNK] = west[at : at + A_ROWS]
    even = even_level()
    for msg, top in ((corner_a, even), (corner_b, jnp.logical_not(even))):
        near = jnp.where(top, levels - 1, 0)
        msg[0] = halo_v[near]
        msg[1] = halo_v[jnp.where(top, levels - 2, 1)]
        for comp in range(3):
            msg[2 + comp] = halo_a[comp, near]
    total = count_refs[0][...]
    for ref in count_refs[1:]:
        total = total + ref[...]
    counts[...] = total


def stencil_kernel(
    levels, cols, lat, columns, n_counts,
    lw, beta_prev, v, prev, vel, owner, west, west_b, east_b, east, halo_v, halo_a,
    lev_a, lev_b, corner_a, corner_b, *refs,
):
    count_refs = refs[:n_counts]
    applied, send_a, send_b = refs[n_counts : n_counts + 3]
    (vv, la, ff, halo_b, own_h, w_in, w_e, w_w, w_u, w_d, u_in, u_e, u_w, u_u, u_d, out) = refs[n_counts + 3 :]
    chunks = cols // CHUNK
    level = lax.axis_index("lev")
    last = lax.axis_size("lev") - 1
    even = even_level()
    has = (level > 0, level < last)
    lanes = lane_iota((CHUNK, lat))
    first_lane, last_lane = lanes == 0, lanes == lat - 1

    def rows(k, shift=0):
        return slice(CHUNK * (k + 1) + shift, CHUNK * (k + 2) + shift)

    def put_west(ref, at, k, value):
        ref[at, rows(k)] = value
        if k == chunks:
            ref[at, 0:CHUNK] = value

    def put_east(ref, at, k, value):
        ref[at, rows(k)] = value
        if k == 0:
            ref[at, rows(chunks + 1)] = value

    def put_both(ref, at, k, value):
        put_west(ref, at, k, value)
        if k == 0:
            ref[at, rows(chunks + 1)] = value

    def from_south(x):
        return jnp.where(first_lane, 0.0, pltpu.roll(x, 1, 1))

    def from_north(x):
        return jnp.where(last_lane, 0.0, pltpu.roll(x, lat - 1, 1))

    for k in range(chunks + 1):
        cells = slice(CHUNK * k, CHUNK * (k + 1))
        got_a, got_b = (lev_a, lev_b) if k < chunks else (corner_a, corner_b)
        src = cells if k < chunks else slice(0, CHUNK)
        for item in range(5):
            a, b = got_a[item, src], got_b[item, src]
            below, above = jnp.where(even, b, a), jnp.where(even, a, b)
            if item < 2:
                put_both(vv, 1 - item, k, jnp.where(has[0], below, 0.0))
                put_both(vv, levels + 2 + item, k, jnp.where(has[1], above, 0.0))
            else:
                la[0, item - 2, cells] = below
                la[1, item - 2, cells] = above
        for lev in range(levels):
            put_both(vv, lev + 2, k, v[lev, cells] if k < chunks else halo_v[lev])
    halo_b[...] = jnp.zeros(halo_b.shape, f32)
    for lev in range(levels):
        for comp in range(3):
            at = (lev * 3 + comp) * B_ROWS
            halo_b[comp, lev, 0:B_ROWS] = east_b[at : at + B_ROWS]
            halo_b[comp, lev, CHUNK - B_ROWS : CHUNK] = west_b[at : at + B_ROWS]
    own_h[...] = jnp.zeros(own_h.shape, f32)
    at = levels * LEVEL_ROWS
    own_h[0:B_ROWS] = east[at : at + B_ROWS]
    own_h[CHUNK - B_ROWS : CHUNK] = west[at : at + B_ROWS]

    def flow(section, k, lev):
        if k < chunks:
            return [vel[section, comp, lev, CHUNK * k : CHUNK * (k + 1)] for comp in range(3)]
        return [(halo_b if section else halo_a)[comp, lev] for comp in range(3)]

    def flow_beyond(side, k):
        return [la[side, comp, CHUNK * k : CHUNK * (k + 1)] for comp in range(3)]

    def tangent(ref, at, k, abc):
        here = ref[at, rows(k)]
        e, w = ref[at, rows(k, 1)], ref[at, rows(k, -1)]
        n, s = from_north(here), from_south(here)
        u, d = ref[at + 1, rows(k)], ref[at - 1, rows(k)]
        a, b, c = abc
        around = ((e + w) + (n + s)) + (u + d)
        drift = a * (w - e) + b * (s - n) + c * (d - u)
        return centre * here + kappa * around + 0.5 * drift

    def push(x, abc, dst, at, k):
        inside, to_e, to_w, to_u, to_d = dst
        a, b, c = abc
        base, half = kappa * x, 0.5 * x
        a, b, c = a * half, b * half, c * half
        inside[at, rows(k)] = centre * x + (from_south(base - b) + from_north(base + b))
        put_west(to_e, at, k, base - a)
        put_east(to_w, at, k, base + a)
        to_u[at, rows(k)] = base - c
        to_d[at, rows(k)] = base + c

    for k in range(chunks + 1):
        for side, at in ((0, 0), (1, levels + 1)):
            value = tangent(vv, at + 1, k, flow_beyond(side, k))
            put_both(ff, at, k, jnp.where(has[side], value, 0.0))

    def first_level(lev, carry):
        for k in range(chunks + 1):
            put_both(ff, lev + 1, k, tangent(vv, lev + 2, k, flow(0, k, lev)))
        return carry

    lax.fori_loop(0, levels, first_level, 0)

    total = count_refs[0][...]
    for ref in count_refs[1:]:
        total = total + ref[...]
    scales = columns / (NBOX * jnp.maximum(total, 1.0))
    for k in range(chunks + 1):
        mine = owner[CHUNK * k : CHUNK * (k + 1)].astype(f32) if k < chunks else own_h[...]
        factor = jnp.zeros((CHUNK, lat), f32)
        for box in range(1, NBOX + 1):
            factor = jnp.where(mine == float(box), jnp.broadcast_to(scales[:, box - 1 : box], (CHUNK, lat)), factor)
        out[0, CHUNK * k : CHUNK * (k + 1)] = factor

    def second_level(lev, carry):
        weight = lw[lev]
        for k in range(chunks + 1):
            abc = flow(1, k, lev)
            x = tangent(ff, lev + 1, k, abc)
            x = (weight * out[0, CHUNK * k : CHUNK * (k + 1)]) * x
            push(x, abc, (w_in, w_e, w_w, w_u, w_d), lev + 1, k)
        return carry

    lax.fori_loop(0, levels, second_level, 0)
    for k in range(chunks + 1):
        w_u[0, rows(k)] = jnp.zeros((CHUNK, lat), f32)
        w_d[levels + 1, rows(k)] = jnp.zeros((CHUNK, lat), f32)

    def third_level(lev, carry):
        for k in range(chunks + 1):
            x = (
                w_in[lev + 1, rows(k)]
                + (w_e[lev + 1, rows(k, -1)] + w_w[lev + 1, rows(k, 1)])
                + (w_u[lev, rows(k)] + w_d[lev + 2, rows(k)])
            )
            push(x, flow(0, k, lev), (u_in, u_e, u_w, u_u, u_d), lev + 1, k)
        return carry

    lax.fori_loop(0, levels, third_level, 0)
    for k in range(chunks + 1):
        for side, at, x in ((0, 0, w_d[1, rows(k)]), (1, levels + 1, w_u[levels, rows(k)])):
            x = jnp.where(has[side], x, 0.0)
            push(x, flow_beyond(side, k), (u_in, u_e, u_w, u_u, u_d), at, k)

    beta = beta_prev[0]
    for k in range(chunks):
        cells = slice(CHUNK * k, CHUNK * (k + 1))
        out[0, cells] = u_d[0, rows(k)]
        out[levels + 3, cells] = u_u[levels + 1, rows(k)]
        for at in range(levels + 2):
            x = u_in[at, rows(k)] + (u_e[at, rows(k, -1)] + u_w[at, rows(k, 1)])
            if at > 0:
                x = x + u_u[at - 1, rows(k)]
            if at < levels + 1:
                x = x + u_d[at + 1, rows(k)]
            if 1 <= at <= levels:
                applied[at - 1, cells] = x - beta * prev[at - 1, cells]
            else:
                out[at + 1, cells] = x
    up = jnp.where(even, levels + 2, 0)
    down = levels + 2 - up
    for i in range(SECOND):
        send_a[i] = out[up + i, 0:cols]
        send_b[i] = out[down + i, 0:cols]


def put_sum(rows_ref, at, acc):
    rows_ref[at : at + 1] = jnp.sum(acc, axis=0, keepdims=True)


def to_lanes(rows_ref, at):
    return jnp.sum(jnp.transpose(rows_ref[at : at + 128, :]), axis=0, keepdims=True)


def tiles(lat):
    return [slice(t, t + 128) for t in range(0, lat, 128)]


def gram_kernel(nvec, levels, cols, lat, s, v, out, sums):
    sums[...] = jnp.zeros(sums.shape, f32)
    steps = levels * (cols // CHUNK)
    block = 4

    def place(step):
        lev = step // (cols // CHUNK)
        row = pl.multiple_of((step - lev * (cols // CHUNK)) * CHUNK, CHUNK)
        return lev, pl.ds(row, CHUNK)

    for i0 in range(0, nvec, block):
        for j0 in range(i0, nvec, block):
            pairs = [(i, j) for i in range(i0, i0 + block) for j in range(j0, j0 + block) if i <= j]

            def body(step, acc, pairs=pairs, need=sorted({*range(i0, i0 + block), *range(j0, j0 + block)})):
                lev, cells = place(step)
                for t in tiles(lat):
                    held = {i: s[i, lev, cells, t] for i in need}
                    acc = tuple(x + held[i] * held[j] for x, (i, j) in zip(acc, pairs))
                return acc

            acc = lax.fori_loop(0, steps, body, tuple(jnp.zeros((CHUNK, 128), f32) for _ in pairs))
            for (i, j), x in zip(pairs, acc):
                put_sum(sums, nvec * i + j, x)

    def body_v(step, acc):
        lev, cells = place(step)
        for t in tiles(lat):
            x = v[lev, cells, t]
            acc = tuple(y + x * s[i, lev, cells, t] for i, y in enumerate(acc[:-1])) + (acc[-1] + x * x,)
        return acc

    acc = lax.fori_loop(0, steps, body_v, tuple(jnp.zeros((CHUNK, 128), f32) for _ in range(nvec + 1)))
    base = nvec * nvec
    for i in range(nvec):
        put_sum(sums, base + nvec + i, acc[i])
    put_sum(sums, base + 2 * nvec + 2, acc[nvec])
    for r in range(base // 128 + 1):
        out[r : r + 1] = to_lanes(sums, 128 * r)


def gather_kernel(nvec, levels, cols, lat, count, part, got_a, got_b, v, s, gram, applied, msg, sums):
    level = lax.axis_index("lev")
    has = (level > 0, level < lax.axis_size("lev") - 1)
    even = even_level()
    for k in range(cols // CHUNK):
        cells = slice(CHUNK * k, CHUNK * (k + 1))
        for i in range(SECOND):
            a, b = got_a[i, cells], got_b[i, cells]
            below, above = jnp.where(even, b, a), jnp.where(even, a, b)
            applied[i, cells] = part[i, cells] + jnp.where(has[0], below, 0.0)
            top = levels - SECOND + i
            applied[top, cells] = part[top, cells] + jnp.where(has[1], above, 0.0)
    sums[...] = jnp.zeros(sums.shape, f32)
    steps = levels * (cols // CHUNK)

    def body(step, acc):
        lev = step // (cols // CHUNK)
        cells = pl.ds(pl.multiple_of((step - lev * (cols // CHUNK)) * CHUNK, CHUNK), CHUNK)
        for t in tiles(lat):
            x = applied[lev, cells, t]
            acc = tuple(y + x * s[i, lev, cells, t] for i, y in enumerate(acc[:nvec])) + (
                acc[nvec] + x * x,
                acc[nvec + 1] + x * v[lev, cells, t],
            )
        return acc

    acc = lax.fori_loop(0, steps, body, tuple(jnp.zeros((CHUNK, 128), f32) for _ in range(nvec + 2)))
    for i in range(nvec):
        put_sum(sums, i, acc[i])
    put_sum(sums, 2 * nvec, acc[nvec])
    put_sum(sums, 2 * nvec + 1, acc[nvec + 1])
    r = gram.shape[0] - 1
    row = to_lanes(sums, 0) + gram[r : r + 1]
    msg[:, 0:r] = jnp.broadcast_to(gram[0:r][None], (count, r, 128))
    msg[:, r : r + 1] = jnp.broadcast_to(row[None], (count, 1, 128))


def finish_kernel(nvec, levels, cols, lat, cells_all, count, msg, applied, v, s, result, coefs, trust):
    total = jnp.sum(msg[...], axis=0) * (1.0 / cells_all)
    r = total.shape[0] - 1
    row = total[r : r + 1]
    aa = row[:, 2 * nvec : 2 * nvec + 1]
    alpha = row[:, 2 * nvec + 1 : 2 * nvec + 2]
    vv = row[:, 2 * nvec + 2 : 2 * nvec + 3]
    lanes = lane_iota((1, 128))
    pv = row - alpha * pltpu.roll(row, 128 - nvec, 1)
    p = [jnp.broadcast_to(pv[:, k : k + 1], (1, 128)) for k in range(nvec)]
    tiled = jnp.zeros((1, 128), f32)
    for k in range(nvec):
        tiled = jnp.where(lax.rem(lanes, nvec) == k, p[k], tiled)
    quad = jnp.zeros((1, 128), f32)
    per = 128 // nvec
    for g in range(r):
        rep = jnp.zeros((1, 128), f32)
        for i in range(per):
            rep = jnp.where(lanes // nvec == i, p[g * per + i], rep)
        i, j = g * per + lanes // nvec, lax.rem(lanes, nvec)
        weight = jnp.where(i == j, 1.0, jnp.where(i < j, 2.0, 0.0))
        quad = quad + weight * rep * tiled * total[g : g + 1]
    quad = jnp.sum(quad, axis=1, keepdims=True)
    pp = jnp.sum(jnp.where(lanes < nvec, pv * pv, 0.0), axis=1, keepdims=True)
    square = (aa - 2.0 * alpha * alpha + alpha * alpha * vv) + (quad - 2.0 * pp)
    size = aa + alpha * alpha * (2.0 + vv) + 2.0 * pp + jnp.abs(quad)
    trust[...] = jnp.where((square > 0.03125 * size) & (size < 1e36), 1.0, 0.0)
    beta = jnp.sqrt(square + 1e-12)
    inverse = 1.0 / beta
    line = jnp.where(lanes == 0, alpha, jnp.where(lanes == 1, beta, pltpu.roll(pv, 2, 1)))
    coefs[...] = line[:, 0 : nvec + 2]
    weights = [jnp.broadcast_to(x * inverse, (CHUNK, 128)) for x in p]
    a_w = jnp.broadcast_to(alpha * inverse, (CHUNK, 128))
    scale = jnp.broadcast_to(inverse, (CHUNK, 128))

    def body(step, carry):
        lev = step // (cols // CHUNK)
        at = pl.ds(pl.multiple_of((step - lev * (cols // CHUNK)) * CHUNK, CHUNK), CHUNK)
        for t in tiles(lat):
            x = scale * applied[lev, at, t] - a_w * v[lev, at, t]
            y = weights[0] * s[0, lev, at, t]
            for k in range(1, nvec):
                y = y + weights[k] * s[k, lev, at, t]
            result[lev, at, t] = x - y
        return carry

    lax.fori_loop(0, levels * (cols // CHUNK), body, 0)


def body(v, prev, beta_prev, s, vel, lw, owner):
    lon_n, lev_n = lax.axis_size("lon"), lax.axis_size("lev")
    count = lon_n * lev_n
    levels, cols, lat = v.shape
    nvec = s.shape[0]
    lines = levels * LEVEL_ROWS + B_ROWS
    lines += -lines % CHUNK
    lines_b = levels * 3 * B_ROWS

    lo_a, lo_b, hi_a, hi_b, lev_a, lev_b, counts = call(
        functools.partial(pack_kernel, levels, cols),
        (sds(lines, lat), sds(lines_b, lat), sds(lines, lat), sds(lines_b, lat),
         sds(5, cols, lat), sds(5, cols, lat), sds(1, 128)),
        (v, vel, owner), flops=1 << 20,
    )
    east_of = [(i, (i + 1) % lon_n) for i in range(lon_n)]
    west_of = [((i + 1) % lon_n, i) for i in range(lon_n)]
    pairs_a = [(i, i ^ 1) for i in range(lev_n)]
    pairs_b = [(i, (i + 1) % lev_n if i % 2 else (i - 1) % lev_n) for i in range(lev_n)]

    def both(a, b):
        return lax.ppermute(a, "lev", pairs_a), lax.ppermute(b, "lev", pairs_b)

    def across(x, k):
        return lax.ppermute(x, "lon", [(i, i ^ k) for i in range(lon_n)])

    west, east = lax.ppermute(hi_a, "lon", east_of), lax.ppermute(lo_a, "lon", west_of)
    lev_a, lev_b = both(lev_a, lev_b)
    near = [counts] + [across(counts, k) for k in (1, 2, 3)]
    west_b, east_b = lax.ppermute(hi_b, "lon", east_of), lax.ppermute(lo_b, "lon", west_of)

    gram_rows = nvec * nvec // 128 + 1
    gram = call(
        functools.partial(gram_kernel, nvec, levels, cols, lat),
        sds(gram_rows, 128), (s, v),
        scratch=[pltpu.VMEM((128 * gram_rows, 128), f32)], flops=20 << 20,
    )

    halo_v, halo_a, corner_a, corner_b, counts = call(
        functools.partial(corner_kernel, levels, len(near)),
        (sds(levels, CHUNK, lat), sds(3, levels, CHUNK, lat), sds(5, CHUNK, lat), sds(5, CHUNK, lat), sds(1, 128)),
        (west, east, *near),
    )
    corner_a, corner_b = both(corner_a, corner_b)
    step = 4
    while 2 * step < lon_n:
        counts = counts + across(counts, step)
        step *= 2
    near = [counts, across(counts, step)]

    padded = cols + 3 * CHUNK
    scratch = [
        pltpu.VMEM((levels + 4, padded, lat), f32),
        pltpu.VMEM((2, 3, cols + CHUNK, lat), f32),
        pltpu.VMEM((levels + 2, padded, lat), f32),
        pltpu.VMEM((3, levels, CHUNK, lat), f32),
        pltpu.VMEM((CHUNK, lat), f32),
    ]
    scratch += [pltpu.VMEM((levels + 2, padded, lat), f32)] * 10
    scratch += [pltpu.VMEM((levels + 4, cols + CHUNK, lat), f32)]
    operands = (lw, beta_prev.reshape(1), v, prev, vel, owner, west, west_b, east_b, east, halo_v, halo_a,
                lev_a, lev_b, corner_a, corner_b, *near)
    part, send_a, send_b = call(
        functools.partial(stencil_kernel, levels, cols, lat, float(cols * lon_n * lat), len(near)),
        (sds(levels, cols, lat), sds(SECOND, cols, lat), sds(SECOND, cols, lat)),
        operands, specs=[SM, SM] + [VM] * (len(operands) - 2), scratch=scratch, flops=8 << 20,
    )
    got_a, got_b = both(send_a, send_b)
    applied, msg = call(
        functools.partial(gather_kernel, nvec, levels, cols, lat, count),
        (sds(levels, cols, lat), sds(count, gram_rows, 128)),
        (part, got_a, got_b, v, s, gram),
        scratch=[pltpu.VMEM((128, 128), f32)],
    )
    msg = lax.all_to_all(msg, ("lon", "lev"), 0, 0, tiled=True)
    cells = float(v.size * count)
    result, coefs, trust = call(
        functools.partial(finish_kernel, nvec, levels, cols, lat, cells, count),
        (sds(levels, cols, lat), sds(1, nvec + 2), sds(1, 1)),
        (msg, applied, v, s),
    )
    coefs = coefs.reshape(nvec + 2)

    def keep():
        return result, coefs

    def direct():
        orthogonal = applied - coefs[0] * v - jnp.sum(coefs[2:, None, None, None] * s, axis=0)
        square = lax.psum(jnp.sum(orthogonal * orthogonal), ("lon", "lev")) / cells
        beta = jnp.sqrt(square + 1e-12)
        return orthogonal / beta, jnp.concatenate([coefs[:1], beta[None], coefs[2:]])

    return lax.cond(trust[0, 0] > 0.5, keep, direct)


def solution(mesh):
    placed = (
        P("lev", "lon", None),
        P("lev", "lon", None),
        P(),
        P(None, "lev", "lon", None),
        P(None, None, "lev", "lon", None),
        P("lev"),
        P("lon", None),
    )
    return jax.shard_map(
        body, mesh=mesh, in_specs=placed, out_specs=(P("lev", "lon", None), P()), check_vma=False
    )
```

time: 219 us -> 71.7 us (0.33)
  blocking collectives: 146 us -> 11.2 us
  starting transfers between devices: 34 us -> 12.6 us
  Pallas kernels: 0 us -> 15.4 us
  matrix products: 15 us -> 0 us
  waiting for transfers between devices: 7.72 us -> 22.7 us
  other arithmetic: 9.36 us -> 0 us
  local copies, waits for them, and re-layouts: 3.22 us -> 7.3 us
    psum x4 -> x0, blocking collectives: 146 us -> none  [the longest x1 43.7 us: body(): lax.psum(jnp.sum(applied * current_vector), ('lon', 'lev')) / cells]
    ppermute x16 -> x14, starting transfers between devices: 34 us -> 12.6 us  [the longest x6 4.56 us: both(): return (lax.ppermute(a, 'lev', pairs_a), lax.ppermute(b, 'lev', pairs_b))]
    pallas_call x0 -> x6, Pallas kernels: none -> 15.4 us  [call(): pl.pallas_call(kernel, out_shape=outs, in_specs=specs or [VM] * len(opera...]
    dot_general x2 -> x0, matrix products: 15 us -> none  [the longest x1 8.61 us: body(): partial_value = jnp.dot(basis, lanczos.reshape(-1), precision=highest)]
    ppermute x16 -> x14, waiting for transfers between devices: 7.72 us -> 22.7 us  [the longest x4 12.9 us: across(): return lax.ppermute(x, 'lon', [(i, i ^ k) for i in range(lon_n)])]
    all_to_all x0 -> x1, blocking collectives: none -> 11.2 us  [body(): msg = lax.all_to_all(msg, ('lon', 'lev'), 0, 0, tiled=True)]
    unnamed x8 -> x20, local copies, waits for them, and re-layouts: 0.02 us -> 7.3 us
    reduce_sum x4 -> x0, other arithmetic: 3.51 us -> none  [the longest x1 1.04 us: body(): counts = lax.psum(jnp.sum(owner_hot, axis=(1, 2)), 'lon')]
  transfers between devices with their start and end apart: 16 -> 14, of which waited for: 4 -> 6; matrix products, arithmetic and copies ran while one was open for 3% -> 0% of each run, Pallas kernels for 0% -> 11%
where the time goes in v1:
time: 71.7 us; the launch traced here: 71.3 us
  waiting for transfers between devices  22.7 us (32%)
  Pallas kernels  15.4 us (21%)
  starting transfers between devices  12.6 us (18%)
  blocking collectives  11.2 us (16%)
  local copies, waits for them, and re-layouts  7.3 us (10%)
  between operations  2.06 us (3%)
    pallas_call x6, Pallas kernels, call(): pl.pallas_call(kernel, out_shape=outs, in_specs=specs or [VM] * len(opera...  15.4 us
    ppermute x4, waiting for transfers between devices, across(): return lax.ppermute(x, 'lon', [(i, i ^ k) for i in range(lon_n)])  12.9 us
    all_to_all x1, blocking collectives, body(): msg = lax.all_to_all(msg, ('lon', 'lev'), 0, 0, tiled=True)  11.2 us
    unnamed x20, local copies, waits for them, and re-layouts  7.3 us
    ppermute x1, waiting for transfers between devices, body(): lax.ppermute(hi_b, 'lon', east_of)  5.68 us
    ppermute x6, starting transfers between devices, both(): return (lax.ppermute(a, 'lev', pairs_a), lax.ppermute(b, 'lev', pairs_b))  4.56 us
    ppermute x1, waiting for transfers between devices, body(): lax.ppermute(lo_b, 'lon', west_of)  4.09 us
    ppermute x1, starting transfers between devices, body(): lax.ppermute(lo_a, 'lon', west_of)  3.2 us
  transfers between devices with their start and end apart: 14, of which 6 were waited for; matrix products, arithmetic and copies ran while one was open for 0% of the time, Pallas kernels for 11%

profile of v1, /device:TPU:0, one launch (start us, length us, event | category | flops | bytes accessed | tf_op | source)
XLA Modules:
  0.0 71.3 jit_solution(9998621439958367718)
XLA Ops:
  0.6 1.4 %copy-done = f32[2,3,4,32,512]{4,3,2,1,0:T(8,128)S(1)} copy-done((f32[2,3,4,32,512]{4,3,2,1,0:T(8,128)S(1)}, f32[2,3,4,32,512]{4,3,2,1,0:T(8,128)}, u32[]{:S(2)}) %copy-start) | copy-done | bytes 1572888
  2.0 0.8 %copy-done.3 = s32[32,512]{1,0:T(8,128)S(1)} copy-done((s32[32,512]{1,0:T(8,128)S(1)}, s32[32,512]{1,0:T(8,128)}, u32[]{:S(2)}) %copy-start.3) | copy-done | bytes 65560
  2.9 1.2 %shard_map.90 = (f32[56,512]{1,0:T(8,128)S(1)}, f32[24,512]{1,0:T(8,128)S(1)}, f32[56,512]{1,0:T(8,128)S(1)}, f32[24,512]{1,0:T(8,128)S(1)}, f32[5,32,512]{2,1,0...) custom-call(f32[4,32,512]{2,1,0:T(8,128)} %v.9, f32[2,3,4,32,512]{4,3,2,1,0:T(8,128)S(1)} %copy-done, ...), custom_call_target="tpu_custom_call" | custom-call | flops 1048576 | bytes 1900544 | tf_op jit(solution)/shard_map/pallas_call | solution.py:30
  4.1 0.5 collective-permute-start.7
  4.6 2.6 %collective-permute-start.8 = (f32[5,32,512]{2,1,0:T(8,128)S(1)}, f32[5,32,512]{2,1,0:T(8,128)S(1)}, u32[]{:S(2)}, u32[]{:S(2)}) collective-permute-start(f32[5,32,512]{2,1,0:T(8,128)S(1)} %get-tuple-element.46), channel_id=1, source_target_pairs={{0,3},{1,2},{2,1},{3,0},{4,7},{5,6},{6,5},{7,4},{8,11},{9,10},{10,... | collective-permute-start | bytes 983048 | tf_op jit(solution)/shard_map/ppermute | solution.py:435
  7.2 1.5 %collective-permute-start = (f32[56,512]{1,0:T(8,128)S(1)}, f32[56,512]{1,0:T(8,128)S(1)}, u32[]{:S(2)}, u32[]{:S(2)}) collective-permute-start(f32[56,512]{1,0:T(8,128)S(1)} %get-tuple-element.38), channel_id=1, source_target_pairs={{0,4},{4,8},{8,12},{12,16},{16,20},{20,24},{24,28},{28,0},{1,5},{5... | collective-permute-start | bytes 344072 | tf_op jit(solution)/shard_map/ppermute | solution.py:440
  8.8 3.2 %collective-permute-start.3 = (f32[56,512]{1,0:T(8,128)S(1)}, f32[56,512]{1,0:T(8,128)S(1)}, u32[]{:S(2)}, u32[]{:S(2)}) collective-permute-start(f32[56,512]{1,0:T(8,128)S(1)} %get-tuple-element.41), channel_id=1, source_target_pairs={{4,0},{8,4},{12,8},{16,12},{20,16},{24,20},{28,24},{0,28},{5,1},{9... | collective-permute-start | bytes 344072 | tf_op jit(solution)/shard_map/ppermute | solution.py:440
  12.0 4.2 %collective-permute-done.4.refs_1_ = f32[1,128]{1,0:T(1,128)S(1)} collective-permute-done((f32[1,128]{1,0:T(1,128)S(1)}, f32[1,128]{1,0:T(1,128)S(1)}, u32[]{:S(2)}, u32[]{:S(2)}) %collective-permute-start.4) | collective-permute-done | bytes 544 | tf_op jit(solution)/shard_map/ppermute | solution.py:438
  16.1 1.2 %collective-permute-start.5 = (f32[1,128]{1,0:T(1,128)S(1)}, f32[1,128]{1,0:T(1,128)S(1)}, u32[]{:S(2)}, u32[]{:S(2)}) collective-permute-start(f32[1,128]{1,0:T(1,128)S(1)} %get-tuple-element.42.refs_0_), channel_id=1, source_target_pairs={{0,8},{4,12},{8,0},{12,4},{16,24},{20,28},{24,16},{28,20},{1,9},{5... | collective-permute-start | bytes 1544 | tf_op jit(solution)/shard_map/ppermute | solution.py:438
  17.3 2.3 %collective-permute-done.5.refs_2_ = f32[1,128]{1,0:T(1,128)S(1)} collective-permute-done((f32[1,128]{1,0:T(1,128)S(1)}, f32[1,128]{1,0:T(1,128)S(1)}, u32[]{:S(2)}, u32[]{:S(2)}) %collective-permute-start.5) | collective-permute-done | bytes 544 | tf_op jit(solution)/shard_map/ppermute | solution.py:438
  19.7 1.3 %collective-permute-start.6 = (f32[1,128]{1,0:T(1,128)S(1)}, f32[1,128]{1,0:T(1,128)S(1)}, u32[]{:S(2)}, u32[]{:S(2)}) collective-permute-start(f32[1,128]{1,0:T(1,128)S(1)} %get-tuple-element.42.refs_0_), channel_id=1, source_target_pairs={{0,12},{4,8},{8,4},{12,0},{16,28},{20,24},{24,20},{28,16},{1,13},{... | collective-permute-start | bytes 1544 | tf_op jit(solution)/shard_map/ppermute | solution.py:438
  20.9 3.1 %collective-permute-done.6.refs_3_ = f32[1,128]{1,0:T(1,128)S(1)} collective-permute-done((f32[1,128]{1,0:T(1,128)S(1)}, f32[1,128]{1,0:T(1,128)S(1)}, u32[]{:S(2)}, u32[]{:S(2)}) %collective-permute-start.6) | collective-permute-done | bytes 544 | tf_op jit(solution)/shard_map/ppermute | solution.py:438
  24.1 0.3 collective-permute-start.1
  24.4 0.1 shard_map.91
  24.6 0.6 collective-permute-start.9
  25.2 5.7 %collective-permute-done.1.west_b = f32[24,512]{1,0:T(8,128)S(1)} collective-permute-done((f32[24,512]{1,0:T(8,128)S(1)}, f32[24,512]{1,0:T(8,128)S(1)}, u32[]{:S(2)}, u32[]{:S(2)}) %collective-permute-start.1) | collective-permute-done | bytes 49184 | tf_op jit(solution)/shard_map/ppermute | solution.py:443
  30.9 4.1 %collective-permute-done.2.east_b = f32[24,512]{1,0:T(8,128)S(1)} collective-permute-done((f32[24,512]{1,0:T(8,128)S(1)}, f32[24,512]{1,0:T(8,128)S(1)}, u32[]{:S(2)}, u32[]{:S(2)}) %collective-permute-start.2) | collective-permute-done | bytes 49184 | tf_op jit(solution)/shard_map/ppermute | solution.py:443
  35.0 0.5 collective-permute-start.11
  36.1 3.3 %collective-permute-done.11.refs_1_ = f32[1,128]{1,0:T(1,128)S(1)} collective-permute-done((f32[1,128]{1,0:T(1,128)S(1)}, f32[1,128]{1,0:T(1,128)S(1)}, u32[]{:S(2)}, u32[]{:S(2)}) %collective-permute-start.11) | collective-permute-done | bytes 544 | tf_op jit(solution)/shard_map/ppermute | solution.py:438
  39.4 1.4 %copy-done.1 = f32[2,3,4,32,512]{4,3,2,1,0:T(8,128)S(1)} copy-done((f32[2,3,4,32,512]{4,3,2,1,0:T(8,128)S(1)}, f32[2,3,4,32,512]{4,3,2,1,0:T(8,128)}, u32[]{:S(2)}) %copy-start.1) | copy-done | bytes 1572888
  40.8 0.9 %copy-done.2 = f32[4,32,512]{2,1,0:T(8,128)S(1)} copy-done((f32[4,32,512]{2,1,0:T(8,128)S(1)}, f32[4,32,512]{2,1,0:T(8,128)}, u32[]{:S(2)}) %copy-start.2) | copy-done | bytes 262168
  41.8 0.8 %copy-done.4 = s32[32,512]{1,0:T(8,128)S(1)} copy-done((s32[32,512]{1,0:T(8,128)S(1)}, s32[32,512]{1,0:T(8,128)}, u32[]{:S(2)}) %copy-start.4) | copy-done | bytes 65560
  42.6 0.7 copy-done.5
  43.3 4.1 %shard_map.92 = (f32[4,32,512]{2,1,0:T(8,128)S(1)}, f32[2,32,512]{2,1,0:T(8,128)S(1)}, f32[2,32,512]{2,1,0:T(8,128)S(1)}) custom-call(f32[4]{0:T(128)S(1)} %copy-done.5, f32[1]{0:T(128)} %bitcast.6.beta_prev, f32[4,32,512]{2,1,0:T(8,128)} %v.9, f32[4,32,512]{2,1,0:T(8,128)S(1)} %copy-done.2, f32[2,3,4,32,512]{4,3,2,1,0:T(8,128)S(1)} %copy-done.1, ...), custom_call_target="tpu_custom_call" | custom-call | flops 8388608 | bytes 3572756 | tf_op jit(solution)/shard_map/pallas_call | solution.py:30
  47.5 0.1 collective-permute-start.12
  47.5 0.7 collective-permute-start.13
  48.2 7.7 %shard_map.93.gram = f32[3,128]{1,0:T(4,128)S(1)} custom-call(f32[16,4,32,512]{3,2,1,0:T(8,128)} %s.5, f32[4,32,512]{2,1,0:T(8,128)S(1)} %copy-done.7), custom_call_target="tpu_custom_call" | custom-call | flops 20971520 | bytes 4456448 | tf_op jit(solution)/shard_map/pallas_call | solution.py:30
  55.9 0.8 %shard_map.94 = (f32[4,32,512]{2,1,0:T(8,128)S(1)}, f32[32,3,128]{2,1,0:T(4,128)S(1)}) custom-call(f32[4,32,512]{2,1,0:T(8,128)S(1)} %get-tuple-element.50.part, f32[2,32,512]{2,1,0:T(8,128)S(1)} %collective-permute-done.12.got_a, f32[2,32,512]{2,1,0:T(8,128)S(1)} %collective-permute-done.13.got_b, f32[4,32,512]{2,1,0:T(8,128)S(1)} %copy-done.7, ...), custom_call_target="tpu_custom_call" | custom-call | bytes 4982272 | tf_op jit(solution)/shard_map/pallas_call | solution.py:30
  56.7 11.2 %all_to_all.5.msg = f32[32,3,128]{2,1,0:T(4,128)S(1)} all-to-all(f32[32,3,128]{2,1,0:T(4,128)S(1)} %get-tuple-element.53), channel_id=1, replica_groups=mesh['lon'=8,'lev'=4] {'lon','lev'}, dimensions={0} | all-to-all | bytes 98304 | tf_op jit(solution)/shard_map/all_to_all | solution.py:488
  67.9 1.5 %shard_map.95 = (f32[4,32,512]{2,1,0:T(8,128)S(1)}, f32[1,18]{1,0:T(1,128)S(1)}, f32[1,1]{1,0:T(1,128)}) custom-call(f32[32,3,128]{2,1,0:T(4,128)S(1)} %all_to_all.5.msg, f32[4,32,512]{2,1,0:T(8,128)S(1)} %get-tuple-element.54.applied, f32[4,32,512]{2,1,0:T(8,128)S(1)} %copy-done.7, f32[16,4,32,512]{3,2,1,0:T(8,128)S(1)} %copy-done.6), custom_call_target="tpu_custom_call" | custom-call | bytes 4767744 | tf_op jit(solution)/shard_map/pallas_call | solution.py:30
  70.1 0.7 copy-done.8
  70.8 0.5 copy-done.9
  (24 shorter events, 0.1 us)
Async XLA Ops:
  0.6 1.4 %copy-start = (f32[2,3,4,32,512]{4,3,2,1,0:T(8,128)S(1)}, f32[2,3,4,32,512]{4,3,2,1,0:T(8,128)}, u32[]{:S(2)}) copy-start(f32[2,3,4,32,512]{4,3,2,1,0:T(8,128)} %vel.3) | copy-start | bytes 4718596
  2.0 0.8 %copy-start.3 = (s32[32,512]{1,0:T(8,128)S(1)}, s32[32,512]{1,0:T(8,128)}, u32[]{:S(2)}) copy-start(s32[32,512]{1,0:T(8,128)} %owner.3) | copy-start | bytes 196612
  2.9 45.3 %copy-start.7 = (f32[4,32,512]{2,1,0:T(8,128)S(1)}, f32[4,32,512]{2,1,0:T(8,128)}, u32[]{:S(2)}) copy-start(f32[4,32,512]{2,1,0:T(8,128)} %v.9) | copy-start | bytes 786436
  4.1 35.3 %collective-permute-start.7 = (f32[5,32,512]{2,1,0:T(8,128)S(1)}, f32[5,32,512]{2,1,0:T(8,128)S(1)}, u32[]{:S(2)}, u32[]{:S(2)}) collective-permute-start(f32[5,32,512]{2,1,0:T(8,128)S(1)} %get-tuple-element.45), channel_id=1, source_target_pairs={{0,1},{1,0},{2,3},{3,2},{4,5},{5,4},{6,7},{7,6},{8,9},{9,8},{10,11... | collective-permute-start | bytes 983048 | tf_op jit(solution)/shard_map/ppermute | solution.py:435
  4.6 34.8 %collective-permute-start.8 = (f32[5,32,512]{2,1,0:T(8,128)S(1)}, f32[5,32,512]{2,1,0:T(8,128)S(1)}, u32[]{:S(2)}, u32[]{:S(2)}) collective-permute-start(f32[5,32,512]{2,1,0:T(8,128)S(1)} %get-tuple-element.46), channel_id=1, source_target_pairs={{0,3},{1,2},{2,1},{3,0},{4,7},{5,6},{6,5},{7,4},{8,11},{9,10},{10,... | collective-permute-start | bytes 983048 | tf_op jit(solution)/shard_map/ppermute | solution.py:435
  7.2 17.1 %collective-permute-start = (f32[56,512]{1,0:T(8,128)S(1)}, f32[56,512]{1,0:T(8,128)S(1)}, u32[]{:S(2)}, u32[]{:S(2)}) collective-permute-start(f32[56,512]{1,0:T(8,128)S(1)} %get-tuple-element.38), channel_id=1, source_target_pairs={{0,4},{4,8},{8,12},{12,16},{16,20},{20,24},{24,28},{28,0},{1,5},{5... | collective-permute-start | bytes 344072 | tf_op jit(solution)/shard_map/ppermute | solution.py:440
  8.8 15.6 %collective-permute-start.3 = (f32[56,512]{1,0:T(8,128)S(1)}, f32[56,512]{1,0:T(8,128)S(1)}, u32[]{:S(2)}, u32[]{:S(2)}) collective-permute-start(f32[56,512]{1,0:T(8,128)S(1)} %get-tuple-element.41), channel_id=1, source_target_pairs={{4,0},{8,4},{12,8},{16,12},{20,16},{24,20},{28,24},{0,28},{5,1},{9... | collective-permute-start | bytes 344072 | tf_op jit(solution)/shard_map/ppermute | solution.py:440
  12.0 4.2 %collective-permute-start.4 = (f32[1,128]{1,0:T(1,128)S(1)}, f32[1,128]{1,0:T(1,128)S(1)}, u32[]{:S(2)}, u32[]{:S(2)}) collective-permute-start(f32[1,128]{1,0:T(1,128)S(1)} %get-tuple-element.42.refs_0_), channel_id=1, source_target_pairs={{0,4},{4,0},{8,12},{12,8},{16,20},{20,16},{24,28},{28,24},{1,5},{5... | collective-permute-start | bytes 1544 | tf_op jit(solution)/shard_map/ppermute | solution.py:438
  16.1 3.5 %collective-permute-start.5 = (f32[1,128]{1,0:T(1,128)S(1)}, f32[1,128]{1,0:T(1,128)S(1)}, u32[]{:S(2)}, u32[]{:S(2)}) collective-permute-start(f32[1,128]{1,0:T(1,128)S(1)} %get-tuple-element.42.refs_0_), channel_id=1, source_target_pairs={{0,8},{4,12},{8,0},{12,4},{16,24},{20,28},{24,16},{28,20},{1,9},{5... | collective-permute-start | bytes 1544 | tf_op jit(solution)/shard_map/ppermute | solution.py:438
  19.7 4.4 %collective-permute-start.6 = (f32[1,128]{1,0:T(1,128)S(1)}, f32[1,128]{1,0:T(1,128)S(1)}, u32[]{:S(2)}, u32[]{:S(2)}) collective-permute-start(f32[1,128]{1,0:T(1,128)S(1)} %get-tuple-element.42.refs_0_), channel_id=1, source_target_pairs={{0,12},{4,8},{8,4},{12,0},{16,28},{20,24},{24,20},{28,16},{1,13},{... | collective-permute-start | bytes 1544 | tf_op jit(solution)/shard_map/ppermute | solution.py:438
  24.1 6.8 %collective-permute-start.1 = (f32[24,512]{1,0:T(8,128)S(1)}, f32[24,512]{1,0:T(8,128)S(1)}, u32[]{:S(2)}, u32[]{:S(2)}) collective-permute-start(f32[24,512]{1,0:T(8,128)S(1)} %get-tuple-element.39), channel_id=1, source_target_pairs={{0,4},{4,8},{8,12},{12,16},{16,20},{20,24},{24,28},{28,0},{1,5},{5... | collective-permute-start | bytes 147464 | tf_op jit(solution)/shard_map/ppermute | solution.py:443
  24.5 14.9 %collective-permute-start.10 = (f32[5,8,512]{2,1,0:T(8,128)S(1)}, f32[5,8,512]{2,1,0:T(8,128)S(1)}, u32[]{:S(2)}, u32[]{:S(2)}) collective-permute-start(f32[5,8,512]{2,1,0:T(8,128)S(1)} %get-tuple-element.48), channel_id=1, source_target_pairs={{0,3},{1,2},{2,1},{3,0},{4,7},{5,6},{6,5},{7,4},{8,11},{9,10},{10,... | collective-permute-start | bytes 245768 | tf_op jit(solution)/shard_map/ppermute | solution.py:435
  24.6 14.9 %collective-permute-start.9 = (f32[5,8,512]{2,1,0:T(8,128)S(1)}, f32[5,8,512]{2,1,0:T(8,128)S(1)}, u32[]{:S(2)}, u32[]{:S(2)}) collective-permute-start(f32[5,8,512]{2,1,0:T(8,128)S(1)} %get-tuple-element.47), channel_id=1, source_target_pairs={{0,1},{1,0},{2,3},{3,2},{4,5},{5,4},{6,7},{7,6},{8,9},{9,8},{10,11... | collective-permute-start | bytes 245768 | tf_op jit(solution)/shard_map/ppermute | solution.py:435
  30.9 4.1 %collective-permute-start.2 = (f32[24,512]{1,0:T(8,128)S(1)}, f32[24,512]{1,0:T(8,128)S(1)}, u32[]{:S(2)}, u32[]{:S(2)}) collective-permute-start(f32[24,512]{1,0:T(8,128)S(1)} %get-tuple-element.40), channel_id=1, source_target_pairs={{4,0},{8,4},{12,8},{16,12},{20,16},{24,20},{28,24},{0,28},{5,1},{9... | collective-permute-start | bytes 147464 | tf_op jit(solution)/shard_map/ppermute | solution.py:443
  35.0 4.4 %collective-permute-start.11 = (f32[1,128]{1,0:T(1,128)S(1)}, f32[1,128]{1,0:T(1,128)S(1)}, u32[]{:S(2)}, u32[]{:S(2)}) collective-permute-start(f32[1,128]{1,0:T(1,128)S(1)} %get-tuple-element.49.refs_0_), channel_id=1, source_target_pairs={{0,16},{4,20},{8,24},{12,28},{16,0},{20,4},{24,8},{28,12},{1,17},{... | collective-permute-start | bytes 1544 | tf_op jit(solution)/shard_map/ppermute | solution.py:438
  39.4 1.4 %copy-start.1 = (f32[2,3,4,32,512]{4,3,2,1,0:T(8,128)S(1)}, f32[2,3,4,32,512]{4,3,2,1,0:T(8,128)}, u32[]{:S(2)}) copy-start(f32[2,3,4,32,512]{4,3,2,1,0:T(8,128)} %vel.3) | copy-start | bytes 4718596
  40.8 0.9 %copy-start.2 = (f32[4,32,512]{2,1,0:T(8,128)S(1)}, f32[4,32,512]{2,1,0:T(8,128)}, u32[]{:S(2)}) copy-start(f32[4,32,512]{2,1,0:T(8,128)} %prev.1) | copy-start | bytes 786436
  41.8 0.8 %copy-start.4 = (s32[32,512]{1,0:T(8,128)S(1)}, s32[32,512]{1,0:T(8,128)}, u32[]{:S(2)}) copy-start(s32[32,512]{1,0:T(8,128)} %owner.3) | copy-start | bytes 196612
  42.6 0.7 copy-start.5
  43.3 12.6 %copy-start.6 = (f32[16,4,32,512]{3,2,1,0:T(8,128)S(1)}, f32[16,4,32,512]{3,2,1,0:T(8,128)}, u32[]{:S(2)}) copy-start(f32[16,4,32,512]{3,2,1,0:T(8,128)} %s.5) | copy-start | bytes 12582916
  47.5 8.4 %collective-permute-start.12 = (f32[2,32,512]{2,1,0:T(8,128)S(1)}, f32[2,32,512]{2,1,0:T(8,128)S(1)}, u32[]{:S(2)}, u32[]{:S(2)}) collective-permute-start(f32[2,32,512]{2,1,0:T(8,128)S(1)} %get-tuple-element.51), channel_id=1, source_target_pairs={{0,1},{1,0},{2,3},{3,2},{4,5},{5,4},{6,7},{7,6},{8,9},{9,8},{10,11... | collective-permute-start | bytes 393224 | tf_op jit(solution)/shard_map/ppermute | solution.py:435
  47.5 8.4 %collective-permute-start.13 = (f32[2,32,512]{2,1,0:T(8,128)S(1)}, f32[2,32,512]{2,1,0:T(8,128)S(1)}, u32[]{:S(2)}, u32[]{:S(2)}) collective-permute-start(f32[2,32,512]{2,1,0:T(8,128)S(1)} %get-tuple-element.52), channel_id=1, source_target_pairs={{0,3},{1,2},{2,1},{3,0},{4,7},{5,6},{6,5},{7,4},{8,11},{9,10},{10,... | collective-permute-start | bytes 393224 | tf_op jit(solution)/shard_map/ppermute | solution.py:435
  70.1 0.7 copy-start.8
  70.8 0.5 copy-start.9

commit v2 on v1

--- a/solution.py
+++ b/solution.py
@@ -14,25 +14,28 @@
 
 VM = pl.BlockSpec(memory_space=pltpu.VMEM)
 SM = pl.BlockSpec(memory_space=pltpu.SMEM)
+ANY = pl.BlockSpec(memory_space=pl.ANY)
 CHUNK = 8
 WIDE = 4
 SECOND = 2
 V_ROWS, A_ROWS, B_ROWS = 4, 3, 2
-LEVEL_ROWS = V_ROWS + 3 * A_ROWS
+LEVEL_ROWS = V_ROWS + 3 * (A_ROWS + B_ROWS)
+B_AT = V_ROWS + 3 * A_ROWS
 
 
 def sds(*shape):
     return jax.ShapeDtypeStruct(shape, f32)
 
 
-def call(kernel, outs, operands, specs=None, scratch=(), flops=0):
+def call(kernel, outs, operands, specs=None, scratch=(), flops=0, alias=None, out_specs=None):
     nbytes = sum(4 * x.size for x in operands)
     return pl.pallas_call(
         kernel,
         out_shape=outs,
         in_specs=specs or [VM] * len(operands),
-        out_specs=jax.tree.map(lambda _: VM, outs),
+        out_specs=out_specs or jax.tree.map(lambda _: VM, outs),
         scratch_shapes=list(scratch),
+        input_output_aliases=alias or {},
         compiler_params=pltpu.CompilerParams(vmem_limit_bytes=40 << 20),
         cost_estimate=pl.CostEstimate(flops=flops, bytes_accessed=nbytes, transcendentals=0),
     )(*operands)
@@ -46,29 +49,31 @@
     return lax.rem(lax.axis_index("lev"), 2) == 0
 
 
-def pack_kernel(levels, cols, v, vel, owner, lo_a, lo_b, hi_a, hi_b, lev_a, lev_b, counts):
-    for msg_a, msg_b, low in ((lo_a, lo_b, True), (hi_a, hi_b, False)):
-
-        def edge(n):
-            return slice(0, n) if low else slice(cols - n, cols)
-
+def pack_kernel(
+    levels, cols, v_hbm, vel_hbm, owner_hbm, lo, hi, lev_a, lev_b, counts, v, vel, owner, sems
+):
+    copies = [pltpu.make_async_copy(v_hbm, v, sems.at[0]), pltpu.make_async_copy(owner_hbm, owner, sems.at[1])]
+    for section in range(2):
+        for comp in range(3):
+            sem = sems.at[2 + 3 * section + comp]
+            copies.append(pltpu.make_async_copy(vel_hbm.at[section, comp], vel.at[section, comp], sem))
+    for copy in copies:
+        copy.start()
+
+    def edge(low, n):
+        return slice(0, n) if low else slice(cols - n, cols)
+
+    sides = ((lo, True), (hi, False))
+    even = even_level()
+    tops = ((lev_a, even), (lev_b, jnp.logical_not(even)))
+    copies[0].wait()
+    for msg, low in sides:
         for lev in range(levels):
-            base = lev * LEVEL_ROWS
-            msg_a[base : base + V_ROWS] = v[lev, edge(V_ROWS)]
-            for comp in range(3):
-                at = base + V_ROWS + comp * A_ROWS
-                msg_a[at : at + A_ROWS] = vel[0, comp, lev, edge(A_ROWS)]
-                at = (lev * 3 + comp) * B_ROWS
-                msg_b[at : at + B_ROWS] = vel[1, comp, lev, edge(B_ROWS)]
-        at = levels * LEVEL_ROWS
-        msg_a[at : at + B_ROWS] = owner[edge(B_ROWS)].astype(f32)
-    even = even_level()
-    for msg, top in ((lev_a, even), (lev_b, jnp.logical_not(even))):
-        near = jnp.where(top, levels - 1, 0)
-        msg[0] = v[near]
+            msg[lev * LEVEL_ROWS : lev * LEVEL_ROWS + V_ROWS] = v[lev, edge(low, V_ROWS)]
+    for msg, top in tops:
+        msg[0] = v[jnp.where(top, levels - 1, 0)]
         msg[1] = v[jnp.where(top, levels - 2, 1)]
-        for comp in range(3):
-            msg[2 + comp] = vel[0, comp, near]
+    copies[1].wait()
     lanes = lane_iota((1, 128))
     row = jnp.zeros((1, 128), f32)
     held = owner[...]
@@ -76,19 +81,38 @@
         hot = jnp.sum((held == box).astype(f32), axis=0, keepdims=True)
         row = jnp.where(lanes == box - 1, jnp.sum(hot, axis=1, keepdims=True), row)
     counts[...] = row
-
-
-def corner_kernel(levels, n_counts, west, east, *refs):
-    count_refs, (halo_v, halo_a, corner_a, corner_b, counts) = refs[:n_counts], refs[n_counts:]
+    at = levels * LEVEL_ROWS
+    for msg, low in sides:
+        msg[at : at + B_ROWS] = owner[edge(low, B_ROWS)].astype(f32)
+        msg[at + B_ROWS : at + B_ROWS + 1, 0:128] = row
+    for section, n, start in ((0, A_ROWS, V_ROWS), (1, B_ROWS, B_AT)):
+        for comp in range(3):
+            copies[2 + 3 * section + comp].wait()
+            for msg, low in sides:
+                for lev in range(levels):
+                    at = lev * LEVEL_ROWS + start + comp * n
+                    msg[at : at + n] = vel[section, comp, lev, edge(low, n)]
+            if section == 0:
+                for msg, top in tops:
+                    msg[2 + comp] = vel[0, comp, jnp.where(top, levels - 1, 0)]
+
+
+def corner_kernel(levels, west, east, counts, counts_2, gram, halo_v, halo_a, halo_b, corner_a, corner_b, window):
     halo_a[...] = jnp.zeros(halo_a.shape, f32)
+    halo_b[...] = jnp.zeros(halo_b.shape, f32)
     for lev in range(levels):
-        base = lev * LEVEL_ROWS
-        halo_v[lev, 0:V_ROWS] = east[base : base + V_ROWS]
-        halo_v[lev, CHUNK - V_ROWS : CHUNK] = west[base : base + V_ROWS]
-        for comp in range(3):
-            at = base + V_ROWS + comp * A_ROWS
-            halo_a[comp, lev, 0:A_ROWS] = east[at : at + A_ROWS]
-            halo_a[comp, lev, CHUNK - A_ROWS : CHUNK] = west[at : at + A_ROWS]
+        for msg, low in ((east, True), (west, False)):
+
+            def edge(n):
+                return slice(0, n) if low else slice(CHUNK - n, CHUNK)
+
+            base = lev * LEVEL_ROWS
+            halo_v[lev, edge(V_ROWS)] = msg[base : base + V_ROWS]
+            for comp in range(3):
+                at = base + V_ROWS + comp * A_ROWS
+                halo_a[comp, lev, edge(A_ROWS)] = msg[at : at + A_ROWS]
+                at = base + B_AT + comp * B_ROWS
+                halo_b[comp, lev, edge(B_ROWS)] = msg[at : at + B_ROWS]
     even = even_level()
     for msg, top in ((corner_a, even), (corner_b, jnp.logical_not(even))):
         near = jnp.where(top, levels - 1, 0)
@@ -96,20 +120,18 @@
         msg[1] = halo_v[jnp.where(top, levels - 2, 1)]
         for comp in range(3):
             msg[2 + comp] = halo_a[comp, near]
-    total = count_refs[0][...]
-    for ref in count_refs[1:]:
-        total = total + ref[...]
-    counts[...] = total
+    at = levels * LEVEL_ROWS + B_ROWS
+    window[...] = counts[...] + counts_2[...] + west[at : at + 1, 0:128] + east[at : at + 1, 0:128]
 
 
 def stencil_kernel(
     levels, cols, lat, columns, n_counts,
-    lw, beta_prev, v, prev, vel, owner, west, west_b, east_b, east, halo_v, halo_a,
+    lw, beta_prev, v, prev, vel, owner, west, east, halo_v, halo_a, halo_b,
     lev_a, lev_b, corner_a, corner_b, *refs,
 ):
     count_refs = refs[:n_counts]
     applied, send_a, send_b = refs[n_counts : n_counts + 3]
-    (vv, la, ff, halo_b, own_h, w_in, w_e, w_w, w_u, w_d, u_in, u_e, u_w, u_u, u_d, out) = refs[n_counts + 3 :]
+    (vv, la, ff, own_h, w_in, w_e, w_w, w_u, w_d, u_in, u_e, u_w, u_u, u_d, out) = refs[n_counts + 3 :]
     chunks = cols // CHUNK
     level = lax.axis_index("lev")
     last = lax.axis_size("lev") - 1
@@ -157,12 +179,6 @@
                 la[1, item - 2, cells] = above
         for lev in range(levels):
             put_both(vv, lev + 2, k, v[lev, cells] if k < chunks else halo_v[lev])
-    halo_b[...] = jnp.zeros(halo_b.shape, f32)
-    for lev in range(levels):
-        for comp in range(3):
-            at = (lev * 3 + comp) * B_ROWS
-            halo_b[comp, lev, 0:B_ROWS] = east_b[at : at + B_ROWS]
-            halo_b[comp, lev, CHUNK - B_ROWS : CHUNK] = west_b[at : at + B_ROWS]
     own_h[...] = jnp.zeros(own_h.shape, f32)
     at = levels * LEVEL_ROWS
     own_h[0:B_ROWS] = east[at : at + B_ROWS]
@@ -284,7 +300,7 @@
     return [slice(t, t + 128) for t in range(0, lat, 128)]
 
 
-def gram_kernel(nvec, levels, cols, lat, s, v, out, sums):
+def gram_kernel(nvec, levels, cols, lat, s, v, prev, order, out, s_out, prev_out, sums):
     sums[...] = jnp.zeros(sums.shape, f32)
     steps = levels * (cols // CHUNK)
     block = 4
@@ -305,7 +321,7 @@
                     acc = tuple(x + held[i] * held[j] for x, (i, j) in zip(acc, pairs))
                 return acc
 
-            acc = lax.fori_loop(0, steps, body, tuple(jnp.zeros((CHUNK, 128), f32) for _ in pairs))
+            acc = lax.fori_loop(0, steps, body, tuple(jnp.zeros((CHUNK, 128), f32) for _ in pairs), unroll=4)
             for (i, j), x in zip(pairs, acc):
                 put_sum(sums, nvec * i + j, x)
 
@@ -316,7 +332,7 @@
             acc = tuple(y + x * s[i, lev, cells, t] for i, y in enumerate(acc[:-1])) + (acc[-1] + x * x,)
         return acc
 
-    acc = lax.fori_loop(0, steps, body_v, tuple(jnp.zeros((CHUNK, 128), f32) for _ in range(nvec + 1)))
+    acc = lax.fori_loop(0, steps, body_v, tuple(jnp.zeros((CHUNK, 128), f32) for _ in range(nvec + 1)), unroll=2)
     base = nvec * nvec
     for i in range(nvec):
         put_sum(sums, base + nvec + i, acc[i])
@@ -351,7 +367,7 @@
             )
         return acc
 
-    acc = lax.fori_loop(0, steps, body, tuple(jnp.zeros((CHUNK, 128), f32) for _ in range(nvec + 2)))
+    acc = lax.fori_loop(0, steps, body, tuple(jnp.zeros((CHUNK, 128), f32) for _ in range(nvec + 2)), unroll=2)
     for i in range(nvec):
         put_sum(sums, i, acc[i])
     put_sum(sums, 2 * nvec, acc[nvec])
@@ -362,7 +378,7 @@
     msg[:, r : r + 1] = jnp.broadcast_to(row[None], (count, 1, 128))
 
 
-def finish_kernel(nvec, levels, cols, lat, cells_all, count, msg, applied, v, s, result, coefs, trust):
+def finish_kernel(nvec, levels, cols, lat, cells_all, msg, applied, v, s, result_out, coefs_out, trust, result, coefs, sems):
     total = jnp.sum(msg[...], axis=0) * (1.0 / cells_all)
     r = total.shape[0] - 1
     row = total[r : r + 1]
@@ -393,22 +409,29 @@
     inverse = 1.0 / beta
     line = jnp.where(lanes == 0, alpha, jnp.where(lanes == 1, beta, pltpu.roll(pv, 2, 1)))
     coefs[...] = line[:, 0 : nvec + 2]
+    copies = [pltpu.make_async_copy(result.at[lev], result_out.at[lev], sems.at[lev]) for lev in range(levels)]
+    copies.append(pltpu.make_async_copy(coefs, coefs_out, sems.at[levels]))
+    copies[-1].start()
     weights = [jnp.broadcast_to(x * inverse, (CHUNK, 128)) for x in p]
     a_w = jnp.broadcast_to(alpha * inverse, (CHUNK, 128))
     scale = jnp.broadcast_to(inverse, (CHUNK, 128))
 
-    def body(step, carry):
-        lev = step // (cols // CHUNK)
-        at = pl.ds(pl.multiple_of((step - lev * (cols // CHUNK)) * CHUNK, CHUNK), CHUNK)
-        for t in tiles(lat):
-            x = scale * applied[lev, at, t] - a_w * v[lev, at, t]
-            y = weights[0] * s[0, lev, at, t]
-            for k in range(1, nvec):
-                y = y + weights[k] * s[k, lev, at, t]
-            result[lev, at, t] = x - y
-        return carry
-
-    lax.fori_loop(0, levels * (cols // CHUNK), body, 0)
+    for lev in range(levels):
+
+        def body(step, carry, lev=lev):
+            at = pl.ds(pl.multiple_of(step * CHUNK, CHUNK), CHUNK)
+            for t in tiles(lat):
+                x = scale * applied[lev, at, t] - a_w * v[lev, at, t]
+                y = weights[0] * s[0, lev, at, t]
+                for k in range(1, nvec):
+                    y = y + weights[k] * s[k, lev, at, t]
+                result[lev, at, t] = x - y
+            return carry
+
+        lax.fori_loop(0, cols // CHUNK, body, 0)
+        copies[lev].start()
+    for copy in copies:
+        copy.wait()
 
 
 def body(v, prev, beta_prev, s, vel, lw, owner):
@@ -416,15 +439,14 @@
     count = lon_n * lev_n
     levels, cols, lat = v.shape
     nvec = s.shape[0]
-    lines = levels * LEVEL_ROWS + B_ROWS
+    lines = levels * LEVEL_ROWS + B_ROWS + 1
     lines += -lines % CHUNK
-    lines_b = levels * 3 * B_ROWS
-
-    lo_a, lo_b, hi_a, hi_b, lev_a, lev_b, counts = call(
+
+    lo, hi, lev_a, lev_b, counts, v, vel, owner = call(
         functools.partial(pack_kernel, levels, cols),
-        (sds(lines, lat), sds(lines_b, lat), sds(lines, lat), sds(lines_b, lat),
-         sds(5, cols, lat), sds(5, cols, lat), sds(1, 128)),
-        (v, vel, owner), flops=1 << 20,
+        (sds(lines, lat), sds(lines, lat), sds(5, cols, lat), sds(5, cols, lat), sds(1, 128),
+         sds(*v.shape), sds(*vel.shape), jax.ShapeDtypeStruct(owner.shape, owner.dtype)),
+        (v, vel, owner), specs=[ANY] * 3, scratch=[pltpu.SemaphoreType.DMA((8,))], flops=1 << 20,
     )
     east_of = [(i, (i + 1) % lon_n) for i in range(lon_n)]
     west_of = [((i + 1) % lon_n, i) for i in range(lon_n)]
@@ -434,44 +456,39 @@
     def both(a, b):
         return lax.ppermute(a, "lev", pairs_a), lax.ppermute(b, "lev", pairs_b)
 
-    def across(x, k):
-        return lax.ppermute(x, "lon", [(i, i ^ k) for i in range(lon_n)])
-
-    west, east = lax.ppermute(hi_a, "lon", east_of), lax.ppermute(lo_a, "lon", west_of)
+    west, east = lax.ppermute(hi, "lon", east_of), lax.ppermute(lo, "lon", west_of)
     lev_a, lev_b = both(lev_a, lev_b)
-    near = [counts] + [across(counts, k) for k in (1, 2, 3)]
-    west_b, east_b = lax.ppermute(hi_b, "lon", east_of), lax.ppermute(lo_b, "lon", west_of)
+    counts_2 = lax.ppermute(counts, "lon", [((i + 2) % lon_n, i) for i in range(lon_n)])
 
     gram_rows = nvec * nvec // 128 + 1
-    gram = call(
+    gram, s, prev = call(
         functools.partial(gram_kernel, nvec, levels, cols, lat),
-        sds(gram_rows, 128), (s, v),
-        scratch=[pltpu.VMEM((128 * gram_rows, 128), f32)], flops=20 << 20,
-    )
-
-    halo_v, halo_a, corner_a, corner_b, counts = call(
-        functools.partial(corner_kernel, levels, len(near)),
-        (sds(levels, CHUNK, lat), sds(3, levels, CHUNK, lat), sds(5, CHUNK, lat), sds(5, CHUNK, lat), sds(1, 128)),
-        (west, east, *near),
+        (sds(gram_rows, 128), sds(*s.shape), sds(*prev.shape)), (s, v, prev, counts),
+        scratch=[pltpu.VMEM((128 * gram_rows, 128), f32)], flops=20 << 20, alias={0: 1, 2: 2},
+    )
+
+    halo_v, halo_a, halo_b, corner_a, corner_b, window = call(
+        functools.partial(corner_kernel, levels),
+        (sds(levels, CHUNK, lat), sds(3, levels, CHUNK, lat), sds(3, levels, CHUNK, lat),
+         sds(5, CHUNK, lat), sds(5, CHUNK, lat), sds(1, 128)),
+        (west, east, counts, counts_2, gram),
     )
     corner_a, corner_b = both(corner_a, corner_b)
-    step = 4
-    while 2 * step < lon_n:
-        counts = counts + across(counts, step)
-        step *= 2
-    near = [counts, across(counts, step)]
+    if lon_n == 8:
+        near = [window, lax.ppermute(window, "lon", [(i, i ^ 4) for i in range(lon_n)])]
+    else:
+        near = [lax.psum(counts, "lon")]
 
     padded = cols + 3 * CHUNK
     scratch = [
         pltpu.VMEM((levels + 4, padded, lat), f32),
         pltpu.VMEM((2, 3, cols + CHUNK, lat), f32),
         pltpu.VMEM((levels + 2, padded, lat), f32),
-        pltpu.VMEM((3, levels, CHUNK, lat), f32),
         pltpu.VMEM((CHUNK, lat), f32),
     ]
     scratch += [pltpu.VMEM((levels + 2, padded, lat), f32)] * 10
     scratch += [pltpu.VMEM((levels + 4, cols + CHUNK, lat), f32)]
-    operands = (lw, beta_prev.reshape(1), v, prev, vel, owner, west, west_b, east_b, east, halo_v, halo_a,
+    operands = (lw, beta_prev.reshape(1), v, prev, vel, owner, west, east, halo_v, halo_a, halo_b,
                 lev_a, lev_b, corner_a, corner_b, *near)
     part, send_a, send_b = call(
         functools.partial(stencil_kernel, levels, cols, lat, float(cols * lon_n * lat), len(near)),
@@ -488,9 +505,11 @@
     msg = lax.all_to_all(msg, ("lon", "lev"), 0, 0, tiled=True)
     cells = float(v.size * count)
     result, coefs, trust = call(
-        functools.partial(finish_kernel, nvec, levels, cols, lat, cells, count),
+        functools.partial(finish_kernel, nvec, levels, cols, lat, cells),
         (sds(levels, cols, lat), sds(1, nvec + 2), sds(1, 1)),
-        (msg, applied, v, s),
+        (msg, applied, v, s), out_specs=(ANY, ANY, VM),
+        scratch=[pltpu.VMEM((levels, cols, lat), f32), pltpu.VMEM((1, nvec + 2), f32),
+                 pltpu.SemaphoreType.DMA((levels + 1,))],
     )
     coefs = coefs.reshape(nvec + 2)
 

time: 71.7 us -> 52 us (0.73)
  waiting for transfers between devices: 22.7 us -> 6.43 us
  local copies, waits for them, and re-layouts: 7.3 us -> 2.78 us
  starting transfers between devices: 12.6 us -> 13.8 us
    ppermute x8 -> x4, waiting for transfers between devices: 22.7 us -> 2.74 us  [the longest x1 1.99 us: body(): lax.ppermute(window, 'lon', [(i, i ^ 4) for i in range(lon_n)])]
    unnamed x20 -> x25, local copies, waits for them, and re-layouts: 7.3 us -> 2.78 us
    ppermute x6, waiting for transfers between devices: 0.02 us -> 3.69 us  [both(): return (lax.ppermute(a, 'lev', pairs_a), lax.ppermute(b, 'lev', pairs_b))]
    ppermute x6, starting transfers between devices: 4.56 us -> 5.46 us  [both(): return (lax.ppermute(a, 'lev', pairs_a), lax.ppermute(b, 'lev', pairs_b))]
    ppermute x8 -> x4, starting transfers between devices: 8.01 us -> 8.32 us  [the longest x1 3.2 us: body(): lax.ppermute(lo, 'lon', west_of)]
  transfers between devices with their start and end apart: 14 -> 10, of which waited for: 6 -> 3; matrix products, arithmetic and copies ran while one was open for 0% -> 0% of each run, Pallas kernels for 11% -> 9%
where the time goes in v2:
time: 52 us; the launch traced here: 51.8 us
  Pallas kernels  15.3 us (29%)
  starting transfers between devices  13.8 us (27%)
  blocking collectives  11.4 us (22%)
  waiting for transfers between devices  6.43 us (12%)
  local copies, waits for them, and re-layouts  2.78 us (5%)
  between operations  2.12 us (4%)
    pallas_call x6, Pallas kernels, call(): pl.pallas_call(kernel, out_shape=outs, in_specs=specs or [VM] * len(opera...  15.3 us
    all_to_all x1, blocking collectives, body(): msg = lax.all_to_all(msg, ('lon', 'lev'), 0, 0, tiled=True)  11.4 us
    ppermute x6, starting transfers between devices, both(): return (lax.ppermute(a, 'lev', pairs_a), lax.ppermute(b, 'lev', pairs_b))  5.46 us
    ppermute x6, waiting for transfers between devices, both(): return (lax.ppermute(a, 'lev', pairs_a), lax.ppermute(b, 'lev', pairs_b))  3.69 us
    ppermute x1, starting transfers between devices, body(): lax.ppermute(lo, 'lon', west_of)  3.2 us
    unnamed x25, local copies, waits for them, and re-layouts  2.78 us
    ppermute x1, waiting for transfers between devices, body(): lax.ppermute(window, 'lon', [(i, i ^ 4) for i in range(lon_n)])  1.99 us
    ppermute x1, starting transfers between devices, body(): lax.ppermute(counts, 'lon', [((i + 2) % lon_n, i) for i in range(lon_n)])  1.8 us
  transfers between devices with their start and end apart: 10, of which 3 were waited for; matrix products, arithmetic and copies ran while one was open for 0% of the time, Pallas kernels for 9%

profile of v2, /device:TPU:0, one launch (start us, length us, event | category | flops | bytes accessed | tf_op | source)
XLA Modules:
  0.0 51.8 jit_solution(10918807955820371840)
XLA Ops:
  0.7 1.0 %copy-done.9 = f32[4,32,512]{2,1,0:T(8,128)S(1)} copy-done((f32[4,32,512]{2,1,0:T(8,128)S(1)}, f32[4,32,512]{2,1,0:T(8,128)}, u32[]{:S(2)}) %copy-start.9) | copy-done | bytes 262168
  1.7 0.0 copy-done.1
  1.7 0.6 %copy-done = f32[2,3,4,32,512]{4,3,2,1,0:T(8,128)S(1)} copy-done((f32[2,3,4,32,512]{4,3,2,1,0:T(8,128)S(1)}, f32[2,3,4,32,512]{4,3,2,1,0:T(8,128)}, u32[]{:S(2)}) %copy-start) | copy-done | bytes 1572888
  2.2 1.4 %shard_map.90 = (f32[80,512]{1,0:T(8,128)S(1)}, f32[80,512]{1,0:T(8,128)S(1)}, f32[5,32,512]{2,1,0:T(8,128)}, f32[5,32,512]{2,1,0:T(8,128)}, f32[1,128]{1,0:T(1,...) custom-call(f32[4,32,512]{2,1,0:T(8,128)S(1)} %copy-done.1, ...), custom_call_target="tpu_custom_call" | custom-call | flops 1048576 | bytes 1900544 | tf_op jit(solution)/shard_map/pallas_call | solution.py:32
  3.7 0.0 copy-start.7
  3.7 0.5 collective-permute-start.3
  4.2 2.6 %collective-permute-start.4 = (f32[5,32,512]{2,1,0:T(8,128)}, f32[5,32,512]{2,1,0:T(8,128)S(1)}, u32[]{:S(2)}, u32[]{:S(2)}) collective-permute-start(f32[5,32,512]{2,1,0:T(8,128)} %get-tuple-element.55), channel_id=1, source_target_pairs={{0,3},{1,2},{2,1},{3,0},{4,7},{5,6},{6,5},{7,4},{8,11},{9,10},{10,... | collective-permute-start | bytes 983048 | tf_op jit(solution)/shard_map/ppermute | solution.py:457
  6.8 1.5 %collective-permute-start = (f32[80,512]{1,0:T(8,128)S(1)}, f32[80,512]{1,0:T(8,128)S(1)}, u32[]{:S(2)}, u32[]{:S(2)}) collective-permute-start(f32[80,512]{1,0:T(8,128)S(1)} %get-tuple-element.48), channel_id=1, source_target_pairs={{0,4},{4,8},{8,12},{12,16},{16,20},{20,24},{24,28},{28,0},{1,5},{5... | collective-permute-start | bytes 491528 | tf_op jit(solution)/shard_map/ppermute | solution.py:459
  8.3 3.2 %collective-permute-start.1 = (f32[80,512]{1,0:T(8,128)S(1)}, f32[80,512]{1,0:T(8,128)S(1)}, u32[]{:S(2)}, u32[]{:S(2)}) collective-permute-start(f32[80,512]{1,0:T(8,128)S(1)} %get-tuple-element.49), channel_id=1, source_target_pairs={{4,0},{8,4},{12,8},{16,12},{20,16},{24,20},{28,24},{0,28},{5,1},{9... | collective-permute-start | bytes 491528 | tf_op jit(solution)/shard_map/ppermute | solution.py:459
  11.5 1.8 %collective-permute-start.2 = (f32[1,128]{1,0:T(1,128)S(1)}, f32[1,128]{1,0:T(1,128)S(1)}, u32[]{:S(2)}, u32[]{:S(2)}) collective-permute-start(f32[1,128]{1,0:T(1,128)S(1)} %get-tuple-element.44.order.counts), channel_id=1, source_target_pairs={{8,0},{12,4},{16,8},{20,12},{24,16},{28,20},{0,24},{4,28},{9,1},{1... | collective-permute-start | bytes 1544 | tf_op jit(solution)/shard_map/ppermute | solution.py:461
  13.3 3.6 %shard_map.91 = (f32[3,128]{1,0:T(4,128)S(1)}, f32[16,4,32,512]{3,2,1,0:T(8,128)S(1)}, f32[4,32,512]{2,1,0:T(8,128)S(1)}) custom-call(f32[16,4,32,512]{3,2,1,0:T(8,128)S(1)} %copy-done.6, f32[4,32,512]{2,1,0:T(8,128)S(1)} %get-tuple-element.43.v, f32[4,32,512]{2,1,0:T(8,128)S(1)} %copy.26.prev, ...), custom_call_target="tpu_custom_call", output_to_operand_aliasing={{1}: (0, {}), {2}: (2, {})} | custom-call | flops 20971520 | bytes 4719104 | tf_op jit(solution)/shard_map/pallas_call | solution.py:32
  17.0 0.0 collective-permute-done.2.counts_2
  17.0 0.7 %collective-permute-done.1.east = f32[80,512]{1,0:T(8,128)S(1)} collective-permute-done((f32[80,512]{1,0:T(8,128)S(1)}, f32[80,512]{1,0:T(8,128)S(1)}, u32[]{:S(2)}, u32[]{:S(2)}) %collective-permute-start.1) | collective-permute-done | bytes 163872 | tf_op jit(solution)/shard_map/ppermute | solution.py:459
  17.7 1.2 %shard_map.92 = (f32[4,8,512]{2,1,0:T(8,128)S(1)}, f32[3,4,8,512]{3,2,1,0:T(8,128)S(1)}, f32[3,4,8,512]{3,2,1,0:T(8,128)S(1)}, f32[5,8,512]{2,1,0:T(8,128)}, f32[5,8,512]{2,1,0:T(8,128)}, /*index=5*/f32[1,128]{1,0:T(1,128)S(1)}) custom-call(f32[80,512]{1,0:T(8,128)S(1)} %collective-permute-done.west, f32[80,512]{1,0:T(8,128)S(1)} %collective-permute-done.1.east, ...), custom_call_target="tpu_custom_call" | custom-call | bytes 330240 | tf_op jit(solution)/shard_map/pallas_call | solution.py:32
  19.0 0.6 %collective-permute-start.6 = (f32[5,8,512]{2,1,0:T(8,128)}, f32[5,8,512]{2,1,0:T(8,128)S(1)}, u32[]{:S(2)}, u32[]{:S(2)}) collective-permute-start(f32[5,8,512]{2,1,0:T(8,128)} %get-tuple-element.57), channel_id=1, source_target_pairs={{0,3},{1,2},{2,1},{3,0},{4,7},{5,6},{6,5},{7,4},{8,11},{9,10},{10,... | collective-permute-start | bytes 245768 | tf_op jit(solution)/shard_map/ppermute | solution.py:457
  19.6 1.8 %collective-permute-start.7 = (f32[1,128]{1,0:T(1,128)S(1)}, f32[1,128]{1,0:T(1,128)S(1)}, u32[]{:S(2)}, u32[]{:S(2)}) collective-permute-start(f32[1,128]{1,0:T(1,128)S(1)} %get-tuple-element.58.refs_0_), channel_id=1, source_target_pairs={{0,16},{4,20},{8,24},{12,28},{16,0},{20,4},{24,8},{28,12},{1,17},{... | collective-permute-start | bytes 1544 | tf_op jit(solution)/shard_map/ppermute | solution.py:478
  22.1 2.0 %collective-permute-done.7.refs_1_ = f32[1,128]{1,0:T(1,128)S(1)} collective-permute-done((f32[1,128]{1,0:T(1,128)S(1)}, f32[1,128]{1,0:T(1,128)S(1)}, u32[]{:S(2)}, u32[]{:S(2)}) %collective-permute-start.7) | collective-permute-done | bytes 544 | tf_op jit(solution)/shard_map/ppermute | solution.py:478
  24.1 0.0 collective-permute-done.5.corner_a
  24.1 0.0 collective-permute-done.6.corner_b
  24.1 0.0 collective-permute-done.3.lev_a
  24.1 0.0 collective-permute-done.4.lev_b
  24.1 0.0 copy-start.8
  24.1 4.2 %shard_map.93 = (f32[4,32,512]{2,1,0:T(8,128)S(1)}, f32[2,32,512]{2,1,0:T(8,128)S(1)}, f32[2,32,512]{2,1,0:T(8,128)S(1)}) custom-call(f32[4]{0:T(128)S(1)} %copy-done.3, f32[1]{0:T(128)} %bitcast.6.beta_prev, f32[4,32,512]{2,1,0:T(8,128)} %copy-done.7, f32[4,32,512]{2,1,0:T(8,128)S(1)} %get-tuple-element.45.prev, ...), custom_call_target="tpu_custom_call" | custom-call | flops 8388608 | bytes 3769364 | tf_op jit(solution)/shard_map/pallas_call | solution.py:32
  28.3 0.1 collective-permute-start.8
  28.4 1.6 %collective-permute-start.9 = (f32[2,32,512]{2,1,0:T(8,128)S(1)}, f32[2,32,512]{2,1,0:T(8,128)S(1)}, u32[]{:S(2)}, u32[]{:S(2)}) collective-permute-start(f32[2,32,512]{2,1,0:T(8,128)S(1)} %get-tuple-element.61), channel_id=1, source_target_pairs={{0,3},{1,2},{2,1},{3,0},{4,7},{5,6},{6,5},{7,4},{8,11},{9,10},{10,... | collective-permute-start | bytes 393224 | tf_op jit(solution)/shard_map/ppermute | solution.py:457
  30.0 3.7 %collective-permute-done.9.got_b = f32[2,32,512]{2,1,0:T(8,128)S(1)} collective-permute-done((f32[2,32,512]{2,1,0:T(8,128)S(1)}, f32[2,32,512]{2,1,0:T(8,128)S(1)}, u32[]{:S(2)}, u32[]{:S(2)}) %collective-permute-start.9) | collective-permute-done | bytes 131104 | tf_op jit(solution)/shard_map/ppermute | solution.py:457
  33.7 2.9 %shard_map.94 = (f32[4,32,512]{2,1,0:T(8,128)S(1)}, f32[32,3,128]{2,1,0:T(4,128)S(1)}) custom-call(f32[4,32,512]{2,1,0:T(8,128)S(1)} %get-tuple-element.59.part, f32[2,32,512]{2,1,0:T(8,128)S(1)} %collective-permute-done.8.got_a, f32[2,32,512]{2,1,0:T(8,128)S(1)} %collective-permute-done.9.got_b, f32[4,32,512]{2,1,0:T(8,128)} %copy-done.7, ...), custom_call_target="tpu_custom_call" | custom-call | bytes 4982272 | tf_op jit(solution)/shard_map/pallas_call | solution.py:32
  36.6 11.4 %all_to_all.5.msg = f32[32,3,128]{2,1,0:T(4,128)S(1)} all-to-all(f32[32,3,128]{2,1,0:T(4,128)S(1)} %get-tuple-element.63), channel_id=1, replica_groups=mesh['lon'=8,'lev'=4] {'lon','lev'}, dimensions={0} | all-to-all | bytes 98304 | tf_op jit(solution)/shard_map/all_to_all | solution.py:505
  48.0 1.9 %shard_map.95 = (f32[4,32,512]{2,1,0:T(8,128)S(1)}, f32[1,18]{1,0:T(1,128)S(1)}, f32[1,1]{1,0:T(1,128)}) custom-call(f32[32,3,128]{2,1,0:T(4,128)S(1)} %all_to_all.5.msg, f32[4,32,512]{2,1,0:T(8,128)S(1)} %get-tuple-element.64.applied, f32[4,32,512]{2,1,0:T(8,128)S(1)} %copy-done.8, f32[16,4,32,512]{3,2,1,0:T(8,128)S(1)} %copy-done.5), custom_call_target="tpu_custom_call" | custom-call | bytes 4767744 | tf_op jit(solution)/shard_map/pallas_call | solution.py:32
  50.6 0.0 copy-start.10
  50.6 0.7 %copy-done.10 = f32[4,32,512]{2,1,0:T(8,128)} copy-done((f32[4,32,512]{2,1,0:T(8,128)}, f32[4,32,512]{2,1,0:T(8,128)S(1)}, u32[]{:S(2)}) %copy-start.10) | copy-done | bytes 262168
  51.3 0.5 copy-done.11
  (21 shorter events, 0.1 us)
Async XLA Ops:
  0.6 1.0 %copy-start.1 = (f32[4,32,512]{2,1,0:T(8,128)S(1)}, f32[4,32,512]{2,1,0:T(8,128)}, u32[]{:S(2)}) copy-start(f32[4,32,512]{2,1,0:T(8,128)} %v_hbm.1) | copy-start | bytes 786436
  0.6 1.0 %copy-start.9 = (f32[4,32,512]{2,1,0:T(8,128)S(1)}, f32[4,32,512]{2,1,0:T(8,128)}, u32[]{:S(2)}) copy-start(f32[4,32,512]{2,1,0:T(8,128)} %param.10) | copy-start | bytes 786436
  0.7 12.7 %copy-start.6 = (f32[16,4,32,512]{3,2,1,0:T(8,128)S(1)}, f32[16,4,32,512]{3,2,1,0:T(8,128)}, u32[]{:S(2)}) copy-start(f32[16,4,32,512]{3,2,1,0:T(8,128)} %param.12) | copy-start | bytes 12582916
  0.7 1.6 %copy-start = (f32[2,3,4,32,512]{4,3,2,1,0:T(8,128)S(1)}, f32[2,3,4,32,512]{4,3,2,1,0:T(8,128)}, u32[]{:S(2)}) copy-start(f32[2,3,4,32,512]{4,3,2,1,0:T(8,128)} %vel_hbm.1) | copy-start | bytes 4718596
  0.7 1.6 %copy-start.2 = (s32[32,512]{1,0:T(8,128)S(1)}, s32[32,512]{1,0:T(8,128)}, u32[]{:S(2)}) copy-start(s32[32,512]{1,0:T(8,128)} %owner_hbm.1) | copy-start | bytes 196612
  1.6 22.5 %copy-start.3 = (f32[4]{0:T(128)S(1)}, f32[4]{0:T(128)}, u32[]{:S(2)}) copy-start(f32[4]{0:T(128)} %lw.1) | copy-start | bytes 52
  3.7 16.0 %copy-start.7 = (f32[4,32,512]{2,1,0:T(8,128)}, f32[4,32,512]{2,1,0:T(8,128)S(1)}, u32[]{:S(2)}) copy-start(f32[4,32,512]{2,1,0:T(8,128)S(1)} %get-tuple-element.43.v) | copy-start | bytes 786436
  3.7 20.4 %collective-permute-start.3 = (f32[5,32,512]{2,1,0:T(8,128)}, f32[5,32,512]{2,1,0:T(8,128)S(1)}, u32[]{:S(2)}, u32[]{:S(2)}) collective-permute-start(f32[5,32,512]{2,1,0:T(8,128)} %get-tuple-element.54), channel_id=1, source_target_pairs={{0,1},{1,0},{2,3},{3,2},{4,5},{5,4},{6,7},{7,6},{8,9},{9,8},{10,11... | collective-permute-start | bytes 983048 | tf_op jit(solution)/shard_map/ppermute | solution.py:457
  4.2 19.9 %collective-permute-start.4 = (f32[5,32,512]{2,1,0:T(8,128)}, f32[5,32,512]{2,1,0:T(8,128)S(1)}, u32[]{:S(2)}, u32[]{:S(2)}) collective-permute-start(f32[5,32,512]{2,1,0:T(8,128)} %get-tuple-element.55), channel_id=1, source_target_pairs={{0,3},{1,2},{2,1},{3,0},{4,7},{5,6},{6,5},{7,4},{8,11},{9,10},{10,... | collective-permute-start | bytes 983048 | tf_op jit(solution)/shard_map/ppermute | solution.py:457
  6.8 10.2 %collective-permute-start = (f32[80,512]{1,0:T(8,128)S(1)}, f32[80,512]{1,0:T(8,128)S(1)}, u32[]{:S(2)}, u32[]{:S(2)}) collective-permute-start(f32[80,512]{1,0:T(8,128)S(1)} %get-tuple-element.48), channel_id=1, source_target_pairs={{0,4},{4,8},{8,12},{12,16},{16,20},{20,24},{24,28},{28,0},{1,5},{5... | collective-permute-start | bytes 491528 | tf_op jit(solution)/shard_map/ppermute | solution.py:459
  8.3 9.4 %collective-permute-start.1 = (f32[80,512]{1,0:T(8,128)S(1)}, f32[80,512]{1,0:T(8,128)S(1)}, u32[]{:S(2)}, u32[]{:S(2)}) collective-permute-start(f32[80,512]{1,0:T(8,128)S(1)} %get-tuple-element.49), channel_id=1, source_target_pairs={{4,0},{8,4},{12,8},{16,12},{20,16},{24,20},{28,24},{0,28},{5,1},{9... | collective-permute-start | bytes 491528 | tf_op jit(solution)/shard_map/ppermute | solution.py:459
  11.5 5.4 %collective-permute-start.2 = (f32[1,128]{1,0:T(1,128)S(1)}, f32[1,128]{1,0:T(1,128)S(1)}, u32[]{:S(2)}, u32[]{:S(2)}) collective-permute-start(f32[1,128]{1,0:T(1,128)S(1)} %get-tuple-element.44.order.counts), channel_id=1, source_target_pairs={{8,0},{12,4},{16,8},{20,12},{24,16},{28,20},{0,24},{4,28},{9,1},{1... | collective-permute-start | bytes 1544 | tf_op jit(solution)/shard_map/ppermute | solution.py:461
  17.0 2.7 %copy-start.4 = (f32[16,4,32,512]{3,2,1,0:T(8,128)}, f32[16,4,32,512]{3,2,1,0:T(8,128)S(1)}, u32[]{:S(2)}) copy-start(f32[16,4,32,512]{3,2,1,0:T(8,128)S(1)} %get-tuple-element.62.s) | copy-start | bytes 12582916
  19.0 5.1 %collective-permute-start.5 = (f32[5,8,512]{2,1,0:T(8,128)}, f32[5,8,512]{2,1,0:T(8,128)S(1)}, u32[]{:S(2)}, u32[]{:S(2)}) collective-permute-start(f32[5,8,512]{2,1,0:T(8,128)} %get-tuple-element.56), channel_id=1, source_target_pairs={{0,1},{1,0},{2,3},{3,2},{4,5},{5,4},{6,7},{7,6},{8,9},{9,8},{10,11... | collective-permute-start | bytes 245768 | tf_op jit(solution)/shard_map/ppermute | solution.py:457
  19.0 5.1 %collective-permute-start.6 = (f32[5,8,512]{2,1,0:T(8,128)}, f32[5,8,512]{2,1,0:T(8,128)S(1)}, u32[]{:S(2)}, u32[]{:S(2)}) collective-permute-start(f32[5,8,512]{2,1,0:T(8,128)} %get-tuple-element.57), channel_id=1, source_target_pairs={{0,3},{1,2},{2,1},{3,0},{4,7},{5,6},{6,5},{7,4},{8,11},{9,10},{10,... | collective-permute-start | bytes 245768 | tf_op jit(solution)/shard_map/ppermute | solution.py:457
  19.6 4.4 %collective-permute-start.7 = (f32[1,128]{1,0:T(1,128)S(1)}, f32[1,128]{1,0:T(1,128)S(1)}, u32[]{:S(2)}, u32[]{:S(2)}) collective-permute-start(f32[1,128]{1,0:T(1,128)S(1)} %get-tuple-element.58.refs_0_), channel_id=1, source_target_pairs={{0,16},{4,20},{8,24},{12,28},{16,0},{20,4},{24,8},{28,12},{1,17},{... | collective-permute-start | bytes 1544 | tf_op jit(solution)/shard_map/ppermute | solution.py:478
  24.1 23.9 %copy-start.5 = (f32[16,4,32,512]{3,2,1,0:T(8,128)S(1)}, f32[16,4,32,512]{3,2,1,0:T(8,128)}, u32[]{:S(2)}) copy-start(f32[16,4,32,512]{3,2,1,0:T(8,128)} %copy-done.4) | copy-start | bytes 12582916
  24.1 23.9 %copy-start.8 = (f32[4,32,512]{2,1,0:T(8,128)S(1)}, f32[4,32,512]{2,1,0:T(8,128)}, u32[]{:S(2)}) copy-start(f32[4,32,512]{2,1,0:T(8,128)} %copy-done.7) | copy-start | bytes 786436
  28.3 1.7 %collective-permute-start.8 = (f32[2,32,512]{2,1,0:T(8,128)S(1)}, f32[2,32,512]{2,1,0:T(8,128)S(1)}, u32[]{:S(2)}, u32[]{:S(2)}) collective-permute-start(f32[2,32,512]{2,1,0:T(8,128)S(1)} %get-tuple-element.60), channel_id=1, source_target_pairs={{0,1},{1,0},{2,3},{3,2},{4,5},{5,4},{6,7},{7,6},{8,9},{9,8},{10,11... | collective-permute-start | bytes 393224 | tf_op jit(solution)/shard_map/ppermute | solution.py:457
  28.4 5.3 %collective-permute-start.9 = (f32[2,32,512]{2,1,0:T(8,128)S(1)}, f32[2,32,512]{2,1,0:T(8,128)S(1)}, u32[]{:S(2)}, u32[]{:S(2)}) collective-permute-start(f32[2,32,512]{2,1,0:T(8,128)S(1)} %get-tuple-element.61), channel_id=1, source_target_pairs={{0,3},{1,2},{2,1},{3,0},{4,7},{5,6},{6,5},{7,4},{8,11},{9,10},{10,... | collective-permute-start | bytes 393224 | tf_op jit(solution)/shard_map/ppermute | solution.py:457
  50.6 0.7 %copy-start.10 = (f32[4,32,512]{2,1,0:T(8,128)}, f32[4,32,512]{2,1,0:T(8,128)S(1)}, u32[]{:S(2)}) copy-start(f32[4,32,512]{2,1,0:T(8,128)S(1)} %get-tuple-element.97) | copy-start | bytes 786436
  51.3 0.5 copy-start.11

commit v3 on v2

--- a/solution.py
+++ b/solution.py
@@ -14,7 +14,7 @@
 
 VM = pl.BlockSpec(memory_space=pltpu.VMEM)
 SM = pl.BlockSpec(memory_space=pltpu.SMEM)
-ANY = pl.BlockSpec(memory_space=pl.ANY)
+HBM = pl.BlockSpec(memory_space=pltpu.HBM)
 CHUNK = 8
 WIDE = 4
 SECOND = 2
@@ -36,7 +36,7 @@
         out_specs=out_specs or jax.tree.map(lambda _: VM, outs),
         scratch_shapes=list(scratch),
         input_output_aliases=alias or {},
-        compiler_params=pltpu.CompilerParams(vmem_limit_bytes=40 << 20),
+        compiler_params=pltpu.CompilerParams(vmem_limit_bytes=16 << 20),
         cost_estimate=pl.CostEstimate(flops=flops, bytes_accessed=nbytes, transcendentals=0),
     )(*operands)
 
@@ -49,31 +49,19 @@
     return lax.rem(lax.axis_index("lev"), 2) == 0
 
 
-def pack_kernel(
-    levels, cols, v_hbm, vel_hbm, owner_hbm, lo, hi, lev_a, lev_b, counts, v, vel, owner, sems
-):
-    copies = [pltpu.make_async_copy(v_hbm, v, sems.at[0]), pltpu.make_async_copy(owner_hbm, owner, sems.at[1])]
-    for section in range(2):
-        for comp in range(3):
-            sem = sems.at[2 + 3 * section + comp]
-            copies.append(pltpu.make_async_copy(vel_hbm.at[section, comp], vel.at[section, comp], sem))
-    for copy in copies:
-        copy.start()
-
+def pack_kernel(levels, cols, v, vel, owner, lo, hi, lev_a, lev_b, counts, v_out, vel_out, owner_out):
     def edge(low, n):
         return slice(0, n) if low else slice(cols - n, cols)
 
     sides = ((lo, True), (hi, False))
     even = even_level()
     tops = ((lev_a, even), (lev_b, jnp.logical_not(even)))
-    copies[0].wait()
     for msg, low in sides:
         for lev in range(levels):
             msg[lev * LEVEL_ROWS : lev * LEVEL_ROWS + V_ROWS] = v[lev, edge(low, V_ROWS)]
     for msg, top in tops:
         msg[0] = v[jnp.where(top, levels - 1, 0)]
         msg[1] = v[jnp.where(top, levels - 2, 1)]
-    copies[1].wait()
     lanes = lane_iota((1, 128))
     row = jnp.zeros((1, 128), f32)
     held = owner[...]
@@ -87,7 +75,6 @@
         msg[at + B_ROWS : at + B_ROWS + 1, 0:128] = row
     for section, n, start in ((0, A_ROWS, V_ROWS), (1, B_ROWS, B_AT)):
         for comp in range(3):
-            copies[2 + 3 * section + comp].wait()
             for msg, low in sides:
                 for lev in range(levels):
                     at = lev * LEVEL_ROWS + start + comp * n
@@ -124,94 +111,119 @@
     window[...] = counts[...] + counts_2[...] + west[at : at + 1, 0:128] + east[at : at + 1, 0:128]
 
 
-def stencil_kernel(
-    levels, cols, lat, columns, n_counts,
-    lw, beta_prev, v, prev, vel, owner, west, east, halo_v, halo_a, halo_b,
-    lev_a, lev_b, corner_a, corner_b, *refs,
-):
-    count_refs = refs[:n_counts]
-    applied, send_a, send_b = refs[n_counts : n_counts + 3]
-    (vv, la, ff, own_h, w_in, w_e, w_w, w_u, w_d, u_in, u_e, u_w, u_u, u_d, out) = refs[n_counts + 3 :]
-    chunks = cols // CHUNK
-    level = lax.axis_index("lev")
-    last = lax.axis_size("lev") - 1
-    even = even_level()
-    has = (level > 0, level < last)
-    lanes = lane_iota((CHUNK, lat))
-    first_lane, last_lane = lanes == 0, lanes == lat - 1
-
-    def rows(k, shift=0):
-        return slice(CHUNK * (k + 1) + shift, CHUNK * (k + 2) + shift)
-
-    def put_west(ref, at, k, value):
+class Block:
+    def __init__(self, levels, cols, lat):
+        self.levels, self.lat, self.chunks = levels, lat, cols // CHUNK
+        level = lax.axis_index("lev")
+        self.has = (level > 0, level < lax.axis_size("lev") - 1)
+        self.even = even_level()
+        lanes = lane_iota((CHUNK, lat))
+        self.first_lane, self.last_lane = lanes == 0, lanes == lat - 1
+
+    def put_west(self, ref, at, k, value):
         ref[at, rows(k)] = value
-        if k == chunks:
+        if k == self.chunks:
             ref[at, 0:CHUNK] = value
 
-    def put_east(ref, at, k, value):
+    def put_east(self, ref, at, k, value):
         ref[at, rows(k)] = value
         if k == 0:
-            ref[at, rows(chunks + 1)] = value
-
-    def put_both(ref, at, k, value):
-        put_west(ref, at, k, value)
+            ref[at, rows(self.chunks + 1)] = value
+
+    def put_both(self, ref, at, k, value):
+        self.put_west(ref, at, k, value)
         if k == 0:
-            ref[at, rows(chunks + 1)] = value
-
-    def from_south(x):
-        return jnp.where(first_lane, 0.0, pltpu.roll(x, 1, 1))
-
-    def from_north(x):
-        return jnp.where(last_lane, 0.0, pltpu.roll(x, lat - 1, 1))
-
-    for k in range(chunks + 1):
-        cells = slice(CHUNK * k, CHUNK * (k + 1))
-        got_a, got_b = (lev_a, lev_b) if k < chunks else (corner_a, corner_b)
-        src = cells if k < chunks else slice(0, CHUNK)
+            ref[at, rows(self.chunks + 1)] = value
+
+    def from_south(self, x):
+        return jnp.where(self.first_lane, 0.0, pltpu.roll(x, 1, 1))
+
+    def from_north(self, x):
+        return jnp.where(self.last_lane, 0.0, pltpu.roll(x, self.lat - 1, 1))
+
+    def beyond(self, got_a, got_b, src, k, vv, la):
         for item in range(5):
             a, b = got_a[item, src], got_b[item, src]
-            below, above = jnp.where(even, b, a), jnp.where(even, a, b)
+            below, above = jnp.where(self.even, b, a), jnp.where(self.even, a, b)
             if item < 2:
-                put_both(vv, 1 - item, k, jnp.where(has[0], below, 0.0))
-                put_both(vv, levels + 2 + item, k, jnp.where(has[1], above, 0.0))
+                self.put_both(vv, 1 - item, k, jnp.where(self.has[0], below, 0.0))
+                self.put_both(vv, self.levels + 2 + item, k, jnp.where(self.has[1], above, 0.0))
             else:
-                la[0, item - 2, cells] = below
-                la[1, item - 2, cells] = above
-        for lev in range(levels):
-            put_both(vv, lev + 2, k, v[lev, cells] if k < chunks else halo_v[lev])
-    own_h[...] = jnp.zeros(own_h.shape, f32)
-    at = levels * LEVEL_ROWS
-    own_h[0:B_ROWS] = east[at : at + B_ROWS]
-    own_h[CHUNK - B_ROWS : CHUNK] = west[at : at + B_ROWS]
-
-    def flow(section, k, lev):
-        if k < chunks:
-            return [vel[section, comp, lev, CHUNK * k : CHUNK * (k + 1)] for comp in range(3)]
-        return [(halo_b if section else halo_a)[comp, lev] for comp in range(3)]
-
-    def flow_beyond(side, k):
-        return [la[side, comp, CHUNK * k : CHUNK * (k + 1)] for comp in range(3)]
-
-    def tangent(ref, at, k, abc):
+                la[0, item - 2, tile(k)] = below
+                la[1, item - 2, tile(k)] = above
+
+    def tangent(self, ref, at, k, abc):
         here = ref[at, rows(k)]
         e, w = ref[at, rows(k, 1)], ref[at, rows(k, -1)]
-        n, s = from_north(here), from_south(here)
+        n, s = self.from_north(here), self.from_south(here)
         u, d = ref[at + 1, rows(k)], ref[at - 1, rows(k)]
         a, b, c = abc
         around = ((e + w) + (n + s)) + (u + d)
         drift = a * (w - e) + b * (s - n) + c * (d - u)
         return centre * here + kappa * around + 0.5 * drift
 
-    def push(x, abc, dst, at, k):
+    def push(self, x, abc, dst, at, k):
         inside, to_e, to_w, to_u, to_d = dst
         a, b, c = abc
         base, half = kappa * x, 0.5 * x
         a, b, c = a * half, b * half, c * half
-        inside[at, rows(k)] = centre * x + (from_south(base - b) + from_north(base + b))
-        put_west(to_e, at, k, base - a)
-        put_east(to_w, at, k, base + a)
+        inside[at, rows(k)] = centre * x + (self.from_south(base - b) + self.from_north(base + b))
+        self.put_west(to_e, at, k, base - a)
+        self.put_east(to_w, at, k, base + a)
         to_u[at, rows(k)] = base - c
         to_d[at, rows(k)] = base + c
+
+
+def rows(k, shift=0):
+    return slice(CHUNK * (k + 1) + shift, CHUNK * (k + 2) + shift)
+
+
+def tile(k):
+    return slice(CHUNK * k, CHUNK * (k + 1))
+
+
+def first_kernel(levels, cols, lat, v, vel, halo_v, lev_a, lev_b, vv, la, ff):
+    block = Block(levels, cols, lat)
+    for k in range(block.chunks):
+        block.beyond(lev_a, lev_b, tile(k), k, vv, la)
+    for k in range(block.chunks + 1):
+        for lev in range(levels):
+            block.put_both(vv, lev + 2, k, v[lev, tile(k)] if k < block.chunks else halo_v[lev])
+
+    def first_level(lev, carry):
+        for k in range(block.chunks):
+            abc = [vel[0, comp, lev, tile(k)] for comp in range(3)]
+            block.put_both(ff, lev + 1, k, block.tangent(vv, lev + 2, k, abc))
+        return carry
+
+    lax.fori_loop(0, levels, first_level, 0)
+
+
+def stencil_kernel(
+    levels, cols, lat, columns, n_counts,
+    lw, beta_prev, prev, vel, owner, west, east, halo_a, halo_b,
+    vv_in, la_in, ff_in, corner_a, corner_b, *refs,
+):
+    count_refs = refs[:n_counts]
+    applied, send_a, send_b, vv, la, ff = refs[n_counts : n_counts + 6]
+    (own_h, w_in, w_e, w_w, w_u, w_d, u_in, u_e, u_w, u_u, u_d, out) = refs[n_counts + 6 :]
+    block = Block(levels, cols, lat)
+    chunks, has, even = block.chunks, block.has, block.even
+    tangent, push, put_both = block.tangent, block.push, block.put_both
+
+    block.beyond(corner_a, corner_b, slice(0, CHUNK), chunks, vv, la)
+    own_h[...] = jnp.zeros(own_h.shape, f32)
+    at = levels * LEVEL_ROWS
+    own_h[0:B_ROWS] = east[at : at + B_ROWS]
+    own_h[CHUNK - B_ROWS : CHUNK] = west[at : at + B_ROWS]
+
+    def flow(section, k, lev):
+        if k < chunks:
+            return [vel[section, comp, lev, tile(k)] for comp in range(3)]
+        return [(halo_b if section else halo_a)[comp, lev] for comp in range(3)]
+
+    def flow_beyond(side, k):
+        return [la[side, comp, tile(k)] for comp in range(3)]
 
     for k in range(chunks + 1):
         for side, at in ((0, 0), (1, levels + 1)):
@@ -219,8 +231,7 @@
             put_both(ff, at, k, jnp.where(has[side], value, 0.0))
 
     def first_level(lev, carry):
-        for k in range(chunks + 1):
-            put_both(ff, lev + 1, k, tangent(vv, lev + 2, k, flow(0, k, lev)))
+        put_both(ff, lev + 1, chunks, tangent(vv, lev + 2, chunks, flow(0, chunks, lev)))
         return carry
 
     lax.fori_loop(0, levels, first_level, 0)
@@ -378,7 +389,7 @@
     msg[:, r : r + 1] = jnp.broadcast_to(row[None], (count, 1, 128))
 
 
-def finish_kernel(nvec, levels, cols, lat, cells_all, msg, applied, v, s, result_out, coefs_out, trust, result, coefs, sems):
+def scalar_kernel(nvec, cells_all, msg, out, trust):
     total = jnp.sum(msg[...], axis=0) * (1.0 / cells_all)
     r = total.shape[0] - 1
     row = total[r : r + 1]
@@ -406,15 +417,19 @@
     size = aa + alpha * alpha * (2.0 + vv) + 2.0 * pp + jnp.abs(quad)
     trust[...] = jnp.where((square > 0.03125 * size) & (size < 1e36), 1.0, 0.0)
     beta = jnp.sqrt(square + 1e-12)
-    inverse = 1.0 / beta
-    line = jnp.where(lanes == 0, alpha, jnp.where(lanes == 1, beta, pltpu.roll(pv, 2, 1)))
+    out[...] = jnp.where(lanes == 0, alpha, jnp.where(lanes == 1, beta, pltpu.roll(pv, 2, 1)))
+
+
+def finish_kernel(nvec, levels, cols, lat, row, applied, v, s, result_out, coefs_out, result, coefs, sems):
+    line = row[...]
     coefs[...] = line[:, 0 : nvec + 2]
+    inverse = 1.0 / line[:, 1:2]
+    a_w = jnp.broadcast_to(line[:, 0:1] * inverse, (CHUNK, 128))
+    scale = jnp.broadcast_to(inverse, (CHUNK, 128))
+    weights = [jnp.broadcast_to(line[:, 2 + k : 3 + k] * inverse, (CHUNK, 128)) for k in range(nvec)]
     copies = [pltpu.make_async_copy(result.at[lev], result_out.at[lev], sems.at[lev]) for lev in range(levels)]
     copies.append(pltpu.make_async_copy(coefs, coefs_out, sems.at[levels]))
     copies[-1].start()
-    weights = [jnp.broadcast_to(x * inverse, (CHUNK, 128)) for x in p]
-    a_w = jnp.broadcast_to(alpha * inverse, (CHUNK, 128))
-    scale = jnp.broadcast_to(inverse, (CHUNK, 128))
 
     for lev in range(levels):
 
@@ -446,7 +461,7 @@
         functools.partial(pack_kernel, levels, cols),
         (sds(lines, lat), sds(lines, lat), sds(5, cols, lat), sds(5, cols, lat), sds(1, 128),
          sds(*v.shape), sds(*vel.shape), jax.ShapeDtypeStruct(owner.shape, owner.dtype)),
-        (v, vel, owner), specs=[ANY] * 3, scratch=[pltpu.SemaphoreType.DMA((8,))], flops=1 << 20,
+        (v, vel, owner), flops=1 << 20, alias={0: 5, 1: 6, 2: 7},
     )
     east_of = [(i, (i + 1) % lon_n) for i in range(lon_n)]
     west_of = [((i + 1) % lon_n, i) for i in range(lon_n)]
@@ -473,28 +488,28 @@
          sds(5, CHUNK, lat), sds(5, CHUNK, lat), sds(1, 128)),
         (west, east, counts, counts_2, gram),
     )
-    corner_a, corner_b = both(corner_a, corner_b)
     if lon_n == 8:
         near = [window, lax.ppermute(window, "lon", [(i, i ^ 4) for i in range(lon_n)])]
     else:
         near = [lax.psum(counts, "lon")]
+    corner_a, corner_b = both(corner_a, corner_b)
 
     padded = cols + 3 * CHUNK
-    scratch = [
-        pltpu.VMEM((levels + 4, padded, lat), f32),
-        pltpu.VMEM((2, 3, cols + CHUNK, lat), f32),
-        pltpu.VMEM((levels + 2, padded, lat), f32),
-        pltpu.VMEM((CHUNK, lat), f32),
-    ]
+    state = (sds(levels + 4, padded, lat), sds(2, 3, cols + CHUNK, lat), sds(levels + 2, padded, lat))
+    state = call(
+        functools.partial(first_kernel, levels, cols, lat), state, (v, vel, halo_v, lev_a, lev_b), flops=4 << 20
+    )
+    scratch = [pltpu.VMEM((CHUNK, lat), f32)]
     scratch += [pltpu.VMEM((levels + 2, padded, lat), f32)] * 10
     scratch += [pltpu.VMEM((levels + 4, cols + CHUNK, lat), f32)]
-    operands = (lw, beta_prev.reshape(1), v, prev, vel, owner, west, east, halo_v, halo_a, halo_b,
-                lev_a, lev_b, corner_a, corner_b, *near)
+    operands = (lw, beta_prev.reshape(1), prev, vel, owner, west, east, halo_a, halo_b, *state,
+                corner_a, corner_b, *near)
     part, send_a, send_b = call(
         functools.partial(stencil_kernel, levels, cols, lat, float(cols * lon_n * lat), len(near)),
-        (sds(levels, cols, lat), sds(SECOND, cols, lat), sds(SECOND, cols, lat)),
+        (sds(levels, cols, lat), sds(SECOND, cols, lat), sds(SECOND, cols, lat), *(sds(*x.shape) for x in state)),
         operands, specs=[SM, SM] + [VM] * (len(operands) - 2), scratch=scratch, flops=8 << 20,
-    )
+        alias={9: 3, 10: 4, 11: 5},
+    )[:3]
     got_a, got_b = both(send_a, send_b)
     applied, msg = call(
         functools.partial(gather_kernel, nvec, levels, cols, lat, count),
@@ -504,25 +519,23 @@
     )
     msg = lax.all_to_all(msg, ("lon", "lev"), 0, 0, tiled=True)
     cells = float(v.size * count)
-    result, coefs, trust = call(
-        functools.partial(finish_kernel, nvec, levels, cols, lat, cells),
-        (sds(levels, cols, lat), sds(1, nvec + 2), sds(1, 1)),
-        (msg, applied, v, s), out_specs=(ANY, ANY, VM),
+    row, trust = call(functools.partial(scalar_kernel, nvec, cells), (sds(1, 128), sds(1, 1)), (msg,))
+
+    def direct():
+        weights = row[0, 2 : nvec + 2]
+        orthogonal = applied - row[0, 0] * v - jnp.sum(weights[:, None, None, None] * s, axis=0)
+        square = lax.psum(jnp.sum(orthogonal * orthogonal), ("lon", "lev")) / cells
+        return row.at[0, 1].set(jnp.sqrt(square + 1e-12))
+
+    row = lax.cond(trust[0, 0] > 0.5, lambda: row, direct)
+    result, coefs = call(
+        functools.partial(finish_kernel, nvec, levels, cols, lat),
+        (sds(levels, cols, lat), sds(1, nvec + 2)),
+        (row, applied, v, s), out_specs=(HBM, HBM),
         scratch=[pltpu.VMEM((levels, cols, lat), f32), pltpu.VMEM((1, nvec + 2), f32),
                  pltpu.SemaphoreType.DMA((levels + 1,))],
     )
-    coefs = coefs.reshape(nvec + 2)
-
-    def keep():
-        return result, coefs
-
-    def direct():
-        orthogonal = applied - coefs[0] * v - jnp.sum(coefs[2:, None, None, None] * s, axis=0)
-        square = lax.psum(jnp.sum(orthogonal * orthogonal), ("lon", "lev")) / cells
-        beta = jnp.sqrt(square + 1e-12)
-        return orthogonal / beta, jnp.concatenate([coefs[:1], beta[None], coefs[2:]])
-
-    return lax.cond(trust[0, 0] > 0.5, keep, direct)
+    return result, coefs.reshape(nvec + 2)
 
 
 def solution(mesh):

time: 52 us -> 53 us (1.019)
  local copies, waits for them, and re-layouts: 2.78 us -> 4.18 us
  waiting for transfers between devices: 6.43 us -> 5.46 us
    unnamed x25 -> x19, local copies, waits for them, and re-layouts: 2.78 us -> 4.18 us
    ppermute x1, waiting for transfers between devices: 1.99 us -> 1.02 us  [body(): lax.ppermute(window, 'lon', [(i, i ^ 4) for i in range(lon_n)])]
    pallas_call x6 -> x8, Pallas kernels: 15.3 us -> 15.7 us  [call(): pl.pallas_call(kernel, out_shape=outs, in_specs=specs or [VM] * len(opera...]
  transfers between devices with their start and end apart: 10 -> 10, of which waited for: 3 -> 3; matrix products, arithmetic and copies ran while one was open for 0% -> 0% of each run, Pallas kernels for 9% -> 12%
where the time goes in v3:
time: 53 us; the launch traced here: 52.7 us
  Pallas kernels  15.7 us (30%)
  starting transfers between devices  13.8 us (26%)
  blocking collectives  11.4 us (22%)
  waiting for transfers between devices  5.46 us (10%)
  local copies, waits for them, and re-layouts  4.18 us (8%)
  between operations  2.05 us (4%)
    pallas_call x8, Pallas kernels, call(): pl.pallas_call(kernel, out_shape=outs, in_specs=specs or [VM] * len(opera...  15.7 us
    all_to_all x1, blocking collectives, body(): msg = lax.all_to_all(msg, ('lon', 'lev'), 0, 0, tiled=True)  11.4 us
    ppermute x6, starting transfers between devices, both(): return (lax.ppermute(a, 'lev', pairs_a), lax.ppermute(b, 'lev', pairs_b))  5.38 us
    unnamed x19, local copies, waits for them, and re-layouts  4.18 us
    ppermute x6, waiting for transfers between devices, both(): return (lax.ppermute(a, 'lev', pairs_a), lax.ppermute(b, 'lev', pairs_b))  3.69 us
    ppermute x1, starting transfers between devices, body(): lax.ppermute(lo, 'lon', west_of)  3.2 us
    ppermute x1, starting transfers between devices, body(): lax.ppermute(window, 'lon', [(i, i ^ 4) for i in range(lon_n)])  1.89 us
    ppermute x1, starting transfers between devices, body(): lax.ppermute(counts, 'lon', [((i + 2) % lon_n, i) for i in range(lon_n)])  1.8 us
  transfers between devices with their start and end apart: 10, of which 3 were waited for; matrix products, arithmetic and copies ran while one was open for 0% of the time, Pallas kernels for 12%

profile of v3, /device:TPU:0, one launch (start us, length us, event | category | flops | bytes accessed | tf_op | source)
XLA Modules:
  0.0 52.7 jit_solution(9631853728654596997)
XLA Ops:
  0.6 0.8 %copy.38.owner = s32[32,512]{1,0:T(8,128)S(1)} copy(s32[32,512]{1,0:T(8,128)} %param.17) | data formatting | bytes 131072
  1.5 1.4 %copy.37.vel = f32[2,3,4,32,512]{4,3,2,1,0:T(8,128)S(1)} copy(f32[2,3,4,32,512]{4,3,2,1,0:T(8,128)} %param.15) | data formatting | bytes 3145728
  2.9 0.9 %copy.35.prev = f32[4,32,512]{2,1,0:T(8,128)S(1)} copy(f32[4,32,512]{2,1,0:T(8,128)} %param.12) | data formatting | bytes 524288
  3.8 0.9 %copy-done.7 = f32[4,32,512]{2,1,0:T(8,128)S(1)} copy-done((f32[4,32,512]{2,1,0:T(8,128)S(1)}, f32[4,32,512]{2,1,0:T(8,128)}, u32[]{:S(2)}) %copy-start.7) | copy-done | bytes 262168
  4.8 1.0 %shard_map.86 = (f32[80,512]{1,0:T(8,128)S(1)}, f32[80,512]{1,0:T(8,128)S(1)}, f32[5,32,512]{2,1,0:T(8,128)}, f32[5,32,512]{2,1,0:T(8,128)}, f32[1,128]{1,0:T(1,...) custom-call(f32[4,32,512]{2,1,0:T(8,128)S(1)} %copy-done.7, ...), custom_call_target="tpu_custom_call", output_to_operand_aliasing={{5}: (0, {}), {6}: (1, {}), {7}: (2, {})} | custom-call | flops 1048576 | bytes 1900544 | tf_op jit(solution)/shard_map/pallas_call | solution.py:32
  5.8 0.5 collective-permute-start.3
  6.3 2.6 %collective-permute-start.4 = (f32[5,32,512]{2,1,0:T(8,128)}, f32[5,32,512]{2,1,0:T(8,128)S(1)}, u32[]{:S(2)}, u32[]{:S(2)}) collective-permute-start(f32[5,32,512]{2,1,0:T(8,128)} %get-tuple-element.71), channel_id=1, source_target_pairs={{0,3},{1,2},{2,1},{3,0},{4,7},{5,6},{6,5},{7,4},{8,11},{9,10},{10,... | collective-permute-start | bytes 983048 | tf_op jit(solution)/shard_map/ppermute | solution.py:472
  8.9 1.5 %collective-permute-start = (f32[80,512]{1,0:T(8,128)S(1)}, f32[80,512]{1,0:T(8,128)S(1)}, u32[]{:S(2)}, u32[]{:S(2)}) collective-permute-start(f32[80,512]{1,0:T(8,128)S(1)} %get-tuple-element.64), channel_id=1, source_target_pairs={{0,4},{4,8},{8,12},{12,16},{16,20},{20,24},{24,28},{28,0},{1,5},{5... | collective-permute-start | bytes 491528 | tf_op jit(solution)/shard_map/ppermute | solution.py:474
  10.4 3.2 %collective-permute-start.1 = (f32[80,512]{1,0:T(8,128)S(1)}, f32[80,512]{1,0:T(8,128)S(1)}, u32[]{:S(2)}, u32[]{:S(2)}) collective-permute-start(f32[80,512]{1,0:T(8,128)S(1)} %get-tuple-element.65), channel_id=1, source_target_pairs={{4,0},{8,4},{12,8},{16,12},{20,16},{24,20},{28,24},{0,28},{5,1},{9... | collective-permute-start | bytes 491528 | tf_op jit(solution)/shard_map/ppermute | solution.py:474
  13.6 1.8 %collective-permute-start.2 = (f32[1,128]{1,0:T(1,128)S(1)}, f32[1,128]{1,0:T(1,128)S(1)}, u32[]{:S(2)}, u32[]{:S(2)}) collective-permute-start(f32[1,128]{1,0:T(1,128)S(1)} %get-tuple-element.60.order.counts), channel_id=1, source_target_pairs={{8,0},{12,4},{16,8},{20,12},{24,16},{28,20},{0,24},{4,28},{9,1},{1... | collective-permute-start | bytes 1544 | tf_op jit(solution)/shard_map/ppermute | solution.py:476
  15.4 3.6 %shard_map.87 = (f32[3,128]{1,0:T(4,128)S(1)}, f32[16,4,32,512]{3,2,1,0:T(8,128)S(1)}, f32[4,32,512]{2,1,0:T(8,128)S(1)}) custom-call(f32[16,4,32,512]{3,2,1,0:T(8,128)S(1)} %copy-done.3, f32[4,32,512]{2,1,0:T(8,128)S(1)} %get-tuple-element.59.v, f32[4,32,512]{2,1,0:T(8,128)S(1)} %copy.35.prev, ...), custom_call_target="tpu_custom_call", output_to_operand_aliasing={{1}: (0, {}), {2}: (2, {})} | custom-call | flops 20971520 | bytes 4719104 | tf_op jit(solution)/shard_map/pallas_call | solution.py:32
  19.0 0.0 collective-permute-done.2.counts_2
  19.0 0.0 collective-permute-done.west
  19.0 0.7 %collective-permute-done.1.east = f32[80,512]{1,0:T(8,128)S(1)} collective-permute-done((f32[80,512]{1,0:T(8,128)S(1)}, f32[80,512]{1,0:T(8,128)S(1)}, u32[]{:S(2)}, u32[]{:S(2)}) %collective-permute-start.1) | collective-permute-done | bytes 163872 | tf_op jit(solution)/shard_map/ppermute | solution.py:474
  19.8 1.2 %shard_map.88 = (f32[4,8,512]{2,1,0:T(8,128)S(1)}, f32[3,4,8,512]{3,2,1,0:T(8,128)S(1)}, f32[3,4,8,512]{3,2,1,0:T(8,128)S(1)}, f32[5,8,512]{2,1,0:T(8,128)}, f32[5,8,512]{2,1,0:T(8,128)}, /*index=5*/f32[1,128]{1,0:T(1,128)S(1)}) custom-call(f32[80,512]{1,0:T(8,128)S(1)} %collective-permute-done.west, f32[80,512]{1,0:T(8,128)S(1)} %collective-permute-done.1.east, ...), custom_call_target="tpu_custom_call" | custom-call | bytes 330240 | tf_op jit(solution)/shard_map/pallas_call | solution.py:32
  21.0 0.0 collective-permute-start.5
  21.0 0.6 %collective-permute-start.6 = (f32[5,8,512]{2,1,0:T(8,128)}, f32[5,8,512]{2,1,0:T(8,128)S(1)}, u32[]{:S(2)}, u32[]{:S(2)}) collective-permute-start(f32[5,8,512]{2,1,0:T(8,128)} %get-tuple-element.76), channel_id=1, source_target_pairs={{0,3},{1,2},{2,1},{3,0},{4,7},{5,6},{6,5},{7,4},{8,11},{9,10},{10,... | collective-permute-start | bytes 245768 | tf_op jit(solution)/shard_map/ppermute | solution.py:472
  22.3 0.0 copy-start.5
  22.3 1.9 %collective-permute-start.7 = (f32[1,128]{1,0:T(1,128)S(1)}, f32[1,128]{1,0:T(1,128)S(1)}, u32[]{:S(2)}, u32[]{:S(2)}) collective-permute-start(f32[1,128]{1,0:T(1,128)S(1)} %get-tuple-element.77.refs_0_), channel_id=1, source_target_pairs={{0,16},{4,20},{8,24},{12,28},{16,0},{20,4},{24,8},{28,12},{1,17},{... | collective-permute-start | bytes 1544 | tf_op jit(solution)/shard_map/ppermute | solution.py:492
  24.2 0.0 collective-permute-done.3.lev_a
  24.2 0.0 collective-permute-done.4.lev_b
  24.2 1.6 %shard_map.89 = (f32[8,56,512]{2,1,0:T(8,128)S(1)}, f32[2,3,40,512]{3,2,1,0:T(8,128)S(1)}, f32[6,56,512]{2,1,0:T(8,128)S(1)}) custom-call(f32[4,32,512]{2,1,0:T(8,128)} %copy-done.4, f32[2,3,4,32,512]{4,3,2,1,0:T(8,128)S(1)} %get-tuple-element.62.vel, f32[4,8,512]{2,1,0:T(8,128)S(1)} %get-tuple-element.69.halo_v, ...), custom_call_target="tpu_custom_call" | custom-call | flops 4194304 | bytes 2555904 | tf_op jit(solution)/shard_map/pallas_call | solution.py:32
  25.8 1.0 %collective-permute-done.7.refs_1_ = f32[1,128]{1,0:T(1,128)S(1)} collective-permute-done((f32[1,128]{1,0:T(1,128)S(1)}, f32[1,128]{1,0:T(1,128)S(1)}, u32[]{:S(2)}, u32[]{:S(2)}) %collective-permute-start.7) | collective-permute-done | bytes 544 | tf_op jit(solution)/shard_map/ppermute | solution.py:492
  26.9 3.3 %shard_map.90 = (f32[4,32,512]{2,1,0:T(8,128)S(1)}, f32[2,32,512]{2,1,0:T(8,128)S(1)}, f32[2,32,512]{2,1,0:T(8,128)S(1)}, f32[8,56,512]{2,1,0:T(8,128)S(1)}, f32...) custom-call(f32[4]{0:T(128)S(1)} %copy-done, ...), custom_call_target="tpu_custom_call", output_to_operand_aliasing={{3}: (9, {}), {4}: (10, {}), {5}: (11, {})} | custom-call | flops 8388608 | bytes 4883476 | tf_op jit(solution)/shard_map/pallas_call | solution.py:32
  30.1 0.1 collective-permute-start.8
  30.2 1.6 %collective-permute-start.9 = (f32[2,32,512]{2,1,0:T(8,128)S(1)}, f32[2,32,512]{2,1,0:T(8,128)S(1)}, u32[]{:S(2)}, u32[]{:S(2)}) collective-permute-start(f32[2,32,512]{2,1,0:T(8,128)S(1)} %get-tuple-element.80), channel_id=1, source_target_pairs={{0,3},{1,2},{2,1},{3,0},{4,7},{5,6},{6,5},{7,4},{8,11},{9,10},{10,... | collective-permute-start | bytes 393224 | tf_op jit(solution)/shard_map/ppermute | solution.py:472
  31.8 0.0 collective-permute-done.8.got_a
  31.8 3.7 %collective-permute-done.9.got_b = f32[2,32,512]{2,1,0:T(8,128)S(1)} collective-permute-done((f32[2,32,512]{2,1,0:T(8,128)S(1)}, f32[2,32,512]{2,1,0:T(8,128)S(1)}, u32[]{:S(2)}, u32[]{:S(2)}) %collective-permute-start.9) | collective-permute-done | bytes 131104 | tf_op jit(solution)/shard_map/ppermute | solution.py:472
  35.5 0.6 %shard_map.91 = (f32[4,32,512]{2,1,0:T(8,128)S(1)}, f32[32,3,128]{2,1,0:T(4,128)S(1)}) custom-call(f32[4,32,512]{2,1,0:T(8,128)S(1)} %get-tuple-element.78.part, f32[2,32,512]{2,1,0:T(8,128)S(1)} %collective-permute-done.8.got_a, f32[2,32,512]{2,1,0:T(8,128)S(1)} %collective-permute-done.9.got_b, f32[4,32,512]{2,1,0:T(8,128)S(1)} %copy-done.5, ...), custom_call_target="tpu_custom_call" | custom-call | bytes 4982272 | tf_op jit(solution)/shard_map/pallas_call | solution.py:32
  36.2 11.4 %all_to_all.5.msg = f32[32,3,128]{2,1,0:T(4,128)S(1)} all-to-all(f32[32,3,128]{2,1,0:T(4,128)S(1)} %get-tuple-element.82), channel_id=1, replica_groups=mesh['lon'=8,'lev'=4] {'lon','lev'}, dimensions={0} | all-to-all | bytes 98304 | tf_op jit(solution)/shard_map/all_to_all | solution.py:520
  47.6 0.9 %shard_map.92 = (f32[1,128]{1,0:T(1,128)S(1)}, f32[1,1]{1,0:T(1,128)}) custom-call(f32[32,3,128]{2,1,0:T(4,128)S(1)} %all_to_all.5.msg), custom_call_target="tpu_custom_call" | custom-call | bytes 49152 | tf_op jit(solution)/shard_map/pallas_call | solution.py:32
  49.1 3.5 %shard_map.93 = (f32[4,32,512]{2,1,0:T(8,128)}, f32[1,18]{1,0:T(1,128)}) custom-call(f32[1,128]{1,0:T(1,128)S(1)} %get-tuple-element.90.row, f32[4,32,512]{2,1,0:T(8,128)S(1)} %get-tuple-element.85.applied, f32[4,32,512]{2,1,0:T(8,128)S(1)} %copy-done.6, f32[16,4,32,512]{3,2,1,0:T(8,128)} %copy-done.1), custom_call_target="tpu_custom_call" | custom-call | bytes 4719104 | tf_op jit(solution)/shard_map/pallas_call | solution.py:32
  (17 shorter events, 0.0 us)
Async XLA Ops:
  3.8 0.9 %copy-start.7 = (f32[4,32,512]{2,1,0:T(8,128)S(1)}, f32[4,32,512]{2,1,0:T(8,128)}, u32[]{:S(2)}) copy-start(f32[4,32,512]{2,1,0:T(8,128)} %param.11) | copy-start | bytes 786436
  3.8 11.6 %copy-start.3 = (f32[16,4,32,512]{3,2,1,0:T(8,128)S(1)}, f32[16,4,32,512]{3,2,1,0:T(8,128)}, u32[]{:S(2)}) copy-start(f32[16,4,32,512]{3,2,1,0:T(8,128)} %param.14) | copy-start | bytes 12582916
  5.8 14.0 %copy-start.4 = (f32[4,32,512]{2,1,0:T(8,128)}, f32[4,32,512]{2,1,0:T(8,128)S(1)}, u32[]{:S(2)}) copy-start(f32[4,32,512]{2,1,0:T(8,128)S(1)} %get-tuple-element.59.v) | copy-start | bytes 786436
  5.8 21.1 %copy-start = (f32[4]{0:T(128)S(1)}, f32[4]{0:T(128)}, u32[]{:S(2)}) copy-start(f32[4]{0:T(128)} %lw.1) | copy-start | bytes 52
  5.8 18.4 %collective-permute-start.3 = (f32[5,32,512]{2,1,0:T(8,128)}, f32[5,32,512]{2,1,0:T(8,128)S(1)}, u32[]{:S(2)}, u32[]{:S(2)}) collective-permute-start(f32[5,32,512]{2,1,0:T(8,128)} %get-tuple-element.70), channel_id=1, source_target_pairs={{0,1},{1,0},{2,3},{3,2},{4,5},{5,4},{6,7},{7,6},{8,9},{9,8},{10,11... | collective-permute-start | bytes 983048 | tf_op jit(solution)/shard_map/ppermute | solution.py:472
  6.3 18.0 %collective-permute-start.4 = (f32[5,32,512]{2,1,0:T(8,128)}, f32[5,32,512]{2,1,0:T(8,128)S(1)}, u32[]{:S(2)}, u32[]{:S(2)}) collective-permute-start(f32[5,32,512]{2,1,0:T(8,128)} %get-tuple-element.71), channel_id=1, source_target_pairs={{0,3},{1,2},{2,1},{3,0},{4,7},{5,6},{6,5},{7,4},{8,11},{9,10},{10,... | collective-permute-start | bytes 983048 | tf_op jit(solution)/shard_map/ppermute | solution.py:472
  8.9 10.2 %collective-permute-start = (f32[80,512]{1,0:T(8,128)S(1)}, f32[80,512]{1,0:T(8,128)S(1)}, u32[]{:S(2)}, u32[]{:S(2)}) collective-permute-start(f32[80,512]{1,0:T(8,128)S(1)} %get-tuple-element.64), channel_id=1, source_target_pairs={{0,4},{4,8},{8,12},{12,16},{16,20},{20,24},{24,28},{28,0},{1,5},{5... | collective-permute-start | bytes 491528 | tf_op jit(solution)/shard_map/ppermute | solution.py:474
  10.4 9.4 %collective-permute-start.1 = (f32[80,512]{1,0:T(8,128)S(1)}, f32[80,512]{1,0:T(8,128)S(1)}, u32[]{:S(2)}, u32[]{:S(2)}) collective-permute-start(f32[80,512]{1,0:T(8,128)S(1)} %get-tuple-element.65), channel_id=1, source_target_pairs={{4,0},{8,4},{12,8},{16,12},{20,16},{24,20},{28,24},{0,28},{5,1},{9... | collective-permute-start | bytes 491528 | tf_op jit(solution)/shard_map/ppermute | solution.py:474
  13.6 5.4 %collective-permute-start.2 = (f32[1,128]{1,0:T(1,128)S(1)}, f32[1,128]{1,0:T(1,128)S(1)}, u32[]{:S(2)}, u32[]{:S(2)}) collective-permute-start(f32[1,128]{1,0:T(1,128)S(1)} %get-tuple-element.60.order.counts), channel_id=1, source_target_pairs={{8,0},{12,4},{16,8},{20,12},{24,16},{28,20},{0,24},{4,28},{9,1},{1... | collective-permute-start | bytes 1544 | tf_op jit(solution)/shard_map/ppermute | solution.py:476
  19.0 2.0 %copy-start.1 = (f32[16,4,32,512]{3,2,1,0:T(8,128)}, f32[16,4,32,512]{3,2,1,0:T(8,128)S(1)}, u32[]{:S(2)}) copy-start(f32[16,4,32,512]{3,2,1,0:T(8,128)S(1)} %get-tuple-element.81.s) | copy-start | bytes 12582916
  21.0 5.8 %collective-permute-start.5 = (f32[5,8,512]{2,1,0:T(8,128)}, f32[5,8,512]{2,1,0:T(8,128)S(1)}, u32[]{:S(2)}, u32[]{:S(2)}) collective-permute-start(f32[5,8,512]{2,1,0:T(8,128)} %get-tuple-element.75), channel_id=1, source_target_pairs={{0,1},{1,0},{2,3},{3,2},{4,5},{5,4},{6,7},{7,6},{8,9},{9,8},{10,11... | collective-permute-start | bytes 245768 | tf_op jit(solution)/shard_map/ppermute | solution.py:472
  21.0 5.8 %collective-permute-start.6 = (f32[5,8,512]{2,1,0:T(8,128)}, f32[5,8,512]{2,1,0:T(8,128)S(1)}, u32[]{:S(2)}, u32[]{:S(2)}) collective-permute-start(f32[5,8,512]{2,1,0:T(8,128)} %get-tuple-element.76), channel_id=1, source_target_pairs={{0,3},{1,2},{2,1},{3,0},{4,7},{5,6},{6,5},{7,4},{8,11},{9,10},{10,... | collective-permute-start | bytes 245768 | tf_op jit(solution)/shard_map/ppermute | solution.py:472
  22.3 13.2 %copy-start.2 = (f32[16,4,32,512]{3,2,1,0:T(8,128)S(1)}, f32[16,4,32,512]{3,2,1,0:T(8,128)}, u32[]{:S(2)}) copy-start(f32[16,4,32,512]{3,2,1,0:T(8,128)} %copy-done.1) | copy-start | bytes 12582916
  22.3 13.2 %copy-start.5 = (f32[4,32,512]{2,1,0:T(8,128)S(1)}, f32[4,32,512]{2,1,0:T(8,128)}, u32[]{:S(2)}) copy-start(f32[4,32,512]{2,1,0:T(8,128)} %copy-done.4) | copy-start | bytes 786436
  22.3 4.5 %collective-permute-start.7 = (f32[1,128]{1,0:T(1,128)S(1)}, f32[1,128]{1,0:T(1,128)S(1)}, u32[]{:S(2)}, u32[]{:S(2)}) collective-permute-start(f32[1,128]{1,0:T(1,128)S(1)} %get-tuple-element.77.refs_0_), channel_id=1, source_target_pairs={{0,16},{4,20},{8,24},{12,28},{16,0},{20,4},{24,8},{28,12},{1,17},{... | collective-permute-start | bytes 1544 | tf_op jit(solution)/shard_map/ppermute | solution.py:492
  30.1 1.7 %collective-permute-start.8 = (f32[2,32,512]{2,1,0:T(8,128)S(1)}, f32[2,32,512]{2,1,0:T(8,128)S(1)}, u32[]{:S(2)}, u32[]{:S(2)}) collective-permute-start(f32[2,32,512]{2,1,0:T(8,128)S(1)} %get-tuple-element.79), channel_id=1, source_target_pairs={{0,1},{1,0},{2,3},{3,2},{4,5},{5,4},{6,7},{7,6},{8,9},{9,8},{10,11... | collective-permute-start | bytes 393224 | tf_op jit(solution)/shard_map/ppermute | solution.py:472
  30.2 5.3 %collective-permute-start.9 = (f32[2,32,512]{2,1,0:T(8,128)S(1)}, f32[2,32,512]{2,1,0:T(8,128)S(1)}, u32[]{:S(2)}, u32[]{:S(2)}) collective-permute-start(f32[2,32,512]{2,1,0:T(8,128)S(1)} %get-tuple-element.80), channel_id=1, source_target_pairs={{0,3},{1,2},{2,1},{3,0},{4,7},{5,6},{6,5},{7,4},{8,11},{9,10},{10,... | collective-permute-start | bytes 393224 | tf_op jit(solution)/shard_map/ppermute | solution.py:472
  35.5 13.6 %copy-start.6 = (f32[4,32,512]{2,1,0:T(8,128)S(1)}, f32[4,32,512]{2,1,0:T(8,128)}, u32[]{:S(2)}) copy-start(f32[4,32,512]{2,1,0:T(8,128)} %copy-done.4) | copy-start | bytes 786436

commit v4 on v3

--- a/solution.py
+++ b/solution.py
@@ -49,19 +49,29 @@
     return lax.rem(lax.axis_index("lev"), 2) == 0
 
 
-def pack_kernel(levels, cols, v, vel, owner, lo, hi, lev_a, lev_b, counts, v_out, vel_out, owner_out):
+def pack_kernel(levels, cols, v_hbm, vel_hbm, owner_hbm, lo, hi, lev_a, lev_b, counts, v, vel, owner, sems):
+    copies = [pltpu.make_async_copy(v_hbm, v, sems.at[0]), pltpu.make_async_copy(owner_hbm, owner, sems.at[1])]
+    for section in range(2):
+        for comp in range(3):
+            sem = sems.at[2 + 3 * section + comp]
+            copies.append(pltpu.make_async_copy(vel_hbm.at[section, comp], vel.at[section, comp], sem))
+    for copy in copies:
+        copy.start()
+
     def edge(low, n):
         return slice(0, n) if low else slice(cols - n, cols)
 
     sides = ((lo, True), (hi, False))
     even = even_level()
     tops = ((lev_a, even), (lev_b, jnp.logical_not(even)))
+    copies[0].wait()
     for msg, low in sides:
         for lev in range(levels):
             msg[lev * LEVEL_ROWS : lev * LEVEL_ROWS + V_ROWS] = v[lev, edge(low, V_ROWS)]
     for msg, top in tops:
         msg[0] = v[jnp.where(top, levels - 1, 0)]
         msg[1] = v[jnp.where(top, levels - 2, 1)]
+    copies[1].wait()
     lanes = lane_iota((1, 128))
     row = jnp.zeros((1, 128), f32)
     held = owner[...]
@@ -75,6 +85,7 @@
         msg[at + B_ROWS : at + B_ROWS + 1, 0:128] = row
     for section, n, start in ((0, A_ROWS, V_ROWS), (1, B_ROWS, B_AT)):
         for comp in range(3):
+            copies[2 + 3 * section + comp].wait()
             for msg, low in sides:
                 for lev in range(levels):
                     at = lev * LEVEL_ROWS + start + comp * n
@@ -84,29 +95,26 @@
                     msg[2 + comp] = vel[0, comp, jnp.where(top, levels - 1, 0)]
 
 
-def corner_kernel(levels, west, east, counts, counts_2, gram, halo_v, halo_a, halo_b, corner_a, corner_b, window):
-    halo_a[...] = jnp.zeros(halo_a.shape, f32)
-    halo_b[...] = jnp.zeros(halo_b.shape, f32)
-    for lev in range(levels):
-        for msg, low in ((east, True), (west, False)):
-
-            def edge(n):
-                return slice(0, n) if low else slice(CHUNK - n, CHUNK)
-
-            base = lev * LEVEL_ROWS
-            halo_v[lev, edge(V_ROWS)] = msg[base : base + V_ROWS]
-            for comp in range(3):
-                at = base + V_ROWS + comp * A_ROWS
-                halo_a[comp, lev, edge(A_ROWS)] = msg[at : at + A_ROWS]
-                at = base + B_AT + comp * B_ROWS
-                halo_b[comp, lev, edge(B_ROWS)] = msg[at : at + B_ROWS]
+def unpack(west, east, n, at):
+    gap = jnp.zeros((CHUNK - 2 * n, west.shape[1]), f32)
+    parts = [east[at : at + n], gap, west[at : at + n]]
+    return jnp.concatenate([x for x in parts if x.shape[0]], axis=0)
+
+
+def corner_kernel(levels, west, east, counts, counts_2, gram, corner_a, corner_b, window):
     even = even_level()
-    for msg, top in ((corner_a, even), (corner_b, jnp.logical_not(even))):
-        near = jnp.where(top, levels - 1, 0)
-        msg[0] = halo_v[near]
-        msg[1] = halo_v[jnp.where(top, levels - 2, 1)]
-        for comp in range(3):
-            msg[2 + comp] = halo_a[comp, near]
+
+    def put(item, top, bottom):
+        corner_a[item] = jnp.where(even, top, bottom)
+        corner_b[item] = jnp.where(even, bottom, top)
+
+    def both(n, start, near=0):
+        return [unpack(west, east, n, lev * LEVEL_ROWS + start) for lev in (levels - 1 - near, near)]
+
+    put(0, *both(V_ROWS, 0))
+    put(1, *both(V_ROWS, 0, 1))
+    for comp in range(3):
+        put(2 + comp, *both(A_ROWS, V_ROWS + comp * A_ROWS))
     at = levels * LEVEL_ROWS + B_ROWS
     window[...] = counts[...] + counts_2[...] + west[at : at + 1, 0:128] + east[at : at + 1, 0:128]
 
@@ -182,13 +190,20 @@
     return slice(CHUNK * k, CHUNK * (k + 1))
 
 
-def first_kernel(levels, cols, lat, v, vel, halo_v, lev_a, lev_b, vv, la, ff):
+def first_kernel(levels, cols, lat, v, vel, west, east, lev_a, lev_b, vv, la, ff, halo_a, halo_b):
     block = Block(levels, cols, lat)
     for k in range(block.chunks):
         block.beyond(lev_a, lev_b, tile(k), k, vv, la)
     for k in range(block.chunks + 1):
         for lev in range(levels):
-            block.put_both(vv, lev + 2, k, v[lev, tile(k)] if k < block.chunks else halo_v[lev])
+            value = v[lev, tile(k)] if k < block.chunks else unpack(west, east, V_ROWS, lev * LEVEL_ROWS)
+            block.put_both(vv, lev + 2, k, value)
+
+    for lev in range(levels):
+        for comp in range(3):
+            base = lev * LEVEL_ROWS + V_ROWS
+            halo_a[comp, lev] = unpack(west, east, A_ROWS, base + comp * A_ROWS)
+            halo_b[comp, lev] = unpack(west, east, B_ROWS, base + 3 * A_ROWS + comp * B_ROWS)
 
     def first_level(lev, carry):
         for k in range(block.chunks):
@@ -212,10 +227,7 @@
     tangent, push, put_both = block.tangent, block.push, block.put_both
 
     block.beyond(corner_a, corner_b, slice(0, CHUNK), chunks, vv, la)
-    own_h[...] = jnp.zeros(own_h.shape, f32)
-    at = levels * LEVEL_ROWS
-    own_h[0:B_ROWS] = east[at : at + B_ROWS]
-    own_h[CHUNK - B_ROWS : CHUNK] = west[at : at + B_ROWS]
+    own_h[...] = unpack(west, east, B_ROWS, levels * LEVEL_ROWS)
 
     def flow(section, k, lev):
         if k < chunks:
@@ -277,7 +289,7 @@
             x = jnp.where(has[side], x, 0.0)
             push(x, flow_beyond(side, k), (u_in, u_e, u_w, u_u, u_d), at, k)
 
-    beta = beta_prev[0]
+    beta = jnp.broadcast_to(beta_prev[:, 0:1], (CHUNK, lat))
     for k in range(chunks):
         cells = slice(CHUNK * k, CHUNK * (k + 1))
         out[0, cells] = u_d[0, rows(k)]
@@ -311,7 +323,8 @@
     return [slice(t, t + 128) for t in range(0, lat, 128)]
 
 
-def gram_kernel(nvec, levels, cols, lat, s, v, prev, order, out, s_out, prev_out, sums):
+def gram_kernel(nvec, levels, cols, lat, beta_prev, s, v, order, out, beta_out, sums):
+    beta_out[...] = jnp.full((1, 128), beta_prev[0], f32)
     sums[...] = jnp.zeros(sums.shape, f32)
     steps = levels * (cols // CHUNK)
     block = 4
@@ -389,7 +402,7 @@
     msg[:, r : r + 1] = jnp.broadcast_to(row[None], (count, 1, 128))
 
 
-def scalar_kernel(nvec, cells_all, msg, out, trust):
+def orthogonal_kernel(nvec, levels, cols, lat, cells_all, msg, applied, v, s, orthogonal, out, trust):
     total = jnp.sum(msg[...], axis=0) * (1.0 / cells_all)
     r = total.shape[0] - 1
     row = total[r : r + 1]
@@ -420,31 +433,33 @@
     out[...] = jnp.where(lanes == 0, alpha, jnp.where(lanes == 1, beta, pltpu.roll(pv, 2, 1)))
 
 
-def finish_kernel(nvec, levels, cols, lat, row, applied, v, s, result_out, coefs_out, result, coefs, sems):
+    a_w = jnp.broadcast_to(alpha, (CHUNK, 128))
+    weights = [jnp.broadcast_to(x, (CHUNK, 128)) for x in p]
+
+    def body(step, carry):
+        lev = step // (cols // CHUNK)
+        at = pl.ds(pl.multiple_of((step - lev * (cols // CHUNK)) * CHUNK, CHUNK), CHUNK)
+        for t in tiles(lat):
+            x = applied[lev, at, t] - a_w * v[lev, at, t]
+            y = weights[0] * s[0, lev, at, t]
+            for k in range(1, nvec):
+                y = y + weights[k] * s[k, lev, at, t]
+            orthogonal[lev, at, t] = x - y
+        return carry
+
+    lax.fori_loop(0, levels * (cols // CHUNK), body, 0)
+
+
+def scale_kernel(nvec, row, orthogonal, result_out, coefs_out, result, coefs, sems):
     line = row[...]
     coefs[...] = line[:, 0 : nvec + 2]
+    copies = [pltpu.make_async_copy(result.at[i], result_out.at[i], sems.at[i]) for i in range(result.shape[0])]
+    copies.append(pltpu.make_async_copy(coefs, coefs_out, sems.at[result.shape[0]]))
+    copies[-1].start()
     inverse = 1.0 / line[:, 1:2]
-    a_w = jnp.broadcast_to(line[:, 0:1] * inverse, (CHUNK, 128))
-    scale = jnp.broadcast_to(inverse, (CHUNK, 128))
-    weights = [jnp.broadcast_to(line[:, 2 + k : 3 + k] * inverse, (CHUNK, 128)) for k in range(nvec)]
-    copies = [pltpu.make_async_copy(result.at[lev], result_out.at[lev], sems.at[lev]) for lev in range(levels)]
-    copies.append(pltpu.make_async_copy(coefs, coefs_out, sems.at[levels]))
-    copies[-1].start()
-
-    for lev in range(levels):
-
-        def body(step, carry, lev=lev):
-            at = pl.ds(pl.multiple_of(step * CHUNK, CHUNK), CHUNK)
-            for t in tiles(lat):
-                x = scale * applied[lev, at, t] - a_w * v[lev, at, t]
-                y = weights[0] * s[0, lev, at, t]
-                for k in range(1, nvec):
-                    y = y + weights[k] * s[k, lev, at, t]
-                result[lev, at, t] = x - y
-            return carry
-
-        lax.fori_loop(0, cols // CHUNK, body, 0)
-        copies[lev].start()
+    for i in range(result.shape[0]):
+        result[i] = orthogonal[i] * inverse
+        copies[i].start()
     for copy in copies:
         copy.wait()
 
@@ -461,31 +476,36 @@
         functools.partial(pack_kernel, levels, cols),
         (sds(lines, lat), sds(lines, lat), sds(5, cols, lat), sds(5, cols, lat), sds(1, 128),
          sds(*v.shape), sds(*vel.shape), jax.ShapeDtypeStruct(owner.shape, owner.dtype)),
-        (v, vel, owner), flops=1 << 20, alias={0: 5, 1: 6, 2: 7},
+        tuple(pltpu.with_memory_space_constraint(x, pltpu.HBM) for x in (v, vel, owner)), specs=[HBM] * 3, scratch=[pltpu.SemaphoreType.DMA((8,))], flops=1 << 20,
     )
     east_of = [(i, (i + 1) % lon_n) for i in range(lon_n)]
     west_of = [((i + 1) % lon_n, i) for i in range(lon_n)]
     pairs_a = [(i, i ^ 1) for i in range(lev_n)]
-    pairs_b = [(i, (i + 1) % lev_n if i % 2 else (i - 1) % lev_n) for i in range(lev_n)]
+    pairs_b = []
+    for i in range(count):
+        at, level = divmod(i, lev_n)
+        if level in (0, lev_n - 1):
+            pairs_b.append((i, (at ^ 1) * lev_n + level))
+        else:
+            pairs_b.append((i, i + 1 if level % 2 else i - 1))
 
     def both(a, b):
-        return lax.ppermute(a, "lev", pairs_a), lax.ppermute(b, "lev", pairs_b)
+        return lax.ppermute(a, "lev", pairs_a), lax.ppermute(b, ("lon", "lev"), pairs_b)
 
     west, east = lax.ppermute(hi, "lon", east_of), lax.ppermute(lo, "lon", west_of)
     lev_a, lev_b = both(lev_a, lev_b)
     counts_2 = lax.ppermute(counts, "lon", [((i + 2) % lon_n, i) for i in range(lon_n)])
 
     gram_rows = nvec * nvec // 128 + 1
-    gram, s, prev = call(
+    gram, beta_row = call(
         functools.partial(gram_kernel, nvec, levels, cols, lat),
-        (sds(gram_rows, 128), sds(*s.shape), sds(*prev.shape)), (s, v, prev, counts),
-        scratch=[pltpu.VMEM((128 * gram_rows, 128), f32)], flops=20 << 20, alias={0: 1, 2: 2},
-    )
-
-    halo_v, halo_a, halo_b, corner_a, corner_b, window = call(
+        (sds(gram_rows, 128), sds(1, 128)), (beta_prev.reshape(1), s, v, counts), specs=[SM, VM, VM, VM],
+        scratch=[pltpu.VMEM((128 * gram_rows, 128), f32)], flops=20 << 20,
+    )
+
+    corner_a, corner_b, window = call(
         functools.partial(corner_kernel, levels),
-        (sds(levels, CHUNK, lat), sds(3, levels, CHUNK, lat), sds(3, levels, CHUNK, lat),
-         sds(5, CHUNK, lat), sds(5, CHUNK, lat), sds(1, 128)),
+        (sds(5, CHUNK, lat), sds(5, CHUNK, lat), sds(1, 128)),
         (west, east, counts, counts_2, gram),
     )
     if lon_n == 8:
@@ -496,18 +516,20 @@
 
     padded = cols + 3 * CHUNK
     state = (sds(levels + 4, padded, lat), sds(2, 3, cols + CHUNK, lat), sds(levels + 2, padded, lat))
-    state = call(
-        functools.partial(first_kernel, levels, cols, lat), state, (v, vel, halo_v, lev_a, lev_b), flops=4 << 20
+    halo = (sds(3, levels, CHUNK, lat), sds(3, levels, CHUNK, lat))
+    *state, halo_a, halo_b = call(
+        functools.partial(first_kernel, levels, cols, lat), (*state, *halo), (v, vel, west, east, lev_a, lev_b),
+        flops=4 << 20,
     )
     scratch = [pltpu.VMEM((CHUNK, lat), f32)]
     scratch += [pltpu.VMEM((levels + 2, padded, lat), f32)] * 10
     scratch += [pltpu.VMEM((levels + 4, cols + CHUNK, lat), f32)]
-    operands = (lw, beta_prev.reshape(1), prev, vel, owner, west, east, halo_a, halo_b, *state,
+    operands = (lw, beta_row, prev, vel, owner, west, east, halo_a, halo_b, *state,
                 corner_a, corner_b, *near)
     part, send_a, send_b = call(
         functools.partial(stencil_kernel, levels, cols, lat, float(cols * lon_n * lat), len(near)),
         (sds(levels, cols, lat), sds(SECOND, cols, lat), sds(SECOND, cols, lat), *(sds(*x.shape) for x in state)),
-        operands, specs=[SM, SM] + [VM] * (len(operands) - 2), scratch=scratch, flops=8 << 20,
+        operands, specs=[SM] + [VM] * (len(operands) - 1), scratch=scratch, flops=8 << 20,
         alias={9: 3, 10: 4, 11: 5},
     )[:3]
     got_a, got_b = both(send_a, send_b)
@@ -519,19 +541,20 @@
     )
     msg = lax.all_to_all(msg, ("lon", "lev"), 0, 0, tiled=True)
     cells = float(v.size * count)
-    row, trust = call(functools.partial(scalar_kernel, nvec, cells), (sds(1, 128), sds(1, 1)), (msg,))
+    orthogonal, row, trust = call(
+        functools.partial(orthogonal_kernel, nvec, levels, cols, lat, cells),
+        (sds(levels, cols, lat), sds(1, 128), sds(1, 1)), (msg, applied, v, s),
+    )
 
     def direct():
-        weights = row[0, 2 : nvec + 2]
-        orthogonal = applied - row[0, 0] * v - jnp.sum(weights[:, None, None, None] * s, axis=0)
         square = lax.psum(jnp.sum(orthogonal * orthogonal), ("lon", "lev")) / cells
         return row.at[0, 1].set(jnp.sqrt(square + 1e-12))
 
     row = lax.cond(trust[0, 0] > 0.5, lambda: row, direct)
     result, coefs = call(
-        functools.partial(finish_kernel, nvec, levels, cols, lat),
+        functools.partial(scale_kernel, nvec),
         (sds(levels, cols, lat), sds(1, nvec + 2)),
-        (row, applied, v, s), out_specs=(HBM, HBM),
+        (row, orthogonal), out_specs=(HBM, HBM),
         scratch=[pltpu.VMEM((levels, cols, lat), f32), pltpu.VMEM((1, nvec + 2), f32),
                  pltpu.SemaphoreType.DMA((levels + 1,))],
     )

time: 53 us -> 48.5 us (0.915)
  Pallas kernels: 15.7 us -> 12.8 us
  local copies, waits for them, and re-layouts: 4.18 us -> 2.2 us
  starting transfers between devices: 13.8 us -> 14.5 us
    pallas_call x8, Pallas kernels: 15.7 us -> 12.8 us  [call(): pl.pallas_call(kernel, out_shape=outs, in_specs=specs or [VM] * len(opera...]
    unnamed x19 -> x8, local copies, waits for them, and re-layouts: 4.18 us -> 2.2 us
    ppermute x1, starting transfers between devices: 3.2 us -> 4.66 us  [body(): lax.ppermute(lo, 'lon', west_of)]
    ppermute x1, starting transfers between devices: 1.52 us -> 0.07 us  [body(): lax.ppermute(hi, 'lon', east_of)]
    ppermute x1, waiting for transfers between devices: 0.74 us -> 0.01 us  [body(): lax.ppermute(lo, 'lon', west_of)]
    ppermute x1, starting transfers between devices: 1.89 us -> 2.59 us  [body(): lax.ppermute(window, 'lon', [(i, i ^ 4) for i in range(lon_n)])]
  transfers between devices with their start and end apart: 10 -> 10, of which waited for: 3 -> 3; matrix products, arithmetic and copies ran while one was open for 0% -> 0% of each run, Pallas kernels for 12% -> 9%
where the time goes in v4:
time: 48.5 us; the launch traced here: 48.3 us
  starting transfers between devices  14.5 us (30%)
  Pallas kernels  12.8 us (26%)
  blocking collectives  11.5 us (24%)
  waiting for transfers between devices  5.15 us (11%)
  local copies, waits for them, and re-layouts  2.2 us (5%)
  between operations  2.07 us (4%)
    pallas_call x8, Pallas kernels, call(): pl.pallas_call(kernel, out_shape=outs, in_specs=specs or [VM] * len(opera...  12.8 us
    all_to_all x1, blocking collectives, body(): msg = lax.all_to_all(msg, ('lon', 'lev'), 0, 0, tiled=True)  11.5 us
    ppermute x3, starting transfers between devices, both(): lax.ppermute(b, ('lon', 'lev'), pairs_b)  4.75 us
    ppermute x1, starting transfers between devices, body(): lax.ppermute(lo, 'lon', west_of)  4.66 us
    ppermute x3, waiting for transfers between devices, both(): lax.ppermute(b, ('lon', 'lev'), pairs_b)  3.7 us
    ppermute x1, starting transfers between devices, body(): lax.ppermute(window, 'lon', [(i, i ^ 4) for i in range(lon_n)])  2.59 us
    unnamed x8, local copies, waits for them, and re-layouts  2.2 us
    ppermute x1, starting transfers between devices, body(): lax.ppermute(counts, 'lon', [((i + 2) % lon_n, i) for i in range(lon_n)])  1.8 us
  transfers between devices with their start and end apart: 10, of which 3 were waited for; matrix products, arithmetic and copies ran while one was open for 0% of the time, Pallas kernels for 9%

profile of v4, /device:TPU:0, one launch (start us, length us, event | category | flops | bytes accessed | tf_op | source)
XLA Modules:
  0.0 48.3 jit_solution(1739460573412188329)
XLA Ops:
  0.6 2.3 %shard_map.86 = (f32[80,512]{1,0:T(8,128)}, f32[80,512]{1,0:T(8,128)}, f32[5,32,512]{2,1,0:T(8,128)S(1)}, f32[5,32,512]{2,1,0:T(8,128)S(1)}, f32[1,128]{1,0:T(1,...) custom-call(f32[4,32,512]{2,1,0:T(8,128)} %v_hbm.1, ...), custom_call_target="tpu_custom_call" | custom-call | flops 1048576 | bytes 1900544 | tf_op jit(solution)/shard_map/pallas_call | solution.py:32
  2.9 0.5 %collective-permute-start.2 = (f32[5,32,512]{2,1,0:T(8,128)S(1)}, f32[5,32,512]{2,1,0:T(8,128)S(1)}, u32[]{:S(2)}, u32[]{:S(2)}) collective-permute-start(f32[5,32,512]{2,1,0:T(8,128)S(1)} %get-tuple-element.59), channel_id=1, source_target_pairs={{0,1},{1,0},{2,3},{3,2},{4,5},{5,4},{6,7},{7,6},{8,9},{9,8},{10,11... | collective-permute-start | bytes 983048 | tf_op jit(solution)/shard_map/ppermute | solution.py:493
  3.4 2.6 %collective-permute-start.3 = (f32[5,32,512]{2,1,0:T(8,128)S(1)}, f32[5,32,512]{2,1,0:T(8,128)S(1)}, u32[]{:S(2)}, u32[]{:S(2)}) collective-permute-start(f32[5,32,512]{2,1,0:T(8,128)S(1)} %get-tuple-element.60), channel_id=1, source_target_pairs={{0,4},{1,2},{2,1},{3,7},{4,0},{5,6},{6,5},{7,3},{8,12},{9,10},{10,... | collective-permute-start | bytes 983048 | tf_op jit(solution)/shard_map/ppermute | solution.py:493
  6.0 0.1 collective-permute-start
  6.1 4.7 %collective-permute-start.1 = (f32[80,512]{1,0:T(8,128)}, f32[80,512]{1,0:T(8,128)S(1)}, u32[]{:S(2)}, u32[]{:S(2)}) collective-permute-start(f32[80,512]{1,0:T(8,128)} %get-tuple-element.58), channel_id=1, source_target_pairs={{4,0},{8,4},{12,8},{16,12},{20,16},{24,20},{28,24},{0,28},{5,1},{9... | collective-permute-start | bytes 491528 | tf_op jit(solution)/shard_map/ppermute | solution.py:495
  10.7 1.8 %collective-permute-start.4 = (f32[1,128]{1,0:T(1,128)S(1)}, f32[1,128]{1,0:T(1,128)S(1)}, u32[]{:S(2)}, u32[]{:S(2)}) collective-permute-start(f32[1,128]{1,0:T(1,128)S(1)} %get-tuple-element.53.order.counts), channel_id=1, source_target_pairs={{8,0},{12,4},{16,8},{20,12},{24,16},{28,20},{0,24},{4,28},{9,1},{1... | collective-permute-start | bytes 1544 | tf_op jit(solution)/shard_map/ppermute | solution.py:497
  13.2 0.0 copy-start
  13.2 2.2 %copy-done = f32[16,4,32,512]{3,2,1,0:T(8,128)S(1)} copy-done((f32[16,4,32,512]{3,2,1,0:T(8,128)S(1)}, f32[16,4,32,512]{3,2,1,0:T(8,128)}, u32[]{:S(2)}) %copy-start) | copy-done | bytes 4194328
  15.4 3.6 %shard_map.87 = (f32[3,128]{1,0:T(4,128)S(1)}, f32[1,128]{1,0:T(1,128)S(1)}) custom-call(f32[1]{0:T(128)} %bitcast.6.beta_prev, f32[16,4,32,512]{3,2,1,0:T(8,128)S(1)} %copy-done, f32[4,32,512]{2,1,0:T(8,128)S(1)} %get-tuple-element.52.v, f32[1,128]{1,0:T(1,128)S(1)} %get-tuple-element.53.order.counts), custom_call_target="tpu_custom_call" | custom-call | flops 20971520 | bytes 4456964 | tf_op jit(solution)/shard_map/pallas_call | solution.py:32
  19.0 0.0 collective-permute-done.4.counts_2
  19.0 0.0 collective-permute-done.west
  19.0 0.0 collective-permute-done.1.east
  19.0 0.0 copy-start.2
  19.0 0.0 copy-start.3
  19.1 0.1 collective-permute-start.5
  19.2 1.1 %collective-permute-start.6 = (f32[5,8,512]{2,1,0:T(8,128)S(1)}, f32[5,8,512]{2,1,0:T(8,128)S(1)}, u32[]{:S(2)}, u32[]{:S(2)}) collective-permute-start(f32[5,8,512]{2,1,0:T(8,128)S(1)} %get-tuple-element.68), channel_id=1, source_target_pairs={{0,4},{1,2},{2,1},{3,7},{4,0},{5,6},{6,5},{7,3},{8,12},{9,10},{10,... | collective-permute-start | bytes 245768 | tf_op jit(solution)/shard_map/ppermute | solution.py:493
  20.3 2.6 %collective-permute-start.7 = (f32[1,128]{1,0:T(1,128)S(1)}, f32[1,128]{1,0:T(1,128)S(1)}, u32[]{:S(2)}, u32[]{:S(2)}) collective-permute-start(f32[1,128]{1,0:T(1,128)S(1)} %get-tuple-element.69.refs_0_), channel_id=1, source_target_pairs={{0,16},{4,20},{8,24},{12,28},{16,0},{20,4},{24,8},{28,12},{1,17},{... | collective-permute-start | bytes 1544 | tf_op jit(solution)/shard_map/ppermute | solution.py:512
  22.9 0.0 collective-permute-done.2.lev_a
  22.9 0.0 collective-permute-done.3.lev_b
  22.9 0.7 %shard_map.88 = (f32[8,56,512]{2,1,0:T(8,128)S(1)}, f32[2,3,40,512]{3,2,1,0:T(8,128)S(1)}, f32[6,56,512]{2,1,0:T(8,128)S(1)}, f32[3,4,8,512]{3,2,1,0:T(8,128)S(1)}, f32[3,4,8,512]{3,2,1,0:T(8,128)S(1)}) custom-call(f32[4,32,512]{2,1,0:T(8,128)S(1)} %get-tuple-element.52.v, f32[2,3,4,32,512]{4,3,2,1,0:T(8,128)S(1)} %get-tuple-element.55.vel, ...), custom_call_target="tpu_custom_call" | custom-call | flops 4194304 | bytes 2818048 | tf_op jit(solution)/shard_map/pallas_call | solution.py:32
  23.6 1.1 %collective-permute-done.7.refs_1_ = f32[1,128]{1,0:T(1,128)S(1)} collective-permute-done((f32[1,128]{1,0:T(1,128)S(1)}, f32[1,128]{1,0:T(1,128)S(1)}, u32[]{:S(2)}, u32[]{:S(2)}) %collective-permute-start.7) | collective-permute-done | bytes 544 | tf_op jit(solution)/shard_map/ppermute | solution.py:512
  24.7 0.0 collective-permute-done.6.corner_b
  24.8 0.0 copy-start.1
  24.8 3.2 %shard_map.90 = (f32[4,32,512]{2,1,0:T(8,128)S(1)}, f32[2,32,512]{2,1,0:T(8,128)S(1)}, f32[2,32,512]{2,1,0:T(8,128)S(1)}, f32[8,56,512]{2,1,0:T(8,128)S(1)}, f32...) custom-call(f32[4]{0:T(128)S(1)} %copy-done.3, ...), custom_call_target="tpu_custom_call", output_to_operand_aliasing={{3}: (9, {}), {4}: (10, {}), {5}: (11, {})} | custom-call | flops 8388608 | bytes 4883984 | tf_op jit(solution)/shard_map/pallas_call | solution.py:32
  28.0 0.1 collective-permute-start.8
  28.1 1.0 %collective-permute-start.9 = (f32[2,32,512]{2,1,0:T(8,128)S(1)}, f32[2,32,512]{2,1,0:T(8,128)S(1)}, u32[]{:S(2)}, u32[]{:S(2)}) collective-permute-start(f32[2,32,512]{2,1,0:T(8,128)S(1)} %get-tuple-element.72), channel_id=1, source_target_pairs={{0,4},{1,2},{2,1},{3,7},{4,0},{5,6},{6,5},{7,3},{8,12},{9,10},{10,... | collective-permute-start | bytes 393224 | tf_op jit(solution)/shard_map/ppermute | solution.py:493
  29.1 0.3 collective-permute-done.8.got_a
  29.4 3.7 %collective-permute-done.9.got_b = f32[2,32,512]{2,1,0:T(8,128)S(1)} collective-permute-done((f32[2,32,512]{2,1,0:T(8,128)S(1)}, f32[2,32,512]{2,1,0:T(8,128)S(1)}, u32[]{:S(2)}, u32[]{:S(2)}) %collective-permute-start.9) | collective-permute-done | bytes 131104 | tf_op jit(solution)/shard_map/ppermute | solution.py:493
  33.1 0.6 %shard_map.91 = (f32[4,32,512]{2,1,0:T(8,128)S(1)}, f32[32,3,128]{2,1,0:T(4,128)S(1)}) custom-call(f32[4,32,512]{2,1,0:T(8,128)S(1)} %get-tuple-element.70.part, f32[2,32,512]{2,1,0:T(8,128)S(1)} %collective-permute-done.8.got_a, f32[2,32,512]{2,1,0:T(8,128)S(1)} %collective-permute-done.9.got_b, f32[4,32,512]{2,1,0:T(8,128)S(1)} %get-tuple-element.52.v, ...), custom_call_target="tpu_custom_call" | custom-call | bytes 4982272 | tf_op jit(solution)/shard_map/pallas_call | solution.py:32
  33.8 11.5 %all_to_all.5.msg = f32[32,3,128]{2,1,0:T(4,128)S(1)} all-to-all(f32[32,3,128]{2,1,0:T(4,128)S(1)} %get-tuple-element.73), channel_id=1, replica_groups=mesh['lon'=8,'lev'=4] {'lon','lev'}, dimensions={0} | all-to-all | bytes 98304 | tf_op jit(solution)/shard_map/all_to_all | solution.py:542
  45.3 1.5 %shard_map.92 = (f32[4,32,512]{2,1,0:T(8,128)S(1)}, f32[1,128]{1,0:T(1,128)S(1)}, f32[1,1]{1,0:T(1,128)}) custom-call(f32[32,3,128]{2,1,0:T(4,128)S(1)} %all_to_all.5.msg, f32[4,32,512]{2,1,0:T(8,128)S(1)} %get-tuple-element.74.applied, f32[4,32,512]{2,1,0:T(8,128)S(1)} %get-tuple-element.52.v, f32[16,4,32,512]{3,2,1,0:T(8,128)S(1)} %copy-done.1), custom_call_target="tpu_custom_call" | custom-call | bytes 4767744 | tf_op jit(solution)/shard_map/pallas_call | solution.py:32
  47.4 0.8 %shard_map.93 = (f32[4,32,512]{2,1,0:T(8,128)}, f32[1,18]{1,0:T(1,128)}) custom-call(f32[1,128]{1,0:T(1,128)S(1)} %get-tuple-element.80.row, f32[4,32,512]{2,1,0:T(8,128)S(1)} %get-tuple-element.76.orthogonal), custom_call_target="tpu_custom_call" | custom-call | bytes 262656 | tf_op jit(solution)/shard_map/pallas_call | solution.py:32
  (6 shorter events, 0.1 us)
Async XLA Ops:
  2.9 20.0 %collective-permute-start.2 = (f32[5,32,512]{2,1,0:T(8,128)S(1)}, f32[5,32,512]{2,1,0:T(8,128)S(1)}, u32[]{:S(2)}, u32[]{:S(2)}) collective-permute-start(f32[5,32,512]{2,1,0:T(8,128)S(1)} %get-tuple-element.59), channel_id=1, source_target_pairs={{0,1},{1,0},{2,3},{3,2},{4,5},{5,4},{6,7},{7,6},{8,9},{9,8},{10,11... | collective-permute-start | bytes 983048 | tf_op jit(solution)/shard_map/ppermute | solution.py:493
  3.4 19.5 %collective-permute-start.3 = (f32[5,32,512]{2,1,0:T(8,128)S(1)}, f32[5,32,512]{2,1,0:T(8,128)S(1)}, u32[]{:S(2)}, u32[]{:S(2)}) collective-permute-start(f32[5,32,512]{2,1,0:T(8,128)S(1)} %get-tuple-element.60), channel_id=1, source_target_pairs={{0,4},{1,2},{2,1},{3,7},{4,0},{5,6},{6,5},{7,3},{8,12},{9,10},{10,... | collective-permute-start | bytes 983048 | tf_op jit(solution)/shard_map/ppermute | solution.py:493
  6.0 13.0 %collective-permute-start = (f32[80,512]{1,0:T(8,128)}, f32[80,512]{1,0:T(8,128)S(1)}, u32[]{:S(2)}, u32[]{:S(2)}) collective-permute-start(f32[80,512]{1,0:T(8,128)} %get-tuple-element.57), channel_id=1, source_target_pairs={{0,4},{4,8},{8,12},{12,16},{16,20},{20,24},{24,28},{28,0},{1,5},{5... | collective-permute-start | bytes 491528 | tf_op jit(solution)/shard_map/ppermute | solution.py:495
  6.1 12.9 %collective-permute-start.1 = (f32[80,512]{1,0:T(8,128)}, f32[80,512]{1,0:T(8,128)S(1)}, u32[]{:S(2)}, u32[]{:S(2)}) collective-permute-start(f32[80,512]{1,0:T(8,128)} %get-tuple-element.58), channel_id=1, source_target_pairs={{4,0},{8,4},{12,8},{16,12},{20,16},{24,20},{28,24},{0,28},{5,1},{9... | collective-permute-start | bytes 491528 | tf_op jit(solution)/shard_map/ppermute | solution.py:495
  10.7 8.3 %collective-permute-start.4 = (f32[1,128]{1,0:T(1,128)S(1)}, f32[1,128]{1,0:T(1,128)S(1)}, u32[]{:S(2)}, u32[]{:S(2)}) collective-permute-start(f32[1,128]{1,0:T(1,128)S(1)} %get-tuple-element.53.order.counts), channel_id=1, source_target_pairs={{8,0},{12,4},{16,8},{20,12},{24,16},{28,20},{0,24},{4,28},{9,1},{1... | collective-permute-start | bytes 1544 | tf_op jit(solution)/shard_map/ppermute | solution.py:497
  13.2 2.2 %copy-start = (f32[16,4,32,512]{3,2,1,0:T(8,128)S(1)}, f32[16,4,32,512]{3,2,1,0:T(8,128)}, u32[]{:S(2)}) copy-start(f32[16,4,32,512]{3,2,1,0:T(8,128)} %s.5) | copy-start | bytes 12582916
  19.0 5.7 %copy-start.2 = (f32[4,32,512]{2,1,0:T(8,128)S(1)}, f32[4,32,512]{2,1,0:T(8,128)}, u32[]{:S(2)}) copy-start(f32[4,32,512]{2,1,0:T(8,128)} %prev.1) | copy-start | bytes 786436
  19.0 5.7 %copy-start.3 = (f32[4]{0:T(128)S(1)}, f32[4]{0:T(128)}, u32[]{:S(2)}) copy-start(f32[4]{0:T(128)} %lw.1) | copy-start | bytes 52
  19.1 5.6 %collective-permute-start.5 = (f32[5,8,512]{2,1,0:T(8,128)S(1)}, f32[5,8,512]{2,1,0:T(8,128)S(1)}, u32[]{:S(2)}, u32[]{:S(2)}) collective-permute-start(f32[5,8,512]{2,1,0:T(8,128)S(1)} %get-tuple-element.67), channel_id=1, source_target_pairs={{0,1},{1,0},{2,3},{3,2},{4,5},{5,4},{6,7},{7,6},{8,9},{9,8},{10,11... | collective-permute-start | bytes 245768 | tf_op jit(solution)/shard_map/ppermute | solution.py:493
  19.2 5.6 %collective-permute-start.6 = (f32[5,8,512]{2,1,0:T(8,128)S(1)}, f32[5,8,512]{2,1,0:T(8,128)S(1)}, u32[]{:S(2)}, u32[]{:S(2)}) collective-permute-start(f32[5,8,512]{2,1,0:T(8,128)S(1)} %get-tuple-element.68), channel_id=1, source_target_pairs={{0,4},{1,2},{2,1},{3,7},{4,0},{5,6},{6,5},{7,3},{8,12},{9,10},{10,... | collective-permute-start | bytes 245768 | tf_op jit(solution)/shard_map/ppermute | solution.py:493
  20.3 4.4 %collective-permute-start.7 = (f32[1,128]{1,0:T(1,128)S(1)}, f32[1,128]{1,0:T(1,128)S(1)}, u32[]{:S(2)}, u32[]{:S(2)}) collective-permute-start(f32[1,128]{1,0:T(1,128)S(1)} %get-tuple-element.69.refs_0_), channel_id=1, source_target_pairs={{0,16},{4,20},{8,24},{12,28},{16,0},{20,4},{24,8},{28,12},{1,17},{... | collective-permute-start | bytes 1544 | tf_op jit(solution)/shard_map/ppermute | solution.py:512
  24.8 8.4 %copy-start.1 = (f32[16,4,32,512]{3,2,1,0:T(8,128)S(1)}, f32[16,4,32,512]{3,2,1,0:T(8,128)}, u32[]{:S(2)}) copy-start(f32[16,4,32,512]{3,2,1,0:T(8,128)} %s.5) | copy-start | bytes 12582916
  28.0 1.4 %collective-permute-start.8 = (f32[2,32,512]{2,1,0:T(8,128)S(1)}, f32[2,32,512]{2,1,0:T(8,128)S(1)}, u32[]{:S(2)}, u32[]{:S(2)}) collective-permute-start(f32[2,32,512]{2,1,0:T(8,128)S(1)} %get-tuple-element.71), channel_id=1, source_target_pairs={{0,1},{1,0},{2,3},{3,2},{4,5},{5,4},{6,7},{7,6},{8,9},{9,8},{10,11... | collective-permute-start | bytes 393224 | tf_op jit(solution)/shard_map/ppermute | solution.py:493
  28.1 5.0 %collective-permute-start.9 = (f32[2,32,512]{2,1,0:T(8,128)S(1)}, f32[2,32,512]{2,1,0:T(8,128)S(1)}, u32[]{:S(2)}, u32[]{:S(2)}) collective-permute-start(f32[2,32,512]{2,1,0:T(8,128)S(1)} %get-tuple-element.72), channel_id=1, source_target_pairs={{0,4},{1,2},{2,1},{3,7},{4,0},{5,6},{6,5},{7,3},{8,12},{9,10},{10,... | collective-permute-start | bytes 393224 | tf_op jit(solution)/shard_map/ppermute | solution.py:493

commit v5 on v4

--- a/solution.py
+++ b/solution.py
@@ -39,6 +39,10 @@
         compiler_params=pltpu.CompilerParams(vmem_limit_bytes=16 << 20),
         cost_estimate=pl.CostEstimate(flops=flops, bytes_accessed=nbytes, transcendentals=0),
     )(*operands)
+
+
+def in_hbm(x):
+    return pltpu.with_memory_space_constraint(x, pltpu.HBM)
 
 
 def lane_iota(shape):
@@ -101,7 +105,7 @@
     return jnp.concatenate([x for x in parts if x.shape[0]], axis=0)
 
 
-def corner_kernel(levels, west, east, counts, counts_2, gram, corner_a, corner_b, window):
+def corner_kernel(levels, west, east, window, lev_a, lev_b, corner_a, corner_b):
     even = even_level()
 
     def put(item, top, bottom):
@@ -115,6 +119,9 @@
     put(1, *both(V_ROWS, 0, 1))
     for comp in range(3):
         put(2 + comp, *both(A_ROWS, V_ROWS + comp * A_ROWS))
+
+
+def window_kernel(levels, west, east, counts, counts_2, order, window):
     at = levels * LEVEL_ROWS + B_ROWS
     window[...] = counts[...] + counts_2[...] + west[at : at + 1, 0:128] + east[at : at + 1, 0:128]
 
@@ -216,7 +223,7 @@
 
 def stencil_kernel(
     levels, cols, lat, columns, n_counts,
-    lw, beta_prev, prev, vel, owner, west, east, halo_a, halo_b,
+    lw, vel, owner, west, east, halo_a, halo_b,
     vv_in, la_in, ff_in, corner_a, corner_b, *refs,
 ):
     count_refs = refs[:n_counts]
@@ -289,7 +296,6 @@
             x = jnp.where(has[side], x, 0.0)
             push(x, flow_beyond(side, k), (u_in, u_e, u_w, u_u, u_d), at, k)
 
-    beta = jnp.broadcast_to(beta_prev[:, 0:1], (CHUNK, lat))
     for k in range(chunks):
         cells = slice(CHUNK * k, CHUNK * (k + 1))
         out[0, cells] = u_d[0, rows(k)]
@@ -301,7 +307,7 @@
             if at < levels + 1:
                 x = x + u_d[at + 1, rows(k)]
             if 1 <= at <= levels:
-                applied[at - 1, cells] = x - beta * prev[at - 1, cells]
+                applied[at - 1, cells] = x
             else:
                 out[at + 1, cells] = x
     up = jnp.where(even, levels + 2, 0)
@@ -323,8 +329,17 @@
     return [slice(t, t + 128) for t in range(0, lat, 128)]
 
 
-def gram_kernel(nvec, levels, cols, lat, beta_prev, s, v, order, out, beta_out, sums):
+def load_kernel(beta_prev, s_hbm, prev_hbm, order, beta_out, s, prev, sems):
+    copies = [pltpu.make_async_copy(s_hbm.at[i], s.at[i], sems.at[i]) for i in range(s.shape[0])]
+    copies.append(pltpu.make_async_copy(prev_hbm, prev, sems.at[s.shape[0]]))
+    for copy in copies:
+        copy.start()
     beta_out[...] = jnp.full((1, 128), beta_prev[0], f32)
+    for copy in copies:
+        copy.wait()
+
+
+def gram_kernel(nvec, levels, cols, lat, s, v, order, out, sums):
     sums[...] = jnp.zeros(sums.shape, f32)
     steps = levels * (cols // CHUNK)
     block = 4
@@ -365,18 +380,21 @@
         out[r : r + 1] = to_lanes(sums, 128 * r)
 
 
-def gather_kernel(nvec, levels, cols, lat, count, part, got_a, got_b, v, s, gram, applied, msg, sums):
+def gather_kernel(nvec, levels, cols, lat, count, part, got_a, got_b, prev, beta_prev, v, s, gram, applied, msg, sums):
     level = lax.axis_index("lev")
     has = (level > 0, level < lax.axis_size("lev") - 1)
     even = even_level()
+    beta = jnp.broadcast_to(beta_prev[:, 0:1], (CHUNK, lat))
     for k in range(cols // CHUNK):
         cells = slice(CHUNK * k, CHUNK * (k + 1))
-        for i in range(SECOND):
-            a, b = got_a[i, cells], got_b[i, cells]
-            below, above = jnp.where(even, b, a), jnp.where(even, a, b)
-            applied[i, cells] = part[i, cells] + jnp.where(has[0], below, 0.0)
-            top = levels - SECOND + i
-            applied[top, cells] = part[top, cells] + jnp.where(has[1], above, 0.0)
+        for lev in range(levels):
+            x = part[lev, cells] - beta * prev[lev, cells]
+            if lev < SECOND:
+                x = x + jnp.where(has[0], jnp.where(even, got_b[lev, cells], got_a[lev, cells]), 0.0)
+            if lev >= levels - SECOND:
+                i = lev - levels + SECOND
+                x = x + jnp.where(has[1], jnp.where(even, got_a[i, cells], got_b[i, cells]), 0.0)
+            applied[lev, cells] = x
     sums[...] = jnp.zeros(sums.shape, f32)
     steps = levels * (cols // CHUNK)
 
@@ -476,7 +494,7 @@
         functools.partial(pack_kernel, levels, cols),
         (sds(lines, lat), sds(lines, lat), sds(5, cols, lat), sds(5, cols, lat), sds(1, 128),
          sds(*v.shape), sds(*vel.shape), jax.ShapeDtypeStruct(owner.shape, owner.dtype)),
-        tuple(pltpu.with_memory_space_constraint(x, pltpu.HBM) for x in (v, vel, owner)), specs=[HBM] * 3, scratch=[pltpu.SemaphoreType.DMA((8,))], flops=1 << 20,
+        tuple(in_hbm(x) for x in (v, vel, owner)), specs=[HBM] * 3, scratch=[pltpu.SemaphoreType.DMA((8,))], flops=1 << 20,
     )
     east_of = [(i, (i + 1) % lon_n) for i in range(lon_n)]
     west_of = [((i + 1) % lon_n, i) for i in range(lon_n)]
@@ -492,26 +510,26 @@
     def both(a, b):
         return lax.ppermute(a, "lev", pairs_a), lax.ppermute(b, ("lon", "lev"), pairs_b)
 
+    around = [(i, (i + 1) % lev_n if i % 2 else (i - 1) % lev_n) for i in range(lev_n)]
+
     west, east = lax.ppermute(hi, "lon", east_of), lax.ppermute(lo, "lon", west_of)
-    lev_a, lev_b = both(lev_a, lev_b)
+    lev_a, lev_b = lax.ppermute(lev_a, "lev", pairs_a), lax.ppermute(lev_b, "lev", around)
     counts_2 = lax.ppermute(counts, "lon", [((i + 2) % lon_n, i) for i in range(lon_n)])
 
-    gram_rows = nvec * nvec // 128 + 1
-    gram, beta_row = call(
-        functools.partial(gram_kernel, nvec, levels, cols, lat),
-        (sds(gram_rows, 128), sds(1, 128)), (beta_prev.reshape(1), s, v, counts), specs=[SM, VM, VM, VM],
-        scratch=[pltpu.VMEM((128 * gram_rows, 128), f32)], flops=20 << 20,
-    )
-
-    corner_a, corner_b, window = call(
-        functools.partial(corner_kernel, levels),
-        (sds(5, CHUNK, lat), sds(5, CHUNK, lat), sds(1, 128)),
-        (west, east, counts, counts_2, gram),
-    )
+    beta_row, s, prev = call(
+        load_kernel, (sds(1, 128), sds(*s.shape), sds(*prev.shape)),
+        (beta_prev.reshape(1), in_hbm(s), in_hbm(prev), counts), specs=[SM, HBM, HBM, VM],
+        scratch=[pltpu.SemaphoreType.DMA((nvec + 1,))],
+    )
+    window = call(functools.partial(window_kernel, levels), sds(1, 128), (west, east, counts, counts_2, beta_row))
     if lon_n == 8:
         near = [window, lax.ppermute(window, "lon", [(i, i ^ 4) for i in range(lon_n)])]
     else:
         near = [lax.psum(counts, "lon")]
+    corner_a, corner_b = call(
+        functools.partial(corner_kernel, levels),
+        (sds(5, CHUNK, lat), sds(5, CHUNK, lat)), (west, east, window, lev_a, lev_b),
+    )
     corner_a, corner_b = both(corner_a, corner_b)
 
     padded = cols + 3 * CHUNK
@@ -524,19 +542,25 @@
     scratch = [pltpu.VMEM((CHUNK, lat), f32)]
     scratch += [pltpu.VMEM((levels + 2, padded, lat), f32)] * 10
     scratch += [pltpu.VMEM((levels + 4, cols + CHUNK, lat), f32)]
-    operands = (lw, beta_row, prev, vel, owner, west, east, halo_a, halo_b, *state,
+    operands = (lw, vel, owner, west, east, halo_a, halo_b, *state,
                 corner_a, corner_b, *near)
     part, send_a, send_b = call(
         functools.partial(stencil_kernel, levels, cols, lat, float(cols * lon_n * lat), len(near)),
         (sds(levels, cols, lat), sds(SECOND, cols, lat), sds(SECOND, cols, lat), *(sds(*x.shape) for x in state)),
         operands, specs=[SM] + [VM] * (len(operands) - 1), scratch=scratch, flops=8 << 20,
-        alias={9: 3, 10: 4, 11: 5},
+        alias={7: 3, 8: 4, 9: 5},
     )[:3]
     got_a, got_b = both(send_a, send_b)
+    gram_rows = nvec * nvec // 128 + 1
+    gram = call(
+        functools.partial(gram_kernel, nvec, levels, cols, lat),
+        sds(gram_rows, 128), (s, v, send_a),
+        scratch=[pltpu.VMEM((128 * gram_rows, 128), f32)], flops=20 << 20,
+    )
     applied, msg = call(
         functools.partial(gather_kernel, nvec, levels, cols, lat, count),
         (sds(levels, cols, lat), sds(count, gram_rows, 128)),
-        (part, got_a, got_b, v, s, gram),
+        (part, got_a, got_b, prev, beta_row, v, s, gram),
         scratch=[pltpu.VMEM((128, 128), f32)],
     )
     msg = lax.all_to_all(msg, ("lon", "lev"), 0, 0, tiled=True)

time: 48.5 us -> 46.2 us (0.953)
  waiting for transfers between devices: 5.15 us -> 2.72 us
  Pallas kernels: 12.8 us -> 15.2 us
  local copies, waits for them, and re-layouts: 2.2 us -> 0.01 us
    ppermute x3 -> x2, waiting for transfers between devices: 3.7 us -> 0.01 us  [both(): lax.ppermute(b, ('lon', 'lev'), pairs_b)]
    ppermute x0 -> x2, starting transfers between devices: none -> 3.13 us  [the longest x1 2.61 us: body(): lax.ppermute(lev_b, 'lev', around)]
    ppermute x3 -> x2, starting transfers between devices: 4.75 us -> 2.14 us  [both(): lax.ppermute(b, ('lon', 'lev'), pairs_b)]
    pallas_call x8 -> x10, Pallas kernels: 12.8 us -> 15.2 us  [call(): pl.pallas_call(kernel, out_shape=outs, in_specs=specs or [VM] * len(opera...]
    unnamed x8 -> x2, local copies, waits for them, and re-layouts: 2.2 us -> 0.01 us
    ppermute x1, waiting for transfers between devices: 0.01 us -> 1.54 us  [body(): lax.ppermute(lo, 'lon', west_of)]
    ppermute x1, starting transfers between devices: 4.66 us -> 3.2 us  [body(): lax.ppermute(lo, 'lon', west_of)]
    ppermute x1, starting transfers between devices: 0.07 us -> 1.52 us  [body(): lax.ppermute(hi, 'lon', east_of)]
  transfers between devices with their start and end apart: 10 -> 10, of which waited for: 3 -> 2; matrix products, arithmetic and copies ran while one was open for 0% -> 0% of each run, Pallas kernels for 9% -> 15%
where the time goes in v5:
time: 46.2 us; the launch traced here: 46 us
  Pallas kernels  15.2 us (33%)
  starting transfers between devices  14.6 us (32%)
  blocking collectives  11.5 us (25%)
  waiting for transfers between devices  2.72 us (6%)
  between operations  2.05 us (4%)
    pallas_call x10, Pallas kernels, call(): pl.pallas_call(kernel, out_shape=outs, in_specs=specs or [VM] * len(opera...  15.2 us
    all_to_all x1, blocking collectives, body(): msg = lax.all_to_all(msg, ('lon', 'lev'), 0, 0, tiled=True)  11.5 us
    ppermute x1, starting transfers between devices, body(): lax.ppermute(lo, 'lon', west_of)  3.2 us
    ppermute x1, starting transfers between devices, body(): lax.ppermute(lev_b, 'lev', around)  2.61 us
    ppermute x1, starting transfers between devices, body(): lax.ppermute(window, 'lon', [(i, i ^ 4) for i in range(lon_n)])  2.59 us
    ppermute x2, starting transfers between devices, both(): lax.ppermute(b, ('lon', 'lev'), pairs_b)  2.14 us
    ppermute x1, starting transfers between devices, body(): lax.ppermute(counts, 'lon', [((i + 2) % lon_n, i) for i in range(lon_n)])  1.8 us
    ppermute x1, waiting for transfers between devices, body(): lax.ppermute(lo, 'lon', west_of)  1.54 us
  transfers between devices with their start and end apart: 10, of which 2 were waited for; matrix products, arithmetic and copies ran while one was open for 0% of the time, Pallas kernels for 15%

profile of v5, /device:TPU:0, one launch (start us, length us, event | category | flops | bytes accessed | tf_op | source)
XLA Modules:
  0.0 46.0 jit_solution(18075845278137262401)
XLA Ops:
  0.6 2.3 %shard_map.86 = (f32[80,512]{1,0:T(8,128)}, f32[80,512]{1,0:T(8,128)}, f32[5,32,512]{2,1,0:T(8,128)S(1)}, f32[5,32,512]{2,1,0:T(8,128)S(1)}, f32[1,128]{1,0:T(1,...) custom-call(f32[4,32,512]{2,1,0:T(8,128)} %v_hbm.1, ...), custom_call_target="tpu_custom_call" | custom-call | flops 1048576 | bytes 1900544 | tf_op jit(solution)/shard_map/pallas_call | solution.py:32
  2.9 0.5 %collective-permute-start.2 = (f32[5,32,512]{2,1,0:T(8,128)S(1)}, f32[5,32,512]{2,1,0:T(8,128)S(1)}, u32[]{:S(2)}, u32[]{:S(2)}) collective-permute-start(f32[5,32,512]{2,1,0:T(8,128)S(1)} %get-tuple-element.57), channel_id=1, source_target_pairs={{0,1},{1,0},{2,3},{3,2},{4,5},{5,4},{6,7},{7,6},{8,9},{9,8},{10,11... | collective-permute-start | bytes 983048 | tf_op jit(solution)/shard_map/ppermute | solution.py:516
  3.4 2.6 %collective-permute-start.3 = (f32[5,32,512]{2,1,0:T(8,128)S(1)}, f32[5,32,512]{2,1,0:T(8,128)S(1)}, u32[]{:S(2)}, u32[]{:S(2)}) collective-permute-start(f32[5,32,512]{2,1,0:T(8,128)S(1)} %get-tuple-element.58), channel_id=1, source_target_pairs={{0,3},{1,2},{2,1},{3,0},{4,7},{5,6},{6,5},{7,4},{8,11},{9,10},{10,... | collective-permute-start | bytes 983048 | tf_op jit(solution)/shard_map/ppermute | solution.py:516
  6.0 1.5 %collective-permute-start = (f32[80,512]{1,0:T(8,128)}, f32[80,512]{1,0:T(8,128)S(1)}, u32[]{:S(2)}, u32[]{:S(2)}) collective-permute-start(f32[80,512]{1,0:T(8,128)} %get-tuple-element.54), channel_id=1, source_target_pairs={{0,4},{4,8},{8,12},{12,16},{16,20},{20,24},{24,28},{28,0},{1,5},{5... | collective-permute-start | bytes 491528 | tf_op jit(solution)/shard_map/ppermute | solution.py:515
  7.6 3.2 %collective-permute-start.1 = (f32[80,512]{1,0:T(8,128)}, f32[80,512]{1,0:T(8,128)S(1)}, u32[]{:S(2)}, u32[]{:S(2)}) collective-permute-start(f32[80,512]{1,0:T(8,128)} %get-tuple-element.55), channel_id=1, source_target_pairs={{4,0},{8,4},{12,8},{16,12},{20,16},{24,20},{28,24},{0,28},{5,1},{9... | collective-permute-start | bytes 491528 | tf_op jit(solution)/shard_map/ppermute | solution.py:515
  10.8 1.8 %collective-permute-start.4 = (f32[1,128]{1,0:T(1,128)S(1)}, f32[1,128]{1,0:T(1,128)S(1)}, u32[]{:S(2)}, u32[]{:S(2)}) collective-permute-start(f32[1,128]{1,0:T(1,128)S(1)} %get-tuple-element.64.order.counts), channel_id=1, source_target_pairs={{8,0},{12,4},{16,8},{20,12},{24,16},{28,20},{0,24},{4,28},{9,1},{1... | collective-permute-start | bytes 1544 | tf_op jit(solution)/shard_map/ppermute | solution.py:517
  13.2 0.0 copy-start
  13.2 2.4 %shard_map.88 = (f32[1,128]{1,0:T(1,128)S(1)}, f32[16,4,32,512]{3,2,1,0:T(8,128)S(1)}, f32[4,32,512]{2,1,0:T(8,128)S(1)}) custom-call(f32[1]{0:T(128)} %bitcast.6.beta_prev, f32[16,4,32,512]{3,2,1,0:T(8,128)} %s_hbm.1, f32[4,32,512]{2,1,0:T(8,128)} %prev_hbm.1, f32[1,128]{1,0:T(1,128)S(1)} %get-tuple-element.64.order.counts), custom_call_target="tpu_custom_call" | custom-call | bytes 4456964 | tf_op jit(solution)/shard_map/pallas_call | solution.py:32
  15.6 0.0 collective-permute-done.4.counts_2
  15.6 0.0 collective-permute-done.west
  15.6 1.5 %collective-permute-done.1.east = f32[80,512]{1,0:T(8,128)S(1)} collective-permute-done((f32[80,512]{1,0:T(8,128)}, f32[80,512]{1,0:T(8,128)S(1)}, u32[]{:S(2)}, u32[]{:S(2)}) %collective-permute-start.1) | collective-permute-done | bytes 163872 | tf_op jit(solution)/shard_map/ppermute | solution.py:515
  17.2 0.0 collective-permute-done.2.lev_a
  17.2 0.0 collective-permute-done.3.lev_b
  17.2 0.1 collective-permute-start.5
  17.3 0.4 collective-permute-start.6
  17.7 2.6 %collective-permute-start.7 = (f32[1,128]{1,0:T(1,128)S(1)}, f32[1,128]{1,0:T(1,128)S(1)}, u32[]{:S(2)}, u32[]{:S(2)}) collective-permute-start(f32[1,128]{1,0:T(1,128)S(1)} %shard_map.89.window.refs_0_), channel_id=1, source_target_pairs={{0,16},{4,20},{8,24},{12,28},{16,0},{20,4},{24,8},{28,12},{1,17},{... | collective-permute-start | bytes 1544 | tf_op jit(solution)/shard_map/ppermute | solution.py:526
  20.2 0.7 %shard_map.87 = (f32[8,56,512]{2,1,0:T(8,128)S(1)}, f32[2,3,40,512]{3,2,1,0:T(8,128)S(1)}, f32[6,56,512]{2,1,0:T(8,128)S(1)}, f32[3,4,8,512]{3,2,1,0:T(8,128)S(1)}, f32[3,4,8,512]{3,2,1,0:T(8,128)S(1)}) custom-call(f32[4,32,512]{2,1,0:T(8,128)S(1)} %get-tuple-element.56.v, f32[2,3,4,32,512]{4,3,2,1,0:T(8,128)S(1)} %get-tuple-element.52.vel, ...), custom_call_target="tpu_custom_call" | custom-call | flops 4194304 | bytes 2818048 | tf_op jit(solution)/shard_map/pallas_call | solution.py:32
  21.0 1.2 %collective-permute-done.7.refs_1_ = f32[1,128]{1,0:T(1,128)S(1)} collective-permute-done((f32[1,128]{1,0:T(1,128)S(1)}, f32[1,128]{1,0:T(1,128)S(1)}, u32[]{:S(2)}, u32[]{:S(2)}) %collective-permute-start.7) | collective-permute-done | bytes 544 | tf_op jit(solution)/shard_map/ppermute | solution.py:526
  22.1 0.0 collective-permute-done.5.corner_a
  22.1 0.0 collective-permute-done.6.corner_b
  22.1 0.0 copy-done
  22.1 3.2 %shard_map.91 = (f32[4,32,512]{2,1,0:T(8,128)S(1)}, f32[2,32,512]{2,1,0:T(8,128)S(1)}, f32[2,32,512]{2,1,0:T(8,128)S(1)}, f32[8,56,512]{2,1,0:T(8,128)S(1)}, f32...) custom-call(f32[4]{0:T(128)S(1)} %copy-done, ...), custom_call_target="tpu_custom_call", output_to_operand_aliasing={{3}: (7, {}), {4}: (8, {}), {5}: (9, {})} | custom-call | flops 8388608 | bytes 4621328 | tf_op jit(solution)/shard_map/pallas_call | solution.py:32
  25.3 1.8 %collective-permute-start.9 = (f32[2,32,512]{2,1,0:T(8,128)S(1)}, f32[2,32,512]{2,1,0:T(8,128)S(1)}, u32[]{:S(2)}, u32[]{:S(2)}) collective-permute-start(f32[2,32,512]{2,1,0:T(8,128)S(1)} %get-tuple-element.70), channel_id=1, source_target_pairs={{0,4},{1,2},{2,1},{3,7},{4,0},{5,6},{6,5},{7,3},{8,12},{9,10},{10,... | collective-permute-start | bytes 393224 | tf_op jit(solution)/shard_map/ppermute | solution.py:511
  27.1 0.2 collective-permute-start.8
  27.3 3.6 %shard_map.92.gram = f32[3,128]{1,0:T(4,128)S(1)} custom-call(f32[16,4,32,512]{3,2,1,0:T(8,128)S(1)} %get-tuple-element.72.s, f32[4,32,512]{2,1,0:T(8,128)S(1)} %get-tuple-element.56.v, f32[2,32,512]{2,1,0:T(8,128)S(1)} %get-tuple-element.69.order), custom_call_target="tpu_custom_call" | custom-call | flops 20971520 | bytes 4587520 | tf_op jit(solution)/shard_map/pallas_call | solution.py:32
  30.9 0.0 collective-permute-done.9.got_b
  30.9 0.0 collective-permute-done.8.got_a
  30.9 0.7 %shard_map.93 = (f32[4,32,512]{2,1,0:T(8,128)S(1)}, f32[32,3,128]{2,1,0:T(4,128)S(1)}) custom-call(f32[4,32,512]{2,1,0:T(8,128)S(1)} %get-tuple-element.68.part, f32[2,32,512]{2,1,0:T(8,128)S(1)} %collective-permute-done.8.got_a, f32[2,32,512]{2,1,0:T(8,128)S(1)} %collective-permute-done.9.got_b, f32[4,32,512]{2,1,0:T(8,128)S(1)} %get-tuple-element.71.prev, ...), custom_call_target="tpu_custom_call" | custom-call | bytes 5244928 | tf_op jit(solution)/shard_map/pallas_call | solution.py:32
  31.6 11.5 %all_to_all.5.msg = f32[32,3,128]{2,1,0:T(4,128)S(1)} all-to-all(f32[32,3,128]{2,1,0:T(4,128)S(1)} %get-tuple-element.73), channel_id=1, replica_groups=mesh['lon'=8,'lev'=4] {'lon','lev'}, dimensions={0} | all-to-all | bytes 98304 | tf_op jit(solution)/shard_map/all_to_all | solution.py:566
  43.1 1.5 %shard_map.94 = (f32[4,32,512]{2,1,0:T(8,128)S(1)}, f32[1,128]{1,0:T(1,128)S(1)}, f32[1,1]{1,0:T(1,128)}) custom-call(f32[32,3,128]{2,1,0:T(4,128)S(1)} %all_to_all.5.msg, f32[4,32,512]{2,1,0:T(8,128)S(1)} %get-tuple-element.74.applied, f32[4,32,512]{2,1,0:T(8,128)S(1)} %get-tuple-element.56.v, f32[16,4,32,512]{3,2,1,0:T(8,128)S(1)} %get-tuple-element.72.s), custom_call_target="tpu_custom_call" | custom-call | bytes 4767744 | tf_op jit(solution)/shard_map/pallas_call | solution.py:32
  45.2 0.8 %shard_map.95 = (f32[4,32,512]{2,1,0:T(8,128)}, f32[1,18]{1,0:T(1,128)}) custom-call(f32[1,128]{1,0:T(1,128)S(1)} %get-tuple-element.80.row, f32[4,32,512]{2,1,0:T(8,128)S(1)} %get-tuple-element.76.orthogonal), custom_call_target="tpu_custom_call" | custom-call | bytes 262656 | tf_op jit(solution)/shard_map/pallas_call | solution.py:32
  (3 shorter events, 0.1 us)
Async XLA Ops:
  2.9 14.3 %collective-permute-start.2 = (f32[5,32,512]{2,1,0:T(8,128)S(1)}, f32[5,32,512]{2,1,0:T(8,128)S(1)}, u32[]{:S(2)}, u32[]{:S(2)}) collective-permute-start(f32[5,32,512]{2,1,0:T(8,128)S(1)} %get-tuple-element.57), channel_id=1, source_target_pairs={{0,1},{1,0},{2,3},{3,2},{4,5},{5,4},{6,7},{7,6},{8,9},{9,8},{10,11... | collective-permute-start | bytes 983048 | tf_op jit(solution)/shard_map/ppermute | solution.py:516
  3.4 13.8 %collective-permute-start.3 = (f32[5,32,512]{2,1,0:T(8,128)S(1)}, f32[5,32,512]{2,1,0:T(8,128)S(1)}, u32[]{:S(2)}, u32[]{:S(2)}) collective-permute-start(f32[5,32,512]{2,1,0:T(8,128)S(1)} %get-tuple-element.58), channel_id=1, source_target_pairs={{0,3},{1,2},{2,1},{3,0},{4,7},{5,6},{6,5},{7,4},{8,11},{9,10},{10,... | collective-permute-start | bytes 983048 | tf_op jit(solution)/shard_map/ppermute | solution.py:516
  6.0 9.6 %collective-permute-start = (f32[80,512]{1,0:T(8,128)}, f32[80,512]{1,0:T(8,128)S(1)}, u32[]{:S(2)}, u32[]{:S(2)}) collective-permute-start(f32[80,512]{1,0:T(8,128)} %get-tuple-element.54), channel_id=1, source_target_pairs={{0,4},{4,8},{8,12},{12,16},{16,20},{20,24},{24,28},{28,0},{1,5},{5... | collective-permute-start | bytes 491528 | tf_op jit(solution)/shard_map/ppermute | solution.py:515
  7.6 9.6 %collective-permute-start.1 = (f32[80,512]{1,0:T(8,128)}, f32[80,512]{1,0:T(8,128)S(1)}, u32[]{:S(2)}, u32[]{:S(2)}) collective-permute-start(f32[80,512]{1,0:T(8,128)} %get-tuple-element.55), channel_id=1, source_target_pairs={{4,0},{8,4},{12,8},{16,12},{20,16},{24,20},{28,24},{0,28},{5,1},{9... | collective-permute-start | bytes 491528 | tf_op jit(solution)/shard_map/ppermute | solution.py:515
  10.8 4.8 %collective-permute-start.4 = (f32[1,128]{1,0:T(1,128)S(1)}, f32[1,128]{1,0:T(1,128)S(1)}, u32[]{:S(2)}, u32[]{:S(2)}) collective-permute-start(f32[1,128]{1,0:T(1,128)S(1)} %get-tuple-element.64.order.counts), channel_id=1, source_target_pairs={{8,0},{12,4},{16,8},{20,12},{24,16},{28,20},{0,24},{4,28},{9,1},{1... | collective-permute-start | bytes 1544 | tf_op jit(solution)/shard_map/ppermute | solution.py:517
  13.2 8.9 %copy-start = (f32[4]{0:T(128)S(1)}, f32[4]{0:T(128)}, u32[]{:S(2)}) copy-start(f32[4]{0:T(128)} %lw.1) | copy-start | bytes 52
  17.2 4.9 %collective-permute-start.5 = (f32[5,8,512]{2,1,0:T(8,128)S(1)}, f32[5,8,512]{2,1,0:T(8,128)S(1)}, u32[]{:S(2)}, u32[]{:S(2)}) collective-permute-start(f32[5,8,512]{2,1,0:T(8,128)S(1)} %get-tuple-element.66), channel_id=1, source_target_pairs={{0,1},{1,0},{2,3},{3,2},{4,5},{5,4},{6,7},{7,6},{8,9},{9,8},{10,11... | collective-permute-start | bytes 245768 | tf_op jit(solution)/shard_map/ppermute | solution.py:511
  17.3 4.8 %collective-permute-start.6 = (f32[5,8,512]{2,1,0:T(8,128)S(1)}, f32[5,8,512]{2,1,0:T(8,128)S(1)}, u32[]{:S(2)}, u32[]{:S(2)}) collective-permute-start(f32[5,8,512]{2,1,0:T(8,128)S(1)} %get-tuple-element.67), channel_id=1, source_target_pairs={{0,4},{1,2},{2,1},{3,7},{4,0},{5,6},{6,5},{7,3},{8,12},{9,10},{10,... | collective-permute-start | bytes 245768 | tf_op jit(solution)/shard_map/ppermute | solution.py:511
  17.7 4.5 %collective-permute-start.7 = (f32[1,128]{1,0:T(1,128)S(1)}, f32[1,128]{1,0:T(1,128)S(1)}, u32[]{:S(2)}, u32[]{:S(2)}) collective-permute-start(f32[1,128]{1,0:T(1,128)S(1)} %shard_map.89.window.refs_0_), channel_id=1, source_target_pairs={{0,16},{4,20},{8,24},{12,28},{16,0},{20,4},{24,8},{28,12},{1,17},{... | collective-permute-start | bytes 1544 | tf_op jit(solution)/shard_map/ppermute | solution.py:526
  25.3 5.6 %collective-permute-start.9 = (f32[2,32,512]{2,1,0:T(8,128)S(1)}, f32[2,32,512]{2,1,0:T(8,128)S(1)}, u32[]{:S(2)}, u32[]{:S(2)}) collective-permute-start(f32[2,32,512]{2,1,0:T(8,128)S(1)} %get-tuple-element.70), channel_id=1, source_target_pairs={{0,4},{1,2},{2,1},{3,7},{4,0},{5,6},{6,5},{7,3},{8,12},{9,10},{10,... | collective-permute-start | bytes 393224 | tf_op jit(solution)/shard_map/ppermute | solution.py:511
  27.1 3.8 %collective-permute-start.8 = (f32[2,32,512]{2,1,0:T(8,128)S(1)}, f32[2,32,512]{2,1,0:T(8,128)S(1)}, u32[]{:S(2)}, u32[]{:S(2)}) collective-permute-start(f32[2,32,512]{2,1,0:T(8,128)S(1)} %get-tuple-element.69.order), channel_id=1, source_target_pairs={{0,1},{1,0},{2,3},{3,2},{4,5},{5,4},{6,7},{7,6},{8,9},{9,8},{10,11... | collective-permute-start | bytes 393224 | tf_op jit(solution)/shard_map/ppermute | solution.py:511

commit v6 on v5

--- a/solution.py
+++ b/solution.py
@@ -27,7 +27,7 @@
     return jax.ShapeDtypeStruct(shape, f32)
 
 
-def call(kernel, outs, operands, specs=None, scratch=(), flops=0, alias=None, out_specs=None):
+def call(kernel, outs, operands, specs=None, scratch=(), flops=0, alias=None, out_specs=None, mib=4):
     nbytes = sum(4 * x.size for x in operands)
     return pl.pallas_call(
         kernel,
@@ -36,7 +36,7 @@
         out_specs=out_specs or jax.tree.map(lambda _: VM, outs),
         scratch_shapes=list(scratch),
         input_output_aliases=alias or {},
-        compiler_params=pltpu.CompilerParams(vmem_limit_bytes=16 << 20),
+        compiler_params=pltpu.CompilerParams(vmem_limit_bytes=mib << 20),
         cost_estimate=pl.CostEstimate(flops=flops, bytes_accessed=nbytes, transcendentals=0),
     )(*operands)
 
@@ -105,7 +105,7 @@
     return jnp.concatenate([x for x in parts if x.shape[0]], axis=0)
 
 
-def corner_kernel(levels, west, east, window, lev_a, lev_b, corner_a, corner_b):
+def corner_kernel(levels, west, east, window, corner_a, corner_b):
     even = even_level()
 
     def put(item, top, bottom):
@@ -121,7 +121,7 @@
         put(2 + comp, *both(A_ROWS, V_ROWS + comp * A_ROWS))
 
 
-def window_kernel(levels, west, east, counts, counts_2, order, window):
+def window_kernel(levels, west, east, counts, counts_2, order, after, window):
     at = levels * LEVEL_ROWS + B_ROWS
     window[...] = counts[...] + counts_2[...] + west[at : at + 1, 0:128] + east[at : at + 1, 0:128]
 
@@ -177,6 +177,11 @@
         drift = a * (w - e) + b * (s - n) + c * (d - u)
         return centre * here + kappa * around + 0.5 * drift
 
+    def first_beyond(self, vv, la, ff, k):
+        for side, at in ((0, 0), (1, self.levels + 1)):
+            value = self.tangent(vv, at + 1, k, [la[side, comp, tile(k)] for comp in range(3)])
+            self.put_both(ff, at, k, jnp.where(self.has[side], value, 0.0))
+
     def push(self, x, abc, dst, at, k):
         inside, to_e, to_w, to_u, to_d = dst
         a, b, c = abc
@@ -197,43 +202,71 @@
     return slice(CHUNK * k, CHUNK * (k + 1))
 
 
-def first_kernel(levels, cols, lat, v, vel, west, east, lev_a, lev_b, vv, la, ff, halo_a, halo_b):
+def lev_kernel(levels, cols, lat, lev_a, lev_b, vv, la):
     block = Block(levels, cols, lat)
     for k in range(block.chunks):
         block.beyond(lev_a, lev_b, tile(k), k, vv, la)
-    for k in range(block.chunks + 1):
-        for lev in range(levels):
-            value = v[lev, tile(k)] if k < block.chunks else unpack(west, east, V_ROWS, lev * LEVEL_ROWS)
-            block.put_both(vv, lev + 2, k, value)
-
+
+
+def first_kernel(levels, cols, lat, v, vel, west, east, vv_in, la, vv, ff, xx, halo_a, halo_b):
+    block = Block(levels, cols, lat)
+    last = block.chunks
     for lev in range(levels):
+        for k in range(last):
+            block.put_both(vv, lev + 2, k, v[lev, tile(k)])
+        block.put_both(vv, lev + 2, last, unpack(west, east, V_ROWS, lev * LEVEL_ROWS))
         for comp in range(3):
             base = lev * LEVEL_ROWS + V_ROWS
             halo_a[comp, lev] = unpack(west, east, A_ROWS, base + comp * A_ROWS)
             halo_b[comp, lev] = unpack(west, east, B_ROWS, base + 3 * A_ROWS + comp * B_ROWS)
 
+    def flow(section, lev, k):
+        return [vel[section, comp, lev, tile(k)] for comp in range(3)]
+
     def first_level(lev, carry):
-        for k in range(block.chunks):
-            abc = [vel[0, comp, lev, tile(k)] for comp in range(3)]
-            block.put_both(ff, lev + 1, k, block.tangent(vv, lev + 2, k, abc))
+        for k in range(last):
+            block.put_both(ff, lev + 1, k, block.tangent(vv, lev + 2, k, flow(0, lev, k)))
         return carry
 
     lax.fori_loop(0, levels, first_level, 0)
+    for k in range(1, last - 1):
+        block.first_beyond(vv, la, ff, k)
+
+    def inner_level(lev, carry):
+        abc = [halo_a[comp, lev] for comp in range(3)]
+        block.put_both(ff, lev + 1, last, block.tangent(vv, lev + 2, last, abc))
+        for k in range(last):
+            xx[lev, tile(k)] = block.tangent(ff, lev + 1, k, flow(1, lev, k))
+        return carry
+
+    lax.fori_loop(1, levels - 1, inner_level, 0)
+
+
+def edge_kernel(levels, cols, lat, vel, halo_a, halo_b, corner_a, corner_b, vv_in, la_in, ff_in, xx_in, vv, la, ff, xx):
+    block = Block(levels, cols, lat)
+    last = block.chunks
+    block.beyond(corner_a, corner_b, slice(0, CHUNK), last, vv, la)
+    for k in (0, last - 1, last):
+        block.first_beyond(vv, la, ff, k)
+    for lev in (0, levels - 1):
+        abc = [halo_a[comp, lev] for comp in range(3)]
+        block.put_both(ff, lev + 1, last, block.tangent(vv, lev + 2, last, abc))
+    for lev in range(levels):
+        if lev in (0, levels - 1):
+            for k in range(last):
+                abc = [vel[1, comp, lev, tile(k)] for comp in range(3)]
+                xx[lev, tile(k)] = block.tangent(ff, lev + 1, k, abc)
+        xx[lev, tile(last)] = block.tangent(ff, lev + 1, last, [halo_b[comp, lev] for comp in range(3)])
 
 
 def stencil_kernel(
-    levels, cols, lat, columns, n_counts,
-    lw, vel, owner, west, east, halo_a, halo_b,
-    vv_in, la_in, ff_in, corner_a, corner_b, *refs,
+    levels, cols, lat, columns, n_counts, lw, vel, owner, west, east, halo_a, halo_b, la, xx, *refs
 ):
     count_refs = refs[:n_counts]
-    applied, send_a, send_b, vv, la, ff = refs[n_counts : n_counts + 6]
-    (own_h, w_in, w_e, w_w, w_u, w_d, u_in, u_e, u_w, u_u, u_d, out) = refs[n_counts + 6 :]
+    applied, send_a, send_b = refs[n_counts : n_counts + 3]
+    (own_h, w_in, w_e, w_w, w_u, w_d, u_in, u_e, u_w, u_u, u_d, out) = refs[n_counts + 3 :]
     block = Block(levels, cols, lat)
-    chunks, has, even = block.chunks, block.has, block.even
-    tangent, push, put_both = block.tangent, block.push, block.put_both
-
-    block.beyond(corner_a, corner_b, slice(0, CHUNK), chunks, vv, la)
+    chunks, has, even, push = block.chunks, block.has, block.even, block.push
     own_h[...] = unpack(west, east, B_ROWS, levels * LEVEL_ROWS)
 
     def flow(section, k, lev):
@@ -243,17 +276,6 @@
 
     def flow_beyond(side, k):
         return [la[side, comp, tile(k)] for comp in range(3)]
-
-    for k in range(chunks + 1):
-        for side, at in ((0, 0), (1, levels + 1)):
-            value = tangent(vv, at + 1, k, flow_beyond(side, k))
-            put_both(ff, at, k, jnp.where(has[side], value, 0.0))
-
-    def first_level(lev, carry):
-        put_both(ff, lev + 1, chunks, tangent(vv, lev + 2, chunks, flow(0, chunks, lev)))
-        return carry
-
-    lax.fori_loop(0, levels, first_level, 0)
 
     total = count_refs[0][...]
     for ref in count_refs[1:]:
@@ -270,8 +292,7 @@
         weight = lw[lev]
         for k in range(chunks + 1):
             abc = flow(1, k, lev)
-            x = tangent(ff, lev + 1, k, abc)
-            x = (weight * out[0, CHUNK * k : CHUNK * (k + 1)]) * x
+            x = (weight * out[0, tile(k)]) * xx[lev, tile(k)]
             push(x, abc, (w_in, w_e, w_w, w_u, w_d), lev + 1, k)
         return carry
 
@@ -409,7 +430,7 @@
             )
         return acc
 
-    acc = lax.fori_loop(0, steps, body, tuple(jnp.zeros((CHUNK, 128), f32) for _ in range(nvec + 2)), unroll=2)
+    acc = lax.fori_loop(0, steps, body, tuple(jnp.zeros((CHUNK, 128), f32) for _ in range(nvec + 2)), unroll=4)
     for i in range(nvec):
         put_sum(sums, i, acc[i])
     put_sum(sums, 2 * nvec, acc[nvec])
@@ -454,18 +475,14 @@
     a_w = jnp.broadcast_to(alpha, (CHUNK, 128))
     weights = [jnp.broadcast_to(x, (CHUNK, 128)) for x in p]
 
-    def body(step, carry):
-        lev = step // (cols // CHUNK)
-        at = pl.ds(pl.multiple_of((step - lev * (cols // CHUNK)) * CHUNK, CHUNK), CHUNK)
-        for t in tiles(lat):
-            x = applied[lev, at, t] - a_w * v[lev, at, t]
-            y = weights[0] * s[0, lev, at, t]
-            for k in range(1, nvec):
-                y = y + weights[k] * s[k, lev, at, t]
-            orthogonal[lev, at, t] = x - y
-        return carry
-
-    lax.fori_loop(0, levels * (cols // CHUNK), body, 0)
+    for lev in range(levels):
+        for k in range(cols // CHUNK):
+            for t in tiles(lat):
+                x = applied[lev, tile(k), t] - a_w * v[lev, tile(k), t]
+                y = [weights[k0] * s[k0, lev, tile(k), t] for k0 in range(nvec)]
+                while len(y) > 1:
+                    y = [a + b for a, b in zip(y[::2], y[1::2])] + y[len(y) & ~1 :]
+                orthogonal[lev, tile(k), t] = x - y[0]
 
 
 def scale_kernel(nvec, row, orthogonal, result_out, coefs_out, result, coefs, sems):
@@ -521,35 +538,43 @@
         (beta_prev.reshape(1), in_hbm(s), in_hbm(prev), counts), specs=[SM, HBM, HBM, VM],
         scratch=[pltpu.SemaphoreType.DMA((nvec + 1,))],
     )
-    window = call(functools.partial(window_kernel, levels), sds(1, 128), (west, east, counts, counts_2, beta_row))
+    padded = cols + 3 * CHUNK
+    vv, la = call(
+        functools.partial(lev_kernel, levels, cols, lat),
+        (sds(levels + 4, padded, lat), sds(2, 3, cols + CHUNK, lat)), (lev_a, lev_b),
+    )
+    window = call(
+        functools.partial(window_kernel, levels), sds(1, 128), (west, east, counts, counts_2, beta_row, la)
+    )
     if lon_n == 8:
         near = [window, lax.ppermute(window, "lon", [(i, i ^ 4) for i in range(lon_n)])]
     else:
         near = [lax.psum(counts, "lon")]
     corner_a, corner_b = call(
         functools.partial(corner_kernel, levels),
-        (sds(5, CHUNK, lat), sds(5, CHUNK, lat)), (west, east, window, lev_a, lev_b),
+        (sds(5, CHUNK, lat), sds(5, CHUNK, lat)), (west, east, window),
     )
     corner_a, corner_b = both(corner_a, corner_b)
 
-    padded = cols + 3 * CHUNK
-    state = (sds(levels + 4, padded, lat), sds(2, 3, cols + CHUNK, lat), sds(levels + 2, padded, lat))
-    halo = (sds(3, levels, CHUNK, lat), sds(3, levels, CHUNK, lat))
-    *state, halo_a, halo_b = call(
-        functools.partial(first_kernel, levels, cols, lat), (*state, *halo), (v, vel, west, east, lev_a, lev_b),
-        flops=4 << 20,
+    vv, ff, xx, halo_a, halo_b = call(
+        functools.partial(first_kernel, levels, cols, lat),
+        (sds(*vv.shape), sds(levels + 2, padded, lat), sds(levels, cols + CHUNK, lat),
+         sds(3, levels, CHUNK, lat), sds(3, levels, CHUNK, lat)),
+        (v, vel, west, east, vv, la), alias={4: 0}, flops=4 << 20,
+    )
+    vv, la, ff, xx = call(
+        functools.partial(edge_kernel, levels, cols, lat), tuple(sds(*x.shape) for x in (vv, la, ff, xx)),
+        (vel, halo_a, halo_b, corner_a, corner_b, vv, la, ff, xx), alias={5: 0, 6: 1, 7: 2, 8: 3}, flops=2 << 20,
     )
     scratch = [pltpu.VMEM((CHUNK, lat), f32)]
     scratch += [pltpu.VMEM((levels + 2, padded, lat), f32)] * 10
     scratch += [pltpu.VMEM((levels + 4, cols + CHUNK, lat), f32)]
-    operands = (lw, vel, owner, west, east, halo_a, halo_b, *state,
-                corner_a, corner_b, *near)
+    operands = (lw, vel, owner, west, east, halo_a, halo_b, la, xx, *near)
     part, send_a, send_b = call(
         functools.partial(stencil_kernel, levels, cols, lat, float(cols * lon_n * lat), len(near)),
-        (sds(levels, cols, lat), sds(SECOND, cols, lat), sds(SECOND, cols, lat), *(sds(*x.shape) for x in state)),
-        operands, specs=[SM] + [VM] * (len(operands) - 1), scratch=scratch, flops=8 << 20,
-        alias={7: 3, 8: 4, 9: 5},
-    )[:3]
+        (sds(levels, cols, lat), sds(SECOND, cols, lat), sds(SECOND, cols, lat)),
+        operands, specs=[SM] + [VM] * (len(operands) - 1), scratch=scratch, flops=8 << 20, mib=12,
+    )
     got_a, got_b = both(send_a, send_b)
     gram_rows = nvec * nvec // 128 + 1
     gram = call(

time: 46.2 us -> 44.9 us (0.972)
  waiting for transfers between devices: 2.72 us -> 1.94 us
  Pallas kernels: 15.2 us -> 14.6 us
    ppermute x1, waiting for transfers between devices: 1.15 us -> 0.01 us  [body(): lax.ppermute(window, 'lon', [(i, i ^ 4) for i in range(lon_n)])]
    pallas_call x10 -> x12, Pallas kernels: 15.2 us -> 14.6 us  [call(): pl.pallas_call(kernel, out_shape=outs, in_specs=specs or [VM] * len(opera...]
  transfers between devices with their start and end apart: 10 -> 10, of which waited for: 2 -> 2; matrix products, arithmetic and copies ran while one was open for 0% -> 0% of each run, Pallas kernels for 15% -> 17%
where the time goes in v6:
time: 44.9 us; the launch traced here: 44.8 us
  Pallas kernels  14.6 us (33%)
  starting transfers between devices  14.4 us (32%)
  blocking collectives  11.8 us (26%)
  between operations  2.09 us (5%)
  waiting for transfers between devices  1.94 us (4%)
    pallas_call x12, Pallas kernels, call(): pl.pallas_call(kernel, out_shape=outs, in_specs=specs or [VM] * len(opera...  14.6 us
    all_to_all x1, blocking collectives, body(): msg = lax.all_to_all(msg, ('lon', 'lev'), 0, 0, tiled=True)  11.8 us
    ppermute x1, starting transfers between devices, body(): lax.ppermute(lo, 'lon', west_of)  3.2 us
    ppermute x1, starting transfers between devices, body(): lax.ppermute(lev_b, 'lev', around)  2.61 us
    ppermute x1, starting transfers between devices, body(): lax.ppermute(window, 'lon', [(i, i ^ 4) for i in range(lon_n)])  2.59 us
    ppermute x2, starting transfers between devices, both(): lax.ppermute(b, ('lon', 'lev'), pairs_b)  1.82 us
    ppermute x1, starting transfers between devices, body(): lax.ppermute(counts, 'lon', [((i + 2) % lon_n, i) for i in range(lon_n)])  1.8 us
    ppermute x1, starting transfers between devices, body(): lax.ppermute(hi, 'lon', east_of)  1.52 us
  transfers between devices with their start and end apart: 10, of which 2 were waited for; matrix products, arithmetic and copies ran while one was open for 0% of the time, Pallas kernels for 17%

profile of v6, /device:TPU:0, one launch (start us, length us, event | category | flops | bytes accessed | tf_op | source)
XLA Modules:
  0.0 44.8 jit_solution(11302745790558674306)
XLA Ops:
  0.6 2.3 %shard_map.86 = (f32[80,512]{1,0:T(8,128)}, f32[80,512]{1,0:T(8,128)}, f32[5,32,512]{2,1,0:T(8,128)S(1)}, f32[5,32,512]{2,1,0:T(8,128)S(1)}, f32[1,128]{1,0:T(1,...) custom-call(f32[4,32,512]{2,1,0:T(8,128)} %v_hbm.1, ...), custom_call_target="tpu_custom_call" | custom-call | flops 1048576 | bytes 1900544 | tf_op jit(solution)/shard_map/pallas_call | solution.py:32
  2.9 0.5 %collective-permute-start.2 = (f32[5,32,512]{2,1,0:T(8,128)S(1)}, f32[5,32,512]{2,1,0:T(8,128)S(1)}, u32[]{:S(2)}, u32[]{:S(2)}) collective-permute-start(f32[5,32,512]{2,1,0:T(8,128)S(1)} %get-tuple-element.61), channel_id=1, source_target_pairs={{0,1},{1,0},{2,3},{3,2},{4,5},{5,4},{6,7},{7,6},{8,9},{9,8},{10,11... | collective-permute-start | bytes 983048 | tf_op jit(solution)/shard_map/ppermute | solution.py:533
  3.4 2.6 %collective-permute-start.3 = (f32[5,32,512]{2,1,0:T(8,128)S(1)}, f32[5,32,512]{2,1,0:T(8,128)S(1)}, u32[]{:S(2)}, u32[]{:S(2)}) collective-permute-start(f32[5,32,512]{2,1,0:T(8,128)S(1)} %get-tuple-element.62), channel_id=1, source_target_pairs={{0,3},{1,2},{2,1},{3,0},{4,7},{5,6},{6,5},{7,4},{8,11},{9,10},{10,... | collective-permute-start | bytes 983048 | tf_op jit(solution)/shard_map/ppermute | solution.py:533
  6.0 1.5 %collective-permute-start = (f32[80,512]{1,0:T(8,128)}, f32[80,512]{1,0:T(8,128)S(1)}, u32[]{:S(2)}, u32[]{:S(2)}) collective-permute-start(f32[80,512]{1,0:T(8,128)} %get-tuple-element.58), channel_id=1, source_target_pairs={{0,4},{4,8},{8,12},{12,16},{16,20},{20,24},{24,28},{28,0},{1,5},{5... | collective-permute-start | bytes 491528 | tf_op jit(solution)/shard_map/ppermute | solution.py:532
  7.5 3.2 %collective-permute-start.1 = (f32[80,512]{1,0:T(8,128)}, f32[80,512]{1,0:T(8,128)S(1)}, u32[]{:S(2)}, u32[]{:S(2)}) collective-permute-start(f32[80,512]{1,0:T(8,128)} %get-tuple-element.59), channel_id=1, source_target_pairs={{4,0},{8,4},{12,8},{16,12},{20,16},{24,20},{28,24},{0,28},{5,1},{9... | collective-permute-start | bytes 491528 | tf_op jit(solution)/shard_map/ppermute | solution.py:532
  10.8 1.8 %collective-permute-start.4 = (f32[1,128]{1,0:T(1,128)S(1)}, f32[1,128]{1,0:T(1,128)S(1)}, u32[]{:S(2)}, u32[]{:S(2)}) collective-permute-start(f32[1,128]{1,0:T(1,128)S(1)} %get-tuple-element.67.order.counts), channel_id=1, source_target_pairs={{8,0},{12,4},{16,8},{20,12},{24,16},{28,20},{0,24},{4,28},{9,1},{1... | collective-permute-start | bytes 1544 | tf_op jit(solution)/shard_map/ppermute | solution.py:534
  13.2 2.4 %shard_map.89 = (f32[1,128]{1,0:T(1,128)S(1)}, f32[16,4,32,512]{3,2,1,0:T(8,128)S(1)}, f32[4,32,512]{2,1,0:T(8,128)S(1)}) custom-call(f32[1]{0:T(128)} %bitcast.6.beta_prev, f32[16,4,32,512]{3,2,1,0:T(8,128)} %s_hbm.1, f32[4,32,512]{2,1,0:T(8,128)} %prev_hbm.1, f32[1,128]{1,0:T(1,128)S(1)} %get-tuple-element.67.order.counts), custom_call_target="tpu_custom_call" | custom-call | bytes 4456964 | tf_op jit(solution)/shard_map/pallas_call | solution.py:32
  15.6 0.0 collective-permute-done.2.lev_a
  15.6 0.0 collective-permute-done.3.lev_b
  15.6 0.1 shard_map.87
  15.7 0.0 collective-permute-done.4.counts_2
  15.7 0.0 collective-permute-done.west
  15.7 1.5 %collective-permute-done.1.east = f32[80,512]{1,0:T(8,128)S(1)} collective-permute-done((f32[80,512]{1,0:T(8,128)}, f32[80,512]{1,0:T(8,128)S(1)}, u32[]{:S(2)}, u32[]{:S(2)}) %collective-permute-start.1) | collective-permute-done | bytes 163872 | tf_op jit(solution)/shard_map/ppermute | solution.py:532
  17.2 0.1 collective-permute-start.5
  17.3 0.4 collective-permute-start.6
  17.6 2.6 %collective-permute-start.7 = (f32[1,128]{1,0:T(1,128)S(1)}, f32[1,128]{1,0:T(1,128)S(1)}, u32[]{:S(2)}, u32[]{:S(2)}) collective-permute-start(f32[1,128]{1,0:T(1,128)S(1)} %shard_map.90.window.refs_0_), channel_id=1, source_target_pairs={{0,16},{4,20},{8,24},{12,28},{16,0},{20,4},{24,8},{28,12},{1,17},{... | collective-permute-start | bytes 1544 | tf_op jit(solution)/shard_map/ppermute | solution.py:550
  20.2 1.1 %shard_map.88 = (f32[8,56,512]{2,1,0:T(8,128)S(1)}, f32[6,56,512]{2,1,0:T(8,128)S(1)}, f32[4,40,512]{2,1,0:T(8,128)S(1)}, f32[3,4,8,512]{3,2,1,0:T(8,128)S(1)}, f32[3,4,8,512]{3,2,1,0:T(8,128)S(1)}) custom-call(f32[4,32,512]{2,1,0:T(8,128)S(1)} %get-tuple-element.60.v, ...), custom_call_target="tpu_custom_call", output_to_operand_aliasing={{0}: (4, {})} | custom-call | flops 4194304 | bytes 3571712 | tf_op jit(solution)/shard_map/pallas_call | solution.py:32
  21.3 0.0 collective-permute-done.5.corner_a
  21.3 0.5 %collective-permute-done.6.corner_b = f32[5,8,512]{2,1,0:T(8,128)S(1)} collective-permute-done((f32[5,8,512]{2,1,0:T(8,128)S(1)}, f32[5,8,512]{2,1,0:T(8,128)S(1)}, u32[]{:S(2)}, u32[]{:S(2)}) %collective-permute-start.6) | collective-permute-done | bytes 81952 | tf_op jit(solution)/shard_map/ppermute | solution.py:528
  21.8 0.5 %shard_map.92 = (f32[8,56,512]{2,1,0:T(8,128)S(1)}, f32[2,3,40,512]{3,2,1,0:T(8,128)S(1)}, f32[6,56,512]{2,1,0:T(8,128)S(1)}, f32[4,40,512]{2,1,0:T(8,128)S(1)}) custom-call(f32[2,3,4,32,512]{4,3,2,1,0:T(8,128)S(1)} %get-tuple-element.56.vel, ...), custom_call_target="tpu_custom_call", output_to_operand_aliasing={{0}: (5, {}), {1}: (6, {}), {2}: (7, {}), {3}: (8, {})} | custom-call | flops 2097152 | bytes 4554752 | tf_op jit(solution)/shard_map/pallas_call | solution.py:32
  22.3 0.0 collective-permute-done.7.refs_1_
  22.3 0.0 copy-done
  22.3 2.0 %shard_map.93 = (f32[4,32,512]{2,1,0:T(8,128)S(1)}, f32[2,32,512]{2,1,0:T(8,128)S(1)}, f32[2,32,512]{2,1,0:T(8,128)S(1)}) custom-call(f32[4]{0:T(128)S(1)} %copy-done, f32[2,3,4,32,512]{4,3,2,1,0:T(8,128)S(1)} %get-tuple-element.56.vel, s32[32,512]{1,0:T(8,128)S(1)} %get-tuple-element.57.owner, f32[80,512]{1,0:T(8,128)S(1)} %collective-permute-done.west, ...), custom_call_target="tpu_custom_call" | custom-call | flops 8388608 | bytes 3179536 | tf_op jit(solution)/shard_map/pallas_call | solution.py:32
  24.3 0.2 collective-permute-start.8
  24.5 1.5 %collective-permute-start.9 = (f32[2,32,512]{2,1,0:T(8,128)S(1)}, f32[2,32,512]{2,1,0:T(8,128)S(1)}, u32[]{:S(2)}, u32[]{:S(2)}) collective-permute-start(f32[2,32,512]{2,1,0:T(8,128)S(1)} %get-tuple-element.78), channel_id=1, source_target_pairs={{0,4},{1,2},{2,1},{3,7},{4,0},{5,6},{6,5},{7,3},{8,12},{9,10},{10,... | collective-permute-start | bytes 393224 | tf_op jit(solution)/shard_map/ppermute | solution.py:528
  25.9 3.6 %shard_map.94.gram = f32[3,128]{1,0:T(4,128)S(1)} custom-call(f32[16,4,32,512]{3,2,1,0:T(8,128)S(1)} %get-tuple-element.80.s, f32[4,32,512]{2,1,0:T(8,128)S(1)} %get-tuple-element.60.v, f32[2,32,512]{2,1,0:T(8,128)S(1)} %get-tuple-element.77.order), custom_call_target="tpu_custom_call" | custom-call | flops 20971520 | bytes 4587520 | tf_op jit(solution)/shard_map/pallas_call | solution.py:32
  29.5 0.0 collective-permute-done.8.got_a
  29.6 0.0 collective-permute-done.9.got_b
  29.6 0.6 %shard_map.95 = (f32[4,32,512]{2,1,0:T(8,128)S(1)}, f32[32,3,128]{2,1,0:T(4,128)S(1)}) custom-call(f32[4,32,512]{2,1,0:T(8,128)S(1)} %get-tuple-element.76.part, f32[2,32,512]{2,1,0:T(8,128)S(1)} %collective-permute-done.8.got_a, f32[2,32,512]{2,1,0:T(8,128)S(1)} %collective-permute-done.9.got_b, f32[4,32,512]{2,1,0:T(8,128)S(1)} %get-tuple-element.79.prev, ...), custom_call_target="tpu_custom_call" | custom-call | bytes 5244928 | tf_op jit(solution)/shard_map/pallas_call | solution.py:32
  30.2 11.8 %all_to_all.5.msg = f32[32,3,128]{2,1,0:T(4,128)S(1)} all-to-all(f32[32,3,128]{2,1,0:T(4,128)S(1)} %get-tuple-element.81), channel_id=1, replica_groups=mesh['lon'=8,'lev'=4] {'lon','lev'}, dimensions={0} | all-to-all | bytes 98304 | tf_op jit(solution)/shard_map/all_to_all | solution.py:591
  42.0 1.3 %shard_map.96 = (f32[4,32,512]{2,1,0:T(8,128)S(1)}, f32[1,128]{1,0:T(1,128)S(1)}, f32[1,1]{1,0:T(1,128)}) custom-call(f32[32,3,128]{2,1,0:T(4,128)S(1)} %all_to_all.5.msg, f32[4,32,512]{2,1,0:T(8,128)S(1)} %get-tuple-element.82.applied, f32[4,32,512]{2,1,0:T(8,128)S(1)} %get-tuple-element.60.v, f32[16,4,32,512]{3,2,1,0:T(8,128)S(1)} %get-tuple-element.80.s), custom_call_target="tpu_custom_call" | custom-call | bytes 4767744 | tf_op jit(solution)/shard_map/pallas_call | solution.py:32
  43.9 0.8 %shard_map.97 = (f32[4,32,512]{2,1,0:T(8,128)}, f32[1,18]{1,0:T(1,128)}) custom-call(f32[1,128]{1,0:T(1,128)S(1)} %get-tuple-element.88.row, f32[4,32,512]{2,1,0:T(8,128)S(1)} %get-tuple-element.84.orthogonal), custom_call_target="tpu_custom_call" | custom-call | bytes 262656 | tf_op jit(solution)/shard_map/pallas_call | solution.py:32
  (4 shorter events, 0.1 us)
Async XLA Ops:
  2.9 12.7 %collective-permute-start.2 = (f32[5,32,512]{2,1,0:T(8,128)S(1)}, f32[5,32,512]{2,1,0:T(8,128)S(1)}, u32[]{:S(2)}, u32[]{:S(2)}) collective-permute-start(f32[5,32,512]{2,1,0:T(8,128)S(1)} %get-tuple-element.61), channel_id=1, source_target_pairs={{0,1},{1,0},{2,3},{3,2},{4,5},{5,4},{6,7},{7,6},{8,9},{9,8},{10,11... | collective-permute-start | bytes 983048 | tf_op jit(solution)/shard_map/ppermute | solution.py:533
  3.4 12.2 %collective-permute-start.3 = (f32[5,32,512]{2,1,0:T(8,128)S(1)}, f32[5,32,512]{2,1,0:T(8,128)S(1)}, u32[]{:S(2)}, u32[]{:S(2)}) collective-permute-start(f32[5,32,512]{2,1,0:T(8,128)S(1)} %get-tuple-element.62), channel_id=1, source_target_pairs={{0,3},{1,2},{2,1},{3,0},{4,7},{5,6},{6,5},{7,4},{8,11},{9,10},{10,... | collective-permute-start | bytes 983048 | tf_op jit(solution)/shard_map/ppermute | solution.py:533
  6.0 9.7 %collective-permute-start = (f32[80,512]{1,0:T(8,128)}, f32[80,512]{1,0:T(8,128)S(1)}, u32[]{:S(2)}, u32[]{:S(2)}) collective-permute-start(f32[80,512]{1,0:T(8,128)} %get-tuple-element.58), channel_id=1, source_target_pairs={{0,4},{4,8},{8,12},{12,16},{16,20},{20,24},{24,28},{28,0},{1,5},{5... | collective-permute-start | bytes 491528 | tf_op jit(solution)/shard_map/ppermute | solution.py:532
  7.5 9.6 %collective-permute-start.1 = (f32[80,512]{1,0:T(8,128)}, f32[80,512]{1,0:T(8,128)S(1)}, u32[]{:S(2)}, u32[]{:S(2)}) collective-permute-start(f32[80,512]{1,0:T(8,128)} %get-tuple-element.59), channel_id=1, source_target_pairs={{4,0},{8,4},{12,8},{16,12},{20,16},{24,20},{28,24},{0,28},{5,1},{9... | collective-permute-start | bytes 491528 | tf_op jit(solution)/shard_map/ppermute | solution.py:532
  10.8 4.9 %collective-permute-start.4 = (f32[1,128]{1,0:T(1,128)S(1)}, f32[1,128]{1,0:T(1,128)S(1)}, u32[]{:S(2)}, u32[]{:S(2)}) collective-permute-start(f32[1,128]{1,0:T(1,128)S(1)} %get-tuple-element.67.order.counts), channel_id=1, source_target_pairs={{8,0},{12,4},{16,8},{20,12},{24,16},{28,20},{0,24},{4,28},{9,1},{1... | collective-permute-start | bytes 1544 | tf_op jit(solution)/shard_map/ppermute | solution.py:534
  17.2 5.1 %copy-start = (f32[4]{0:T(128)S(1)}, f32[4]{0:T(128)}, u32[]{:S(2)}) copy-start(f32[4]{0:T(128)} %lw.1) | copy-start | bytes 52
  17.2 4.1 %collective-permute-start.5 = (f32[5,8,512]{2,1,0:T(8,128)S(1)}, f32[5,8,512]{2,1,0:T(8,128)S(1)}, u32[]{:S(2)}, u32[]{:S(2)}) collective-permute-start(f32[5,8,512]{2,1,0:T(8,128)S(1)} %get-tuple-element.69), channel_id=1, source_target_pairs={{0,1},{1,0},{2,3},{3,2},{4,5},{5,4},{6,7},{7,6},{8,9},{9,8},{10,11... | collective-permute-start | bytes 245768 | tf_op jit(solution)/shard_map/ppermute | solution.py:528
  17.3 4.5 %collective-permute-start.6 = (f32[5,8,512]{2,1,0:T(8,128)S(1)}, f32[5,8,512]{2,1,0:T(8,128)S(1)}, u32[]{:S(2)}, u32[]{:S(2)}) collective-permute-start(f32[5,8,512]{2,1,0:T(8,128)S(1)} %get-tuple-element.70), channel_id=1, source_target_pairs={{0,4},{1,2},{2,1},{3,7},{4,0},{5,6},{6,5},{7,3},{8,12},{9,10},{10,... | collective-permute-start | bytes 245768 | tf_op jit(solution)/shard_map/ppermute | solution.py:528
  17.6 4.6 %collective-permute-start.7 = (f32[1,128]{1,0:T(1,128)S(1)}, f32[1,128]{1,0:T(1,128)S(1)}, u32[]{:S(2)}, u32[]{:S(2)}) collective-permute-start(f32[1,128]{1,0:T(1,128)S(1)} %shard_map.90.window.refs_0_), channel_id=1, source_target_pairs={{0,16},{4,20},{8,24},{12,28},{16,0},{20,4},{24,8},{28,12},{1,17},{... | collective-permute-start | bytes 1544 | tf_op jit(solution)/shard_map/ppermute | solution.py:550
  24.3 5.3 %collective-permute-start.8 = (f32[2,32,512]{2,1,0:T(8,128)S(1)}, f32[2,32,512]{2,1,0:T(8,128)S(1)}, u32[]{:S(2)}, u32[]{:S(2)}) collective-permute-start(f32[2,32,512]{2,1,0:T(8,128)S(1)} %get-tuple-element.77.order), channel_id=1, source_target_pairs={{0,1},{1,0},{2,3},{3,2},{4,5},{5,4},{6,7},{7,6},{8,9},{9,8},{10,11... | collective-permute-start | bytes 393224 | tf_op jit(solution)/shard_map/ppermute | solution.py:528
  24.5 5.1 %collective-permute-start.9 = (f32[2,32,512]{2,1,0:T(8,128)S(1)}, f32[2,32,512]{2,1,0:T(8,128)S(1)}, u32[]{:S(2)}, u32[]{:S(2)}) collective-permute-start(f32[2,32,512]{2,1,0:T(8,128)S(1)} %get-tuple-element.78), channel_id=1, source_target_pairs={{0,4},{1,2},{2,1},{3,7},{4,0},{5,6},{6,5},{7,3},{8,12},{9,10},{10,... | collective-permute-start | bytes 393224 | tf_op jit(solution)/shard_map/ppermute | solution.py:528

commit v7 on v6

--- a/solution.py
+++ b/solution.py
@@ -228,7 +228,7 @@
             block.put_both(ff, lev + 1, k, block.tangent(vv, lev + 2, k, flow(0, lev, k)))
         return carry
 
-    lax.fori_loop(0, levels, first_level, 0)
+    lax.fori_loop(0, levels, first_level, 0, unroll=True)
     for k in range(1, last - 1):
         block.first_beyond(vv, la, ff, k)
 
@@ -239,7 +239,7 @@
             xx[lev, tile(k)] = block.tangent(ff, lev + 1, k, flow(1, lev, k))
         return carry
 
-    lax.fori_loop(1, levels - 1, inner_level, 0)
+    lax.fori_loop(1, levels - 1, inner_level, 0, unroll=True)
 
 
 def edge_kernel(levels, cols, lat, vel, halo_a, halo_b, corner_a, corner_b, vv_in, la_in, ff_in, xx_in, vv, la, ff, xx):
@@ -296,7 +296,7 @@
             push(x, abc, (w_in, w_e, w_w, w_u, w_d), lev + 1, k)
         return carry
 
-    lax.fori_loop(0, levels, second_level, 0)
+    lax.fori_loop(0, levels, second_level, 0, unroll=True)
     for k in range(chunks + 1):
         w_u[0, rows(k)] = jnp.zeros((CHUNK, lat), f32)
         w_d[levels + 1, rows(k)] = jnp.zeros((CHUNK, lat), f32)
@@ -311,7 +311,7 @@
             push(x, flow(0, k, lev), (u_in, u_e, u_w, u_u, u_d), lev + 1, k)
         return carry
 
-    lax.fori_loop(0, levels, third_level, 0)
+    lax.fori_loop(0, levels, third_level, 0, unroll=True)
     for k in range(chunks + 1):
         for side, at, x in ((0, 0, w_d[1, rows(k)]), (1, levels + 1, w_u[levels, rows(k)])):
             x = jnp.where(has[side], x, 0.0)

time: 44.9 us -> 44.5 us (level)
  Pallas kernels: 14.6 us -> 13.8 us
    pallas_call x12, Pallas kernels: 14.6 us -> 13.8 us  [call(): pl.pallas_call(kernel, out_shape=outs, in_specs=specs or [VM] * len(opera...]
  transfers between devices with their start and end apart: 10 -> 10, of which waited for: 2 -> 2; matrix products, arithmetic and copies ran while one was open for 0% -> 0% of each run, Pallas kernels for 17% -> 16%
where the time goes in v7:
time: 44.5 us; the launch traced here: 44.3 us
  starting transfers between devices  14.4 us (32%)
  Pallas kernels  13.8 us (31%)
  blocking collectives  11.8 us (27%)
  waiting for transfers between devices  2.28 us (5%)
  between operations  2.08 us (5%)
    pallas_call x12, Pallas kernels, call(): pl.pallas_call(kernel, out_shape=outs, in_specs=specs or [VM] * len(opera...  13.8 us
    all_to_all x1, blocking collectives, body(): msg = lax.all_to_all(msg, ('lon', 'lev'), 0, 0, tiled=True)  11.8 us
    ppermute x1, starting transfers between devices, body(): lax.ppermute(lo, 'lon', west_of)  3.2 us
    ppermute x1, starting transfers between devices, body(): lax.ppermute(lev_b, 'lev', around)  2.61 us
    ppermute x1, starting transfers between devices, body(): lax.ppermute(window, 'lon', [(i, i ^ 4) for i in range(lon_n)])  2.59 us
    ppermute x2, starting transfers between devices, both(): lax.ppermute(b, ('lon', 'lev'), pairs_b)  1.82 us
    ppermute x1, starting transfers between devices, body(): lax.ppermute(counts, 'lon', [((i + 2) % lon_n, i) for i in range(lon_n)])  1.8 us
    ppermute x1, starting transfers between devices, body(): lax.ppermute(hi, 'lon', east_of)  1.52 us
  transfers between devices with their start and end apart: 10, of which 2 were waited for; matrix products, arithmetic and copies ran while one was open for 0% of the time, Pallas kernels for 16%

profile of v7, /device:TPU:0, one launch (start us, length us, event | category | flops | bytes accessed | tf_op | source)
XLA Modules:
  0.0 44.3 jit_solution(14545580250069968278)
XLA Ops:
  0.6 2.3 %shard_map.86 = (f32[80,512]{1,0:T(8,128)}, f32[80,512]{1,0:T(8,128)}, f32[5,32,512]{2,1,0:T(8,128)S(1)}, f32[5,32,512]{2,1,0:T(8,128)S(1)}, f32[1,128]{1,0:T(1,...) custom-call(f32[4,32,512]{2,1,0:T(8,128)} %v_hbm.1, ...), custom_call_target="tpu_custom_call" | custom-call | flops 1048576 | bytes 1900544 | tf_op jit(solution)/shard_map/pallas_call | solution.py:32
  2.9 0.5 %collective-permute-start.2 = (f32[5,32,512]{2,1,0:T(8,128)S(1)}, f32[5,32,512]{2,1,0:T(8,128)S(1)}, u32[]{:S(2)}, u32[]{:S(2)}) collective-permute-start(f32[5,32,512]{2,1,0:T(8,128)S(1)} %get-tuple-element.61), channel_id=1, source_target_pairs={{0,1},{1,0},{2,3},{3,2},{4,5},{5,4},{6,7},{7,6},{8,9},{9,8},{10,11... | collective-permute-start | bytes 983048 | tf_op jit(solution)/shard_map/ppermute | solution.py:533
  3.4 2.6 %collective-permute-start.3 = (f32[5,32,512]{2,1,0:T(8,128)S(1)}, f32[5,32,512]{2,1,0:T(8,128)S(1)}, u32[]{:S(2)}, u32[]{:S(2)}) collective-permute-start(f32[5,32,512]{2,1,0:T(8,128)S(1)} %get-tuple-element.62), channel_id=1, source_target_pairs={{0,3},{1,2},{2,1},{3,0},{4,7},{5,6},{6,5},{7,4},{8,11},{9,10},{10,... | collective-permute-start | bytes 983048 | tf_op jit(solution)/shard_map/ppermute | solution.py:533
  6.0 1.5 %collective-permute-start = (f32[80,512]{1,0:T(8,128)}, f32[80,512]{1,0:T(8,128)S(1)}, u32[]{:S(2)}, u32[]{:S(2)}) collective-permute-start(f32[80,512]{1,0:T(8,128)} %get-tuple-element.58), channel_id=1, source_target_pairs={{0,4},{4,8},{8,12},{12,16},{16,20},{20,24},{24,28},{28,0},{1,5},{5... | collective-permute-start | bytes 491528 | tf_op jit(solution)/shard_map/ppermute | solution.py:532
  7.5 3.2 %collective-permute-start.1 = (f32[80,512]{1,0:T(8,128)}, f32[80,512]{1,0:T(8,128)S(1)}, u32[]{:S(2)}, u32[]{:S(2)}) collective-permute-start(f32[80,512]{1,0:T(8,128)} %get-tuple-element.59), channel_id=1, source_target_pairs={{4,0},{8,4},{12,8},{16,12},{20,16},{24,20},{28,24},{0,28},{5,1},{9... | collective-permute-start | bytes 491528 | tf_op jit(solution)/shard_map/ppermute | solution.py:532
  10.8 1.8 %collective-permute-start.4 = (f32[1,128]{1,0:T(1,128)S(1)}, f32[1,128]{1,0:T(1,128)S(1)}, u32[]{:S(2)}, u32[]{:S(2)}) collective-permute-start(f32[1,128]{1,0:T(1,128)S(1)} %get-tuple-element.67.order.counts), channel_id=1, source_target_pairs={{8,0},{12,4},{16,8},{20,12},{24,16},{28,20},{0,24},{4,28},{9,1},{1... | collective-permute-start | bytes 1544 | tf_op jit(solution)/shard_map/ppermute | solution.py:534
  13.2 2.4 %shard_map.89 = (f32[1,128]{1,0:T(1,128)S(1)}, f32[16,4,32,512]{3,2,1,0:T(8,128)S(1)}, f32[4,32,512]{2,1,0:T(8,128)S(1)}) custom-call(f32[1]{0:T(128)} %bitcast.6.beta_prev, f32[16,4,32,512]{3,2,1,0:T(8,128)} %s_hbm.1, f32[4,32,512]{2,1,0:T(8,128)} %prev_hbm.1, f32[1,128]{1,0:T(1,128)S(1)} %get-tuple-element.67.order.counts), custom_call_target="tpu_custom_call" | custom-call | bytes 4456964 | tf_op jit(solution)/shard_map/pallas_call | solution.py:32
  15.6 0.0 collective-permute-done.2.lev_a
  15.6 0.0 collective-permute-done.3.lev_b
  15.6 0.1 shard_map.87
  15.7 0.0 collective-permute-done.4.counts_2
  15.7 0.0 collective-permute-done.west
  15.7 1.5 %collective-permute-done.1.east = f32[80,512]{1,0:T(8,128)S(1)} collective-permute-done((f32[80,512]{1,0:T(8,128)}, f32[80,512]{1,0:T(8,128)S(1)}, u32[]{:S(2)}, u32[]{:S(2)}) %collective-permute-start.1) | collective-permute-done | bytes 163872 | tf_op jit(solution)/shard_map/ppermute | solution.py:532
  17.2 0.1 collective-permute-start.5
  17.3 0.4 collective-permute-start.6
  17.6 2.6 %collective-permute-start.7 = (f32[1,128]{1,0:T(1,128)S(1)}, f32[1,128]{1,0:T(1,128)S(1)}, u32[]{:S(2)}, u32[]{:S(2)}) collective-permute-start(f32[1,128]{1,0:T(1,128)S(1)} %shard_map.90.window.refs_0_), channel_id=1, source_target_pairs={{0,16},{4,20},{8,24},{12,28},{16,0},{20,4},{24,8},{28,12},{1,17},{... | collective-permute-start | bytes 1544 | tf_op jit(solution)/shard_map/ppermute | solution.py:550
  20.2 0.8 %shard_map.88 = (f32[8,56,512]{2,1,0:T(8,128)S(1)}, f32[6,56,512]{2,1,0:T(8,128)S(1)}, f32[4,40,512]{2,1,0:T(8,128)S(1)}, f32[3,4,8,512]{3,2,1,0:T(8,128)S(1)}, f32[3,4,8,512]{3,2,1,0:T(8,128)S(1)}) custom-call(f32[4,32,512]{2,1,0:T(8,128)S(1)} %get-tuple-element.60.v, ...), custom_call_target="tpu_custom_call", output_to_operand_aliasing={{0}: (4, {})} | custom-call | flops 4194304 | bytes 3571712 | tf_op jit(solution)/shard_map/pallas_call | solution.py:32
  21.0 0.0 collective-permute-done.5.corner_a
  21.0 0.8 %collective-permute-done.6.corner_b = f32[5,8,512]{2,1,0:T(8,128)S(1)} collective-permute-done((f32[5,8,512]{2,1,0:T(8,128)S(1)}, f32[5,8,512]{2,1,0:T(8,128)S(1)}, u32[]{:S(2)}, u32[]{:S(2)}) %collective-permute-start.6) | collective-permute-done | bytes 81952 | tf_op jit(solution)/shard_map/ppermute | solution.py:528
  21.8 0.5 %shard_map.92 = (f32[8,56,512]{2,1,0:T(8,128)S(1)}, f32[2,3,40,512]{3,2,1,0:T(8,128)S(1)}, f32[6,56,512]{2,1,0:T(8,128)S(1)}, f32[4,40,512]{2,1,0:T(8,128)S(1)}) custom-call(f32[2,3,4,32,512]{4,3,2,1,0:T(8,128)S(1)} %get-tuple-element.56.vel, ...), custom_call_target="tpu_custom_call", output_to_operand_aliasing={{0}: (5, {}), {1}: (6, {}), {2}: (7, {}), {3}: (8, {})} | custom-call | flops 2097152 | bytes 4554752 | tf_op jit(solution)/shard_map/pallas_call | solution.py:32
  22.3 0.0 collective-permute-done.7.refs_1_
  22.3 0.0 copy-done
  22.3 1.5 %shard_map.93 = (f32[4,32,512]{2,1,0:T(8,128)S(1)}, f32[2,32,512]{2,1,0:T(8,128)S(1)}, f32[2,32,512]{2,1,0:T(8,128)S(1)}) custom-call(f32[4]{0:T(128)S(1)} %copy-done, f32[2,3,4,32,512]{4,3,2,1,0:T(8,128)S(1)} %get-tuple-element.56.vel, s32[32,512]{1,0:T(8,128)S(1)} %get-tuple-element.57.owner, f32[80,512]{1,0:T(8,128)S(1)} %collective-permute-done.west, ...), custom_call_target="tpu_custom_call" | custom-call | flops 8388608 | bytes 3179536 | tf_op jit(solution)/shard_map/pallas_call | solution.py:32
  23.8 0.2 collective-permute-start.8
  24.0 1.5 %collective-permute-start.9 = (f32[2,32,512]{2,1,0:T(8,128)S(1)}, f32[2,32,512]{2,1,0:T(8,128)S(1)}, u32[]{:S(2)}, u32[]{:S(2)}) collective-permute-start(f32[2,32,512]{2,1,0:T(8,128)S(1)} %get-tuple-element.78), channel_id=1, source_target_pairs={{0,4},{1,2},{2,1},{3,7},{4,0},{5,6},{6,5},{7,3},{8,12},{9,10},{10,... | collective-permute-start | bytes 393224 | tf_op jit(solution)/shard_map/ppermute | solution.py:528
  25.5 3.6 %shard_map.94.gram = f32[3,128]{1,0:T(4,128)S(1)} custom-call(f32[16,4,32,512]{3,2,1,0:T(8,128)S(1)} %get-tuple-element.80.s, f32[4,32,512]{2,1,0:T(8,128)S(1)} %get-tuple-element.60.v, f32[2,32,512]{2,1,0:T(8,128)S(1)} %get-tuple-element.77.order), custom_call_target="tpu_custom_call" | custom-call | flops 20971520 | bytes 4587520 | tf_op jit(solution)/shard_map/pallas_call | solution.py:32
  29.1 0.0 collective-permute-done.8.got_a
  29.1 0.0 collective-permute-done.9.got_b
  29.1 0.6 %shard_map.95 = (f32[4,32,512]{2,1,0:T(8,128)S(1)}, f32[32,3,128]{2,1,0:T(4,128)S(1)}) custom-call(f32[4,32,512]{2,1,0:T(8,128)S(1)} %get-tuple-element.76.part, f32[2,32,512]{2,1,0:T(8,128)S(1)} %collective-permute-done.8.got_a, f32[2,32,512]{2,1,0:T(8,128)S(1)} %collective-permute-done.9.got_b, f32[4,32,512]{2,1,0:T(8,128)S(1)} %get-tuple-element.79.prev, ...), custom_call_target="tpu_custom_call" | custom-call | bytes 5244928 | tf_op jit(solution)/shard_map/pallas_call | solution.py:32
  29.7 11.8 %all_to_all.5.msg = f32[32,3,128]{2,1,0:T(4,128)S(1)} all-to-all(f32[32,3,128]{2,1,0:T(4,128)S(1)} %get-tuple-element.81), channel_id=1, replica_groups=mesh['lon'=8,'lev'=4] {'lon','lev'}, dimensions={0} | all-to-all | bytes 98304 | tf_op jit(solution)/shard_map/all_to_all | solution.py:591
  41.5 1.3 %shard_map.96 = (f32[4,32,512]{2,1,0:T(8,128)S(1)}, f32[1,128]{1,0:T(1,128)S(1)}, f32[1,1]{1,0:T(1,128)}) custom-call(f32[32,3,128]{2,1,0:T(4,128)S(1)} %all_to_all.5.msg, f32[4,32,512]{2,1,0:T(8,128)S(1)} %get-tuple-element.82.applied, f32[4,32,512]{2,1,0:T(8,128)S(1)} %get-tuple-element.60.v, f32[16,4,32,512]{3,2,1,0:T(8,128)S(1)} %get-tuple-element.80.s), custom_call_target="tpu_custom_call" | custom-call | bytes 4767744 | tf_op jit(solution)/shard_map/pallas_call | solution.py:32
  43.5 0.8 %shard_map.97 = (f32[4,32,512]{2,1,0:T(8,128)}, f32[1,18]{1,0:T(1,128)}) custom-call(f32[1,128]{1,0:T(1,128)S(1)} %get-tuple-element.88.row, f32[4,32,512]{2,1,0:T(8,128)S(1)} %get-tuple-element.84.orthogonal), custom_call_target="tpu_custom_call" | custom-call | bytes 262656 | tf_op jit(solution)/shard_map/pallas_call | solution.py:32
  (4 shorter events, 0.1 us)
Async XLA Ops:
  2.9 12.7 %collective-permute-start.2 = (f32[5,32,512]{2,1,0:T(8,128)S(1)}, f32[5,32,512]{2,1,0:T(8,128)S(1)}, u32[]{:S(2)}, u32[]{:S(2)}) collective-permute-start(f32[5,32,512]{2,1,0:T(8,128)S(1)} %get-tuple-element.61), channel_id=1, source_target_pairs={{0,1},{1,0},{2,3},{3,2},{4,5},{5,4},{6,7},{7,6},{8,9},{9,8},{10,11... | collective-permute-start | bytes 983048 | tf_op jit(solution)/shard_map/ppermute | solution.py:533
  3.4 12.2 %collective-permute-start.3 = (f32[5,32,512]{2,1,0:T(8,128)S(1)}, f32[5,32,512]{2,1,0:T(8,128)S(1)}, u32[]{:S(2)}, u32[]{:S(2)}) collective-permute-start(f32[5,32,512]{2,1,0:T(8,128)S(1)} %get-tuple-element.62), channel_id=1, source_target_pairs={{0,3},{1,2},{2,1},{3,0},{4,7},{5,6},{6,5},{7,4},{8,11},{9,10},{10,... | collective-permute-start | bytes 983048 | tf_op jit(solution)/shard_map/ppermute | solution.py:533
  6.0 9.7 %collective-permute-start = (f32[80,512]{1,0:T(8,128)}, f32[80,512]{1,0:T(8,128)S(1)}, u32[]{:S(2)}, u32[]{:S(2)}) collective-permute-start(f32[80,512]{1,0:T(8,128)} %get-tuple-element.58), channel_id=1, source_target_pairs={{0,4},{4,8},{8,12},{12,16},{16,20},{20,24},{24,28},{28,0},{1,5},{5... | collective-permute-start | bytes 491528 | tf_op jit(solution)/shard_map/ppermute | solution.py:532
  7.5 9.6 %collective-permute-start.1 = (f32[80,512]{1,0:T(8,128)}, f32[80,512]{1,0:T(8,128)S(1)}, u32[]{:S(2)}, u32[]{:S(2)}) collective-permute-start(f32[80,512]{1,0:T(8,128)} %get-tuple-element.59), channel_id=1, source_target_pairs={{4,0},{8,4},{12,8},{16,12},{20,16},{24,20},{28,24},{0,28},{5,1},{9... | collective-permute-start | bytes 491528 | tf_op jit(solution)/shard_map/ppermute | solution.py:532
  10.8 4.9 %collective-permute-start.4 = (f32[1,128]{1,0:T(1,128)S(1)}, f32[1,128]{1,0:T(1,128)S(1)}, u32[]{:S(2)}, u32[]{:S(2)}) collective-permute-start(f32[1,128]{1,0:T(1,128)S(1)} %get-tuple-element.67.order.counts), channel_id=1, source_target_pairs={{8,0},{12,4},{16,8},{20,12},{24,16},{28,20},{0,24},{4,28},{9,1},{1... | collective-permute-start | bytes 1544 | tf_op jit(solution)/shard_map/ppermute | solution.py:534
  17.2 5.1 %copy-start = (f32[4]{0:T(128)S(1)}, f32[4]{0:T(128)}, u32[]{:S(2)}) copy-start(f32[4]{0:T(128)} %lw.1) | copy-start | bytes 52
  17.2 3.8 %collective-permute-start.5 = (f32[5,8,512]{2,1,0:T(8,128)S(1)}, f32[5,8,512]{2,1,0:T(8,128)S(1)}, u32[]{:S(2)}, u32[]{:S(2)}) collective-permute-start(f32[5,8,512]{2,1,0:T(8,128)S(1)} %get-tuple-element.69), channel_id=1, source_target_pairs={{0,1},{1,0},{2,3},{3,2},{4,5},{5,4},{6,7},{7,6},{8,9},{9,8},{10,11... | collective-permute-start | bytes 245768 | tf_op jit(solution)/shard_map/ppermute | solution.py:528
  17.3 4.5 %collective-permute-start.6 = (f32[5,8,512]{2,1,0:T(8,128)S(1)}, f32[5,8,512]{2,1,0:T(8,128)S(1)}, u32[]{:S(2)}, u32[]{:S(2)}) collective-permute-start(f32[5,8,512]{2,1,0:T(8,128)S(1)} %get-tuple-element.70), channel_id=1, source_target_pairs={{0,4},{1,2},{2,1},{3,7},{4,0},{5,6},{6,5},{7,3},{8,12},{9,10},{10,... | collective-permute-start | bytes 245768 | tf_op jit(solution)/shard_map/ppermute | solution.py:528
  17.6 4.6 %collective-permute-start.7 = (f32[1,128]{1,0:T(1,128)S(1)}, f32[1,128]{1,0:T(1,128)S(1)}, u32[]{:S(2)}, u32[]{:S(2)}) collective-permute-start(f32[1,128]{1,0:T(1,128)S(1)} %shard_map.90.window.refs_0_), channel_id=1, source_target_pairs={{0,16},{4,20},{8,24},{12,28},{16,0},{20,4},{24,8},{28,12},{1,17},{... | collective-permute-start | bytes 1544 | tf_op jit(solution)/shard_map/ppermute | solution.py:550
  23.8 5.3 %collective-permute-start.8 = (f32[2,32,512]{2,1,0:T(8,128)S(1)}, f32[2,32,512]{2,1,0:T(8,128)S(1)}, u32[]{:S(2)}, u32[]{:S(2)}) collective-permute-start(f32[2,32,512]{2,1,0:T(8,128)S(1)} %get-tuple-element.77.order), channel_id=1, source_target_pairs={{0,1},{1,0},{2,3},{3,2},{4,5},{5,4},{6,7},{7,6},{8,9},{9,8},{10,11... | collective-permute-start | bytes 393224 | tf_op jit(solution)/shard_map/ppermute | solution.py:528
  24.0 5.1 %collective-permute-start.9 = (f32[2,32,512]{2,1,0:T(8,128)S(1)}, f32[2,32,512]{2,1,0:T(8,128)S(1)}, u32[]{:S(2)}, u32[]{:S(2)}) collective-permute-start(f32[2,32,512]{2,1,0:T(8,128)S(1)} %get-tuple-element.78), channel_id=1, source_target_pairs={{0,4},{1,2},{2,1},{3,7},{4,0},{5,6},{6,5},{7,3},{8,12},{9,10},{10,... | collective-permute-start | bytes 393224 | tf_op jit(solution)/shard_map/ppermute | solution.py:528

commit v8 on v7

--- a/solution.py
+++ b/solution.py
@@ -105,23 +105,31 @@
     return jnp.concatenate([x for x in parts if x.shape[0]], axis=0)
 
 
+CORNER_ROWS = (3, 2, 2, 2, 2)
+
+
+def corner_at(item):
+    return 2 * sum(CORNER_ROWS[:item])
+
+
 def corner_kernel(levels, west, east, window, corner_a, corner_b):
     even = even_level()
 
-    def put(item, top, bottom):
-        corner_a[item] = jnp.where(even, top, bottom)
-        corner_b[item] = jnp.where(even, bottom, top)
-
-    def both(n, start, near=0):
-        return [unpack(west, east, n, lev * LEVEL_ROWS + start) for lev in (levels - 1 - near, near)]
-
-    put(0, *both(V_ROWS, 0))
-    put(1, *both(V_ROWS, 0, 1))
-    for comp in range(3):
-        put(2 + comp, *both(A_ROWS, V_ROWS + comp * A_ROWS))
-
-
-def window_kernel(levels, west, east, counts, counts_2, order, after, window):
+    def part(item, lev):
+        n = CORNER_ROWS[item]
+        held = V_ROWS if item < 2 else A_ROWS
+        at = lev * LEVEL_ROWS + (0 if item < 2 else V_ROWS + (item - 2) * A_ROWS)
+        return east[at : at + n], west[at + held - n : at + held]
+
+    for item, n in enumerate(CORNER_ROWS):
+        near = int(item == 1)
+        for i, (top, bottom) in enumerate(zip(part(item, levels - 1 - near), part(item, near))):
+            at = corner_at(item) + i * n
+            corner_a[at : at + n] = jnp.where(even, top, bottom)
+            corner_b[at : at + n] = jnp.where(even, bottom, top)
+
+
+def window_kernel(levels, west, east, counts, counts_2, order, window):
     at = levels * LEVEL_ROWS + B_ROWS
     window[...] = counts[...] + counts_2[...] + west[at : at + 1, 0:128] + east[at : at + 1, 0:128]
 
@@ -156,9 +164,14 @@
     def from_north(self, x):
         return jnp.where(self.last_lane, 0.0, pltpu.roll(x, self.lat - 1, 1))
 
-    def beyond(self, got_a, got_b, src, k, vv, la):
+    def beyond(self, got_a, got_b, k, vv, la):
         for item in range(5):
-            a, b = got_a[item, src], got_b[item, src]
+            if k < self.chunks:
+                a, b = got_a[item, tile(k)], got_b[item, tile(k)]
+            else:
+                n, at = CORNER_ROWS[item], corner_at(item)
+                gap = jnp.zeros((CHUNK - 2 * n, self.lat), f32)
+                a, b = (jnp.concatenate([x[at : at + n], gap, x[at + n : at + 2 * n]], axis=0) for x in (got_a, got_b))
             below, above = jnp.where(self.even, b, a), jnp.where(self.even, a, b)
             if item < 2:
                 self.put_both(vv, 1 - item, k, jnp.where(self.has[0], below, 0.0))
@@ -205,7 +218,7 @@
 def lev_kernel(levels, cols, lat, lev_a, lev_b, vv, la):
     block = Block(levels, cols, lat)
     for k in range(block.chunks):
-        block.beyond(lev_a, lev_b, tile(k), k, vv, la)
+        block.beyond(lev_a, lev_b, k, vv, la)
 
 
 def first_kernel(levels, cols, lat, v, vel, west, east, vv_in, la, vv, ff, xx, halo_a, halo_b):
@@ -242,10 +255,10 @@
     lax.fori_loop(1, levels - 1, inner_level, 0, unroll=True)
 
 
-def edge_kernel(levels, cols, lat, vel, halo_a, halo_b, corner_a, corner_b, vv_in, la_in, ff_in, xx_in, vv, la, ff, xx):
+def edge_kernel(levels, cols, lat, vel, halo_a, halo_b, corner_a, corner_b, vv_in, la_in, ff_in, xx_in, factor, vv, la, ff, xx):
     block = Block(levels, cols, lat)
     last = block.chunks
-    block.beyond(corner_a, corner_b, slice(0, CHUNK), last, vv, la)
+    block.beyond(corner_a, corner_b, last, vv, la)
     for k in (0, last - 1, last):
         block.first_beyond(vv, la, ff, k)
     for lev in (0, levels - 1):
@@ -259,15 +272,30 @@
         xx[lev, tile(last)] = block.tangent(ff, lev + 1, last, [halo_b[comp, lev] for comp in range(3)])
 
 
+def factor_kernel(levels, cols, lat, columns, owner, west, east, *refs):
+    factor = refs[-1]
+    total = refs[0][...]
+    for ref in refs[1:-1]:
+        total = total + ref[...]
+    scales = columns / (NBOX * jnp.maximum(total, 1.0))
+    for k in range(cols // CHUNK + 1):
+        if k < cols // CHUNK:
+            mine = owner[tile(k)].astype(f32)
+        else:
+            mine = unpack(west, east, B_ROWS, levels * LEVEL_ROWS)
+        value = jnp.zeros((CHUNK, lat), f32)
+        for box in range(1, NBOX + 1):
+            value = jnp.where(mine == float(box), jnp.broadcast_to(scales[:, box - 1 : box], (CHUNK, lat)), value)
+        factor[tile(k)] = value
+
+
 def stencil_kernel(
-    levels, cols, lat, columns, n_counts, lw, vel, owner, west, east, halo_a, halo_b, la, xx, *refs
+    levels, cols, lat, lw, vel, factor, halo_a, halo_b, la, xx, *refs
 ):
-    count_refs = refs[:n_counts]
-    applied, send_a, send_b = refs[n_counts : n_counts + 3]
-    (own_h, w_in, w_e, w_w, w_u, w_d, u_in, u_e, u_w, u_u, u_d, out) = refs[n_counts + 3 :]
+    applied, send_a, send_b = refs[:3]
+    (w_in, w_e, w_w, w_u, w_d, u_in, u_e, u_w, u_u, u_d, out) = refs[3:]
     block = Block(levels, cols, lat)
     chunks, has, even, push = block.chunks, block.has, block.even, block.push
-    own_h[...] = unpack(west, east, B_ROWS, levels * LEVEL_ROWS)
 
     def flow(section, k, lev):
         if k < chunks:
@@ -277,22 +305,11 @@
     def flow_beyond(side, k):
         return [la[side, comp, tile(k)] for comp in range(3)]
 
-    total = count_refs[0][...]
-    for ref in count_refs[1:]:
-        total = total + ref[...]
-    scales = columns / (NBOX * jnp.maximum(total, 1.0))
-    for k in range(chunks + 1):
-        mine = owner[CHUNK * k : CHUNK * (k + 1)].astype(f32) if k < chunks else own_h[...]
-        factor = jnp.zeros((CHUNK, lat), f32)
-        for box in range(1, NBOX + 1):
-            factor = jnp.where(mine == float(box), jnp.broadcast_to(scales[:, box - 1 : box], (CHUNK, lat)), factor)
-        out[0, CHUNK * k : CHUNK * (k + 1)] = factor
-
     def second_level(lev, carry):
         weight = lw[lev]
         for k in range(chunks + 1):
             abc = flow(1, k, lev)
-            x = (weight * out[0, tile(k)]) * xx[lev, tile(k)]
+            x = (weight * factor[tile(k)]) * xx[lev, tile(k)]
             push(x, abc, (w_in, w_e, w_w, w_u, w_d), lev + 1, k)
         return carry
 
@@ -544,15 +561,16 @@
         (sds(levels + 4, padded, lat), sds(2, 3, cols + CHUNK, lat)), (lev_a, lev_b),
     )
     window = call(
-        functools.partial(window_kernel, levels), sds(1, 128), (west, east, counts, counts_2, beta_row, la)
+        functools.partial(window_kernel, levels), sds(1, 128), (west, east, counts, counts_2, beta_row)
     )
     if lon_n == 8:
         near = [window, lax.ppermute(window, "lon", [(i, i ^ 4) for i in range(lon_n)])]
     else:
         near = [lax.psum(counts, "lon")]
+    corners = corner_at(5) + -corner_at(5) % CHUNK
     corner_a, corner_b = call(
         functools.partial(corner_kernel, levels),
-        (sds(5, CHUNK, lat), sds(5, CHUNK, lat)), (west, east, window),
+        (sds(corners, lat), sds(corners, lat)), (west, east, window), flops=1 << 33,
     )
     corner_a, corner_b = both(corner_a, corner_b)
 
@@ -562,16 +580,19 @@
          sds(3, levels, CHUNK, lat), sds(3, levels, CHUNK, lat)),
         (v, vel, west, east, vv, la), alias={4: 0}, flops=4 << 20,
     )
+    factor = call(
+        functools.partial(factor_kernel, levels, cols, lat, float(cols * lon_n * lat)),
+        sds(cols + CHUNK, lat), (owner, west, east, *near), flops=1 << 33,
+    )
     vv, la, ff, xx = call(
         functools.partial(edge_kernel, levels, cols, lat), tuple(sds(*x.shape) for x in (vv, la, ff, xx)),
-        (vel, halo_a, halo_b, corner_a, corner_b, vv, la, ff, xx), alias={5: 0, 6: 1, 7: 2, 8: 3}, flops=2 << 20,
-    )
-    scratch = [pltpu.VMEM((CHUNK, lat), f32)]
-    scratch += [pltpu.VMEM((levels + 2, padded, lat), f32)] * 10
+        (vel, halo_a, halo_b, corner_a, corner_b, vv, la, ff, xx, factor), alias={5: 0, 6: 1, 7: 2, 8: 3}, flops=2 << 20,
+    )
+    scratch = [pltpu.VMEM((levels + 2, padded, lat), f32)] * 10
     scratch += [pltpu.VMEM((levels + 4, cols + CHUNK, lat), f32)]
-    operands = (lw, vel, owner, west, east, halo_a, halo_b, la, xx, *near)
+    operands = (lw, vel, factor, halo_a, halo_b, la, xx)
     part, send_a, send_b = call(
-        functools.partial(stencil_kernel, levels, cols, lat, float(cols * lon_n * lat), len(near)),
+        functools.partial(stencil_kernel, levels, cols, lat),
         (sds(levels, cols, lat), sds(SECOND, cols, lat), sds(SECOND, cols, lat)),
         operands, specs=[SM] + [VM] * (len(operands) - 1), scratch=scratch, flops=8 << 20, mib=12,
     )

time: 44.5 us -> 42.6 us (0.957)
  blocking collectives: 11.8 us -> 10.2 us
  starting transfers between devices: 14.4 us -> 13.7 us
    ppermute x1, waiting for transfers between devices: 0.01 us -> 1.67 us  [body(): lax.ppermute(window, 'lon', [(i, i ^ 4) for i in range(lon_n)])]
    all_to_all x1, blocking collectives: 11.8 us -> 10.2 us  [body(): msg = lax.all_to_all(msg, ('lon', 'lev'), 0, 0, tiled=True)]
    ppermute x1, starting transfers between devices: 1.52 us -> 3.02 us  [body(): lax.ppermute(hi, 'lon', east_of)]
    ppermute x1, waiting for transfers between devices: 1.47 us -> 0.01 us  [body(): lax.ppermute(lo, 'lon', west_of)]
    ppermute x1, starting transfers between devices: 2.61 us -> 1.6 us  [body(): lax.ppermute(lev_b, 'lev', around)]
    ppermute x1, starting transfers between devices: 2.59 us -> 1.95 us  [body(): lax.ppermute(window, 'lon', [(i, i ^ 4) for i in range(lon_n)])]
    ppermute x1, starting transfers between devices: 0.52 us -> 0.01 us  [body(): lax.ppermute(lev_a, 'lev', pairs_a)]
    pallas_call x12 -> x13, Pallas kernels: 13.8 us -> 13.8 us  [call(): pl.pallas_call(kernel, out_shape=outs, in_specs=specs or [VM] * len(opera...]
  transfers between devices with their start and end apart: 10 -> 10, of which waited for: 2 -> 4; matrix products, arithmetic and copies ran while one was open for 0% -> 0% of each run, Pallas kernels for 16% -> 16%
where the time goes in v8:
time: 42.6 us; the launch traced here: 42.4 us
  Pallas kernels  13.8 us (32%)
  starting transfers between devices  13.7 us (32%)
  blocking collectives  10.2 us (24%)
  waiting for transfers between devices  2.57 us (6%)
  between operations  2.07 us (5%)
    pallas_call x13, Pallas kernels, call(): pl.pallas_call(kernel, out_shape=outs, in_specs=specs or [VM] * len(opera...  13.8 us
    all_to_all x1, blocking collectives, body(): msg = lax.all_to_all(msg, ('lon', 'lev'), 0, 0, tiled=True)  10.2 us
    ppermute x1, starting transfers between devices, body(): lax.ppermute(lo, 'lon', west_of)  3.1 us
    ppermute x1, starting transfers between devices, body(): lax.ppermute(hi, 'lon', east_of)  3.02 us
    ppermute x1, starting transfers between devices, body(): lax.ppermute(window, 'lon', [(i, i ^ 4) for i in range(lon_n)])  1.95 us
    ppermute x1, starting transfers between devices, body(): lax.ppermute(counts, 'lon', [((i + 2) % lon_n, i) for i in range(lon_n)])  1.9 us
    ppermute x1, waiting for transfers between devices, body(): lax.ppermute(window, 'lon', [(i, i ^ 4) for i in range(lon_n)])  1.67 us
    ppermute x1, starting transfers between devices, body(): lax.ppermute(lev_b, 'lev', around)  1.6 us
  transfers between devices with their start and end apart: 10, of which 4 were waited for; matrix products, arithmetic and copies ran while one was open for 0% of the time, Pallas kernels for 16%

profile of v8, /device:TPU:0, one launch (start us, length us, event | category | flops | bytes accessed | tf_op | source)
XLA Modules:
  0.0 42.4 jit_solution(7842504172070737596)
XLA Ops:
  0.6 2.3 %shard_map.86 = (f32[80,512]{1,0:T(8,128)}, f32[80,512]{1,0:T(8,128)}, f32[5,32,512]{2,1,0:T(8,128)S(1)}, f32[5,32,512]{2,1,0:T(8,128)S(1)}, f32[1,128]{1,0:T(1,...) custom-call(f32[4,32,512]{2,1,0:T(8,128)} %v_hbm.1, ...), custom_call_target="tpu_custom_call" | custom-call | flops 1048576 | bytes 1900544 | tf_op jit(solution)/shard_map/pallas_call | solution.py:32
  2.9 3.0 %collective-permute-start = (f32[80,512]{1,0:T(8,128)}, f32[80,512]{1,0:T(8,128)S(1)}, u32[]{:S(2)}, u32[]{:S(2)}) collective-permute-start(f32[80,512]{1,0:T(8,128)} %get-tuple-element.58), channel_id=1, source_target_pairs={{0,4},{4,8},{8,12},{12,16},{16,20},{20,24},{24,28},{28,0},{1,5},{5... | collective-permute-start | bytes 491528 | tf_op jit(solution)/shard_map/ppermute | solution.py:549
  5.9 3.1 %collective-permute-start.1 = (f32[80,512]{1,0:T(8,128)}, f32[80,512]{1,0:T(8,128)S(1)}, u32[]{:S(2)}, u32[]{:S(2)}) collective-permute-start(f32[80,512]{1,0:T(8,128)} %get-tuple-element.59), channel_id=1, source_target_pairs={{4,0},{8,4},{12,8},{16,12},{20,16},{24,20},{28,24},{0,28},{5,1},{9... | collective-permute-start | bytes 491528 | tf_op jit(solution)/shard_map/ppermute | solution.py:549
  9.0 1.9 %collective-permute-start.2 = (f32[1,128]{1,0:T(1,128)S(1)}, f32[1,128]{1,0:T(1,128)S(1)}, u32[]{:S(2)}, u32[]{:S(2)}) collective-permute-start(f32[1,128]{1,0:T(1,128)S(1)} %get-tuple-element.60.order.counts), channel_id=1, source_target_pairs={{8,0},{12,4},{16,8},{20,12},{24,16},{28,20},{0,24},{4,28},{9,1},{1... | collective-permute-start | bytes 1544 | tf_op jit(solution)/shard_map/ppermute | solution.py:551
  10.9 0.0 collective-permute-start.4
  10.9 1.6 %collective-permute-start.5 = (f32[5,32,512]{2,1,0:T(8,128)S(1)}, f32[5,32,512]{2,1,0:T(8,128)S(1)}, u32[]{:S(2)}, u32[]{:S(2)}) collective-permute-start(f32[5,32,512]{2,1,0:T(8,128)S(1)} %get-tuple-element.64), channel_id=1, source_target_pairs={{0,3},{1,2},{2,1},{3,0},{4,7},{5,6},{6,5},{7,4},{8,11},{9,10},{10,... | collective-permute-start | bytes 983048 | tf_op jit(solution)/shard_map/ppermute | solution.py:550
  13.2 2.4 %shard_map.87 = (f32[1,128]{1,0:T(1,128)S(1)}, f32[16,4,32,512]{3,2,1,0:T(8,128)S(1)}, f32[4,32,512]{2,1,0:T(8,128)S(1)}) custom-call(f32[1]{0:T(128)} %bitcast.6.beta_prev, f32[16,4,32,512]{3,2,1,0:T(8,128)} %s_hbm.1, f32[4,32,512]{2,1,0:T(8,128)} %prev_hbm.1, f32[1,128]{1,0:T(1,128)S(1)} %get-tuple-element.60.order.counts), custom_call_target="tpu_custom_call" | custom-call | bytes 4456964 | tf_op jit(solution)/shard_map/pallas_call | solution.py:32
  15.6 0.0 collective-permute-done.2.counts_2
  15.6 0.0 collective-permute-done.west
  15.6 2.0 %collective-permute-start.3 = (f32[1,128]{1,0:T(1,128)S(1)}, f32[1,128]{1,0:T(1,128)S(1)}, u32[]{:S(2)}, u32[]{:S(2)}) collective-permute-start(f32[1,128]{1,0:T(1,128)S(1)} %shard_map.88.refs_0_.window), channel_id=1, source_target_pairs={{0,16},{4,20},{8,24},{12,28},{16,0},{20,4},{24,8},{28,12},{1,17},{... | collective-permute-start | bytes 1544 | tf_op jit(solution)/shard_map/ppermute | solution.py:567
  17.6 0.1 collective-permute-start.6
  17.7 0.7 %collective-permute-start.7 = (f32[24,512]{1,0:T(8,128)S(1)}, f32[24,512]{1,0:T(8,128)S(1)}, u32[]{:S(2)}, u32[]{:S(2)}) collective-permute-start(f32[24,512]{1,0:T(8,128)S(1)} %get-tuple-element.70), channel_id=1, source_target_pairs={{0,4},{1,2},{2,1},{3,7},{4,0},{5,6},{6,5},{7,3},{8,12},{9,10},{10,... | collective-permute-start | bytes 147464 | tf_op jit(solution)/shard_map/ppermute | solution.py:545
  18.4 1.7 %collective-permute-done.3.refs_1_ = f32[1,128]{1,0:T(1,128)S(1)} collective-permute-done((f32[1,128]{1,0:T(1,128)S(1)}, f32[1,128]{1,0:T(1,128)S(1)}, u32[]{:S(2)}, u32[]{:S(2)}) %collective-permute-start.3) | collective-permute-done | bytes 544 | tf_op jit(solution)/shard_map/ppermute | solution.py:567
  20.1 0.1 shard_map.89.factor
  20.2 0.0 collective-permute-done.4.lev_a
  20.2 0.1 collective-permute-done.5.lev_b
  20.3 0.1 shard_map.90
  20.4 0.0 copy-start
  20.4 0.8 %shard_map.91 = (f32[8,56,512]{2,1,0:T(8,128)S(1)}, f32[6,56,512]{2,1,0:T(8,128)S(1)}, f32[4,40,512]{2,1,0:T(8,128)S(1)}, f32[3,4,8,512]{3,2,1,0:T(8,128)S(1)}, f32[3,4,8,512]{3,2,1,0:T(8,128)S(1)}) custom-call(f32[4,32,512]{2,1,0:T(8,128)S(1)} %get-tuple-element.62.v, ...), custom_call_target="tpu_custom_call", output_to_operand_aliasing={{0}: (4, {})} | custom-call | flops 4194304 | bytes 3571712 | tf_op jit(solution)/shard_map/pallas_call | solution.py:32
  21.1 0.0 collective-permute-done.6.corner_a
  21.1 0.7 %collective-permute-done.7.corner_b = f32[24,512]{1,0:T(8,128)S(1)} collective-permute-done((f32[24,512]{1,0:T(8,128)S(1)}, f32[24,512]{1,0:T(8,128)S(1)}, u32[]{:S(2)}, u32[]{:S(2)}) %collective-permute-start.7) | collective-permute-done | bytes 49184 | tf_op jit(solution)/shard_map/ppermute | solution.py:545
  21.8 0.5 %shard_map.93 = (f32[8,56,512]{2,1,0:T(8,128)S(1)}, f32[2,3,40,512]{3,2,1,0:T(8,128)S(1)}, f32[6,56,512]{2,1,0:T(8,128)S(1)}, f32[4,40,512]{2,1,0:T(8,128)S(1)}) custom-call(f32[2,3,4,32,512]{4,3,2,1,0:T(8,128)S(1)} %get-tuple-element.56.vel, ...), custom_call_target="tpu_custom_call", output_to_operand_aliasing={{0}: (5, {}), {1}: (6, {}), {2}: (7, {}), {3}: (8, {})} | custom-call | flops 2097152 | bytes 4571136 | tf_op jit(solution)/shard_map/pallas_call | solution.py:32
  22.3 1.4 %shard_map.94 = (f32[4,32,512]{2,1,0:T(8,128)S(1)}, f32[2,32,512]{2,1,0:T(8,128)S(1)}, f32[2,32,512]{2,1,0:T(8,128)S(1)}) custom-call(f32[4]{0:T(128)S(1)} %copy-done, f32[2,3,4,32,512]{4,3,2,1,0:T(8,128)S(1)} %get-tuple-element.56.vel, f32[40,512]{1,0:T(8,128)S(1)} %shard_map.89.factor, f32[3,4,8,512]{3,2,1,0:T(8,128)S(1)} %get-tuple-element.67.halo_a, ...), custom_call_target="tpu_custom_call" | custom-call | flops 8388608 | bytes 2867216 | tf_op jit(solution)/shard_map/pallas_call | solution.py:32
  23.7 0.7 %collective-permute-start.9 = (f32[2,32,512]{2,1,0:T(8,128)S(1)}, f32[2,32,512]{2,1,0:T(8,128)S(1)}, u32[]{:S(2)}, u32[]{:S(2)}) collective-permute-start(f32[2,32,512]{2,1,0:T(8,128)S(1)} %get-tuple-element.78), channel_id=1, source_target_pairs={{0,4},{1,2},{2,1},{3,7},{4,0},{5,6},{6,5},{7,3},{8,12},{9,10},{10,... | collective-permute-start | bytes 393224 | tf_op jit(solution)/shard_map/ppermute | solution.py:545
  24.5 0.6 %collective-permute-start.8 = (f32[2,32,512]{2,1,0:T(8,128)S(1)}, f32[2,32,512]{2,1,0:T(8,128)S(1)}, u32[]{:S(2)}, u32[]{:S(2)}) collective-permute-start(f32[2,32,512]{2,1,0:T(8,128)S(1)} %get-tuple-element.77.order), channel_id=1, source_target_pairs={{0,1},{1,0},{2,3},{3,2},{4,5},{5,4},{6,7},{7,6},{8,9},{9,8},{10,11... | collective-permute-start | bytes 393224 | tf_op jit(solution)/shard_map/ppermute | solution.py:545
  25.0 3.6 %shard_map.95.gram = f32[3,128]{1,0:T(4,128)S(1)} custom-call(f32[16,4,32,512]{3,2,1,0:T(8,128)S(1)} %get-tuple-element.80.s, f32[4,32,512]{2,1,0:T(8,128)S(1)} %get-tuple-element.62.v, f32[2,32,512]{2,1,0:T(8,128)S(1)} %get-tuple-element.77.order), custom_call_target="tpu_custom_call" | custom-call | flops 20971520 | bytes 4587520 | tf_op jit(solution)/shard_map/pallas_call | solution.py:32
  28.7 0.1 collective-permute-done.9.got_b
  28.8 0.0 collective-permute-done.8.got_a
  28.8 0.6 %shard_map.96 = (f32[4,32,512]{2,1,0:T(8,128)S(1)}, f32[32,3,128]{2,1,0:T(4,128)S(1)}) custom-call(f32[4,32,512]{2,1,0:T(8,128)S(1)} %get-tuple-element.76.part, f32[2,32,512]{2,1,0:T(8,128)S(1)} %collective-permute-done.8.got_a, f32[2,32,512]{2,1,0:T(8,128)S(1)} %collective-permute-done.9.got_b, f32[4,32,512]{2,1,0:T(8,128)S(1)} %get-tuple-element.79.prev, ...), custom_call_target="tpu_custom_call" | custom-call | bytes 5244928 | tf_op jit(solution)/shard_map/pallas_call | solution.py:32
  29.4 10.2 %all_to_all.5.msg = f32[32,3,128]{2,1,0:T(4,128)S(1)} all-to-all(f32[32,3,128]{2,1,0:T(4,128)S(1)} %get-tuple-element.81), channel_id=1, replica_groups=mesh['lon'=8,'lev'=4] {'lon','lev'}, dimensions={0} | all-to-all | bytes 98304 | tf_op jit(solution)/shard_map/all_to_all | solution.py:612
  39.6 1.3 %shard_map.97 = (f32[4,32,512]{2,1,0:T(8,128)S(1)}, f32[1,128]{1,0:T(1,128)S(1)}, f32[1,1]{1,0:T(1,128)}) custom-call(f32[32,3,128]{2,1,0:T(4,128)S(1)} %all_to_all.5.msg, f32[4,32,512]{2,1,0:T(8,128)S(1)} %get-tuple-element.82.applied, f32[4,32,512]{2,1,0:T(8,128)S(1)} %get-tuple-element.62.v, f32[16,4,32,512]{3,2,1,0:T(8,128)S(1)} %get-tuple-element.80.s), custom_call_target="tpu_custom_call" | custom-call | bytes 4767744 | tf_op jit(solution)/shard_map/pallas_call | solution.py:32
  41.6 0.8 %shard_map.98 = (f32[4,32,512]{2,1,0:T(8,128)}, f32[1,18]{1,0:T(1,128)}) custom-call(f32[1,128]{1,0:T(1,128)S(1)} %get-tuple-element.88.row, f32[4,32,512]{2,1,0:T(8,128)S(1)} %get-tuple-element.84.orthogonal), custom_call_target="tpu_custom_call" | custom-call | bytes 262656 | tf_op jit(solution)/shard_map/pallas_call | solution.py:32
  (5 shorter events, 0.1 us)
Async XLA Ops:
  2.9 12.7 %collective-permute-start = (f32[80,512]{1,0:T(8,128)}, f32[80,512]{1,0:T(8,128)S(1)}, u32[]{:S(2)}, u32[]{:S(2)}) collective-permute-start(f32[80,512]{1,0:T(8,128)} %get-tuple-element.58), channel_id=1, source_target_pairs={{0,4},{4,8},{8,12},{12,16},{16,20},{20,24},{24,28},{28,0},{1,5},{5... | collective-permute-start | bytes 491528 | tf_op jit(solution)/shard_map/ppermute | solution.py:549
  5.9 9.7 %collective-permute-start.1 = (f32[80,512]{1,0:T(8,128)}, f32[80,512]{1,0:T(8,128)S(1)}, u32[]{:S(2)}, u32[]{:S(2)}) collective-permute-start(f32[80,512]{1,0:T(8,128)} %get-tuple-element.59), channel_id=1, source_target_pairs={{4,0},{8,4},{12,8},{16,12},{20,16},{24,20},{28,24},{0,28},{5,1},{9... | collective-permute-start | bytes 491528 | tf_op jit(solution)/shard_map/ppermute | solution.py:549
  9.0 6.5 %collective-permute-start.2 = (f32[1,128]{1,0:T(1,128)S(1)}, f32[1,128]{1,0:T(1,128)S(1)}, u32[]{:S(2)}, u32[]{:S(2)}) collective-permute-start(f32[1,128]{1,0:T(1,128)S(1)} %get-tuple-element.60.order.counts), channel_id=1, source_target_pairs={{8,0},{12,4},{16,8},{20,12},{24,16},{28,20},{0,24},{4,28},{9,1},{1... | collective-permute-start | bytes 1544 | tf_op jit(solution)/shard_map/ppermute | solution.py:551
  10.9 9.3 %collective-permute-start.4 = (f32[5,32,512]{2,1,0:T(8,128)S(1)}, f32[5,32,512]{2,1,0:T(8,128)S(1)}, u32[]{:S(2)}, u32[]{:S(2)}) collective-permute-start(f32[5,32,512]{2,1,0:T(8,128)S(1)} %get-tuple-element.63), channel_id=1, source_target_pairs={{0,1},{1,0},{2,3},{3,2},{4,5},{5,4},{6,7},{7,6},{8,9},{9,8},{10,11... | collective-permute-start | bytes 983048 | tf_op jit(solution)/shard_map/ppermute | solution.py:550
  10.9 9.4 %collective-permute-start.5 = (f32[5,32,512]{2,1,0:T(8,128)S(1)}, f32[5,32,512]{2,1,0:T(8,128)S(1)}, u32[]{:S(2)}, u32[]{:S(2)}) collective-permute-start(f32[5,32,512]{2,1,0:T(8,128)S(1)} %get-tuple-element.64), channel_id=1, source_target_pairs={{0,3},{1,2},{2,1},{3,0},{4,7},{5,6},{6,5},{7,4},{8,11},{9,10},{10,... | collective-permute-start | bytes 983048 | tf_op jit(solution)/shard_map/ppermute | solution.py:550
  15.6 4.5 %collective-permute-start.3 = (f32[1,128]{1,0:T(1,128)S(1)}, f32[1,128]{1,0:T(1,128)S(1)}, u32[]{:S(2)}, u32[]{:S(2)}) collective-permute-start(f32[1,128]{1,0:T(1,128)S(1)} %shard_map.88.refs_0_.window), channel_id=1, source_target_pairs={{0,16},{4,20},{8,24},{12,28},{16,0},{20,4},{24,8},{28,12},{1,17},{... | collective-permute-start | bytes 1544 | tf_op jit(solution)/shard_map/ppermute | solution.py:567
  17.6 3.5 %collective-permute-start.6 = (f32[24,512]{1,0:T(8,128)S(1)}, f32[24,512]{1,0:T(8,128)S(1)}, u32[]{:S(2)}, u32[]{:S(2)}) collective-permute-start(f32[24,512]{1,0:T(8,128)S(1)} %get-tuple-element.69), channel_id=1, source_target_pairs={{0,1},{1,0},{2,3},{3,2},{4,5},{5,4},{6,7},{7,6},{8,9},{9,8},{10,11... | collective-permute-start | bytes 147464 | tf_op jit(solution)/shard_map/ppermute | solution.py:545
  17.7 4.2 %collective-permute-start.7 = (f32[24,512]{1,0:T(8,128)S(1)}, f32[24,512]{1,0:T(8,128)S(1)}, u32[]{:S(2)}, u32[]{:S(2)}) collective-permute-start(f32[24,512]{1,0:T(8,128)S(1)} %get-tuple-element.70), channel_id=1, source_target_pairs={{0,4},{1,2},{2,1},{3,7},{4,0},{5,6},{6,5},{7,3},{8,12},{9,10},{10,... | collective-permute-start | bytes 147464 | tf_op jit(solution)/shard_map/ppermute | solution.py:545
  20.4 2.0 %copy-start = (f32[4]{0:T(128)S(1)}, f32[4]{0:T(128)}, u32[]{:S(2)}) copy-start(f32[4]{0:T(128)} %lw.1) | copy-start | bytes 52
  23.7 5.0 %collective-permute-start.9 = (f32[2,32,512]{2,1,0:T(8,128)S(1)}, f32[2,32,512]{2,1,0:T(8,128)S(1)}, u32[]{:S(2)}, u32[]{:S(2)}) collective-permute-start(f32[2,32,512]{2,1,0:T(8,128)S(1)} %get-tuple-element.78), channel_id=1, source_target_pairs={{0,4},{1,2},{2,1},{3,7},{4,0},{5,6},{6,5},{7,3},{8,12},{9,10},{10,... | collective-permute-start | bytes 393224 | tf_op jit(solution)/shard_map/ppermute | solution.py:545
  24.5 4.3 %collective-permute-start.8 = (f32[2,32,512]{2,1,0:T(8,128)S(1)}, f32[2,32,512]{2,1,0:T(8,128)S(1)}, u32[]{:S(2)}, u32[]{:S(2)}) collective-permute-start(f32[2,32,512]{2,1,0:T(8,128)S(1)} %get-tuple-element.77.order), channel_id=1, source_target_pairs={{0,1},{1,0},{2,3},{3,2},{4,5},{5,4},{6,7},{7,6},{8,9},{9,8},{10,11... | collective-permute-start | bytes 393224 | tf_op jit(solution)/shard_map/ppermute | solution.py:545

commit v9 on v8

--- a/solution.py
+++ b/solution.py
@@ -272,7 +272,7 @@
         xx[lev, tile(last)] = block.tangent(ff, lev + 1, last, [halo_b[comp, lev] for comp in range(3)])
 
 
-def factor_kernel(levels, cols, lat, columns, owner, west, east, *refs):
+def factor_kernel(levels, cols, lat, columns, owner, west, east, after, *refs):
     factor = refs[-1]
     total = refs[0][...]
     for ref in refs[1:-1]:
@@ -582,7 +582,7 @@
     )
     factor = call(
         functools.partial(factor_kernel, levels, cols, lat, float(cols * lon_n * lat)),
-        sds(cols + CHUNK, lat), (owner, west, east, *near), flops=1 << 33,
+        sds(cols + CHUNK, lat), (owner, west, east, halo_a, *near), flops=1 << 33,
     )
     vv, la, ff, xx = call(
         functools.partial(edge_kernel, levels, cols, lat), tuple(sds(*x.shape) for x in (vv, la, ff, xx)),

time: 42.6 us -> 41.9 us (0.984)
  blocking collectives: 10.2 us -> 9.49 us
    ppermute x1, waiting for transfers between devices: 0.06 us -> 1.86 us  [body(): lax.ppermute(lev_b, 'lev', around)]
    ppermute x1, waiting for transfers between devices: 1.67 us -> 0.01 us  [body(): lax.ppermute(window, 'lon', [(i, i ^ 4) for i in range(lon_n)])]
    all_to_all x1, blocking collectives: 10.2 us -> 9.49 us  [body(): msg = lax.all_to_all(msg, ('lon', 'lev'), 0, 0, tiled=True)]
  transfers between devices with their start and end apart: 10 -> 10, of which waited for: 4 -> 3; matrix products, arithmetic and copies ran while one was open for 0% -> 0% of each run, Pallas kernels for 16% -> 17%
where the time goes in v9:
time: 41.9 us; the launch traced here: 41.7 us
  Pallas kernels  13.8 us (33%)
  starting transfers between devices  13.7 us (33%)
  blocking collectives  9.49 us (23%)
  waiting for transfers between devices  2.57 us (6%)
  between operations  2.07 us (5%)
    pallas_call x13, Pallas kernels, call(): pl.pallas_call(kernel, out_shape=outs, in_specs=specs or [VM] * len(opera...  13.8 us
    all_to_all x1, blocking collectives, body(): msg = lax.all_to_all(msg, ('lon', 'lev'), 0, 0, tiled=True)  9.49 us
    ppermute x1, starting transfers between devices, body(): lax.ppermute(lo, 'lon', west_of)  3.1 us
    ppermute x1, starting transfers between devices, body(): lax.ppermute(hi, 'lon', east_of)  3.02 us
    ppermute x1, starting transfers between devices, body(): lax.ppermute(window, 'lon', [(i, i ^ 4) for i in range(lon_n)])  1.95 us
    ppermute x1, starting transfers between devices, body(): lax.ppermute(counts, 'lon', [((i + 2) % lon_n, i) for i in range(lon_n)])  1.9 us
    ppermute x1, waiting for transfers between devices, body(): lax.ppermute(lev_b, 'lev', around)  1.86 us
    ppermute x1, starting transfers between devices, body(): lax.ppermute(lev_b, 'lev', around)  1.6 us
  transfers between devices with their start and end apart: 10, of which 3 were waited for; matrix products, arithmetic and copies ran while one was open for 0% of the time, Pallas kernels for 17%

profile of v9, /device:TPU:0, one launch (start us, length us, event | category | flops | bytes accessed | tf_op | source)
XLA Modules:
  0.0 41.7 jit_solution(9008571512979285632)
XLA Ops:
  0.6 2.3 %shard_map.86 = (f32[80,512]{1,0:T(8,128)}, f32[80,512]{1,0:T(8,128)}, f32[5,32,512]{2,1,0:T(8,128)S(1)}, f32[5,32,512]{2,1,0:T(8,128)S(1)}, f32[1,128]{1,0:T(1,...) custom-call(f32[4,32,512]{2,1,0:T(8,128)} %v_hbm.1, ...), custom_call_target="tpu_custom_call" | custom-call | flops 1048576 | bytes 1900544 | tf_op jit(solution)/shard_map/pallas_call | solution.py:32
  2.9 3.0 %collective-permute-start = (f32[80,512]{1,0:T(8,128)}, f32[80,512]{1,0:T(8,128)S(1)}, u32[]{:S(2)}, u32[]{:S(2)}) collective-permute-start(f32[80,512]{1,0:T(8,128)} %get-tuple-element.58), channel_id=1, source_target_pairs={{0,4},{4,8},{8,12},{12,16},{16,20},{20,24},{24,28},{28,0},{1,5},{5... | collective-permute-start | bytes 491528 | tf_op jit(solution)/shard_map/ppermute | solution.py:549
  5.9 3.1 %collective-permute-start.1 = (f32[80,512]{1,0:T(8,128)}, f32[80,512]{1,0:T(8,128)S(1)}, u32[]{:S(2)}, u32[]{:S(2)}) collective-permute-start(f32[80,512]{1,0:T(8,128)} %get-tuple-element.59), channel_id=1, source_target_pairs={{4,0},{8,4},{12,8},{16,12},{20,16},{24,20},{28,24},{0,28},{5,1},{9... | collective-permute-start | bytes 491528 | tf_op jit(solution)/shard_map/ppermute | solution.py:549
  9.0 1.9 %collective-permute-start.4 = (f32[1,128]{1,0:T(1,128)S(1)}, f32[1,128]{1,0:T(1,128)S(1)}, u32[]{:S(2)}, u32[]{:S(2)}) collective-permute-start(f32[1,128]{1,0:T(1,128)S(1)} %get-tuple-element.66.order.counts), channel_id=1, source_target_pairs={{8,0},{12,4},{16,8},{20,12},{24,16},{28,20},{0,24},{4,28},{9,1},{1... | collective-permute-start | bytes 1544 | tf_op jit(solution)/shard_map/ppermute | solution.py:551
  10.9 0.0 collective-permute-start.2
  10.9 1.6 %collective-permute-start.3 = (f32[5,32,512]{2,1,0:T(8,128)S(1)}, f32[5,32,512]{2,1,0:T(8,128)S(1)}, u32[]{:S(2)}, u32[]{:S(2)}) collective-permute-start(f32[5,32,512]{2,1,0:T(8,128)S(1)} %get-tuple-element.62), channel_id=1, source_target_pairs={{0,3},{1,2},{2,1},{3,0},{4,7},{5,6},{6,5},{7,4},{8,11},{9,10},{10,... | collective-permute-start | bytes 983048 | tf_op jit(solution)/shard_map/ppermute | solution.py:550
  13.2 2.4 %shard_map.89 = (f32[1,128]{1,0:T(1,128)S(1)}, f32[16,4,32,512]{3,2,1,0:T(8,128)S(1)}, f32[4,32,512]{2,1,0:T(8,128)S(1)}) custom-call(f32[1]{0:T(128)} %bitcast.6.beta_prev, f32[16,4,32,512]{3,2,1,0:T(8,128)} %s_hbm.1, f32[4,32,512]{2,1,0:T(8,128)} %prev_hbm.1, f32[1,128]{1,0:T(1,128)S(1)} %get-tuple-element.66.order.counts), custom_call_target="tpu_custom_call" | custom-call | bytes 4456964 | tf_op jit(solution)/shard_map/pallas_call | solution.py:32
  15.6 0.0 collective-permute-done.4.counts_2
  15.6 0.0 collective-permute-done.west
  15.6 0.0 collective-permute-done.1.east
  15.6 2.0 %collective-permute-start.5 = (f32[1,128]{1,0:T(1,128)S(1)}, f32[1,128]{1,0:T(1,128)S(1)}, u32[]{:S(2)}, u32[]{:S(2)}) collective-permute-start(f32[1,128]{1,0:T(1,128)S(1)} %shard_map.90.refs_0_.window), channel_id=1, source_target_pairs={{0,16},{4,20},{8,24},{12,28},{16,0},{20,4},{24,8},{28,12},{1,17},{... | collective-permute-start | bytes 1544 | tf_op jit(solution)/shard_map/ppermute | solution.py:567
  17.6 0.1 collective-permute-start.6
  17.7 0.7 %collective-permute-start.7 = (f32[24,512]{1,0:T(8,128)S(1)}, f32[24,512]{1,0:T(8,128)S(1)}, u32[]{:S(2)}, u32[]{:S(2)}) collective-permute-start(f32[24,512]{1,0:T(8,128)S(1)} %get-tuple-element.70), channel_id=1, source_target_pairs={{0,4},{1,2},{2,1},{3,7},{4,0},{5,6},{6,5},{7,3},{8,12},{9,10},{10,... | collective-permute-start | bytes 147464 | tf_op jit(solution)/shard_map/ppermute | solution.py:545
  18.4 0.0 collective-permute-done.2.lev_a
  18.4 1.9 %collective-permute-done.3.lev_b = f32[5,32,512]{2,1,0:T(8,128)S(1)} collective-permute-done((f32[5,32,512]{2,1,0:T(8,128)S(1)}, f32[5,32,512]{2,1,0:T(8,128)S(1)}, u32[]{:S(2)}, u32[]{:S(2)}) %collective-permute-start.3) | collective-permute-done | bytes 327712 | tf_op jit(solution)/shard_map/ppermute | solution.py:550
  20.3 0.1 shard_map.87
  20.4 0.8 %shard_map.88 = (f32[8,56,512]{2,1,0:T(8,128)S(1)}, f32[6,56,512]{2,1,0:T(8,128)S(1)}, f32[4,40,512]{2,1,0:T(8,128)S(1)}, f32[3,4,8,512]{3,2,1,0:T(8,128)S(1)}, f32[3,4,8,512]{3,2,1,0:T(8,128)S(1)}) custom-call(f32[4,32,512]{2,1,0:T(8,128)S(1)} %get-tuple-element.60.v, ...), custom_call_target="tpu_custom_call", output_to_operand_aliasing={{0}: (4, {})} | custom-call | flops 4194304 | bytes 3571712 | tf_op jit(solution)/shard_map/pallas_call | solution.py:32
  21.1 0.0 collective-permute-done.5.refs_1_
  21.1 0.1 shard_map.91.factor
  21.2 0.0 copy-start
  21.2 0.0 collective-permute-done.6.corner_a
  21.3 0.6 %collective-permute-done.7.corner_b = f32[24,512]{1,0:T(8,128)S(1)} collective-permute-done((f32[24,512]{1,0:T(8,128)S(1)}, f32[24,512]{1,0:T(8,128)S(1)}, u32[]{:S(2)}, u32[]{:S(2)}) %collective-permute-start.7) | collective-permute-done | bytes 49184 | tf_op jit(solution)/shard_map/ppermute | solution.py:545
  21.8 0.5 %shard_map.93 = (f32[8,56,512]{2,1,0:T(8,128)S(1)}, f32[2,3,40,512]{3,2,1,0:T(8,128)S(1)}, f32[6,56,512]{2,1,0:T(8,128)S(1)}, f32[4,40,512]{2,1,0:T(8,128)S(1)}) custom-call(f32[2,3,4,32,512]{4,3,2,1,0:T(8,128)S(1)} %get-tuple-element.56.vel, ...), custom_call_target="tpu_custom_call", output_to_operand_aliasing={{0}: (5, {}), {1}: (6, {}), {2}: (7, {}), {3}: (8, {})} | custom-call | flops 2097152 | bytes 4571136 | tf_op jit(solution)/shard_map/pallas_call | solution.py:32
  22.3 1.4 %shard_map.94 = (f32[4,32,512]{2,1,0:T(8,128)S(1)}, f32[2,32,512]{2,1,0:T(8,128)S(1)}, f32[2,32,512]{2,1,0:T(8,128)S(1)}) custom-call(f32[4]{0:T(128)S(1)} %copy-done, f32[2,3,4,32,512]{4,3,2,1,0:T(8,128)S(1)} %get-tuple-element.56.vel, f32[40,512]{1,0:T(8,128)S(1)} %shard_map.91.factor, f32[3,4,8,512]{3,2,1,0:T(8,128)S(1)} %get-tuple-element.65.after.halo_a, ...), custom_call_target="tpu_custom_call" | custom-call | flops 8388608 | bytes 2867216 | tf_op jit(solution)/shard_map/pallas_call | solution.py:32
  23.7 0.7 %collective-permute-start.9 = (f32[2,32,512]{2,1,0:T(8,128)S(1)}, f32[2,32,512]{2,1,0:T(8,128)S(1)}, u32[]{:S(2)}, u32[]{:S(2)}) collective-permute-start(f32[2,32,512]{2,1,0:T(8,128)S(1)} %get-tuple-element.78), channel_id=1, source_target_pairs={{0,4},{1,2},{2,1},{3,7},{4,0},{5,6},{6,5},{7,3},{8,12},{9,10},{10,... | collective-permute-start | bytes 393224 | tf_op jit(solution)/shard_map/ppermute | solution.py:545
  24.5 0.6 %collective-permute-start.8 = (f32[2,32,512]{2,1,0:T(8,128)S(1)}, f32[2,32,512]{2,1,0:T(8,128)S(1)}, u32[]{:S(2)}, u32[]{:S(2)}) collective-permute-start(f32[2,32,512]{2,1,0:T(8,128)S(1)} %get-tuple-element.77.order), channel_id=1, source_target_pairs={{0,1},{1,0},{2,3},{3,2},{4,5},{5,4},{6,7},{7,6},{8,9},{9,8},{10,11... | collective-permute-start | bytes 393224 | tf_op jit(solution)/shard_map/ppermute | solution.py:545
  25.0 3.6 %shard_map.95.gram = f32[3,128]{1,0:T(4,128)S(1)} custom-call(f32[16,4,32,512]{3,2,1,0:T(8,128)S(1)} %get-tuple-element.80.s, f32[4,32,512]{2,1,0:T(8,128)S(1)} %get-tuple-element.60.v, f32[2,32,512]{2,1,0:T(8,128)S(1)} %get-tuple-element.77.order), custom_call_target="tpu_custom_call" | custom-call | flops 20971520 | bytes 4587520 | tf_op jit(solution)/shard_map/pallas_call | solution.py:32
  28.7 0.1 collective-permute-done.9.got_b
  28.8 0.6 %shard_map.96 = (f32[4,32,512]{2,1,0:T(8,128)S(1)}, f32[32,3,128]{2,1,0:T(4,128)S(1)}) custom-call(f32[4,32,512]{2,1,0:T(8,128)S(1)} %get-tuple-element.76.part, f32[2,32,512]{2,1,0:T(8,128)S(1)} %collective-permute-done.8.got_a, f32[2,32,512]{2,1,0:T(8,128)S(1)} %collective-permute-done.9.got_b, f32[4,32,512]{2,1,0:T(8,128)S(1)} %get-tuple-element.79.prev, ...), custom_call_target="tpu_custom_call" | custom-call | bytes 5244928 | tf_op jit(solution)/shard_map/pallas_call | solution.py:32
  29.4 9.5 %all_to_all.5.msg = f32[32,3,128]{2,1,0:T(4,128)S(1)} all-to-all(f32[32,3,128]{2,1,0:T(4,128)S(1)} %get-tuple-element.81), channel_id=1, replica_groups=mesh['lon'=8,'lev'=4] {'lon','lev'}, dimensions={0} | all-to-all | bytes 98304 | tf_op jit(solution)/shard_map/all_to_all | solution.py:612
  38.9 1.3 %shard_map.97 = (f32[4,32,512]{2,1,0:T(8,128)S(1)}, f32[1,128]{1,0:T(1,128)S(1)}, f32[1,1]{1,0:T(1,128)}) custom-call(f32[32,3,128]{2,1,0:T(4,128)S(1)} %all_to_all.5.msg, f32[4,32,512]{2,1,0:T(8,128)S(1)} %get-tuple-element.82.applied, f32[4,32,512]{2,1,0:T(8,128)S(1)} %get-tuple-element.60.v, f32[16,4,32,512]{3,2,1,0:T(8,128)S(1)} %get-tuple-element.80.s), custom_call_target="tpu_custom_call" | custom-call | bytes 4767744 | tf_op jit(solution)/shard_map/pallas_call | solution.py:32
  40.9 0.8 %shard_map.98 = (f32[4,32,512]{2,1,0:T(8,128)}, f32[1,18]{1,0:T(1,128)}) custom-call(f32[1,128]{1,0:T(1,128)S(1)} %get-tuple-element.88.row, f32[4,32,512]{2,1,0:T(8,128)S(1)} %get-tuple-element.84.orthogonal), custom_call_target="tpu_custom_call" | custom-call | bytes 262656 | tf_op jit(solution)/shard_map/pallas_call | solution.py:32
  (5 shorter events, 0.1 us)
Async XLA Ops:
  2.9 12.7 %collective-permute-start = (f32[80,512]{1,0:T(8,128)}, f32[80,512]{1,0:T(8,128)S(1)}, u32[]{:S(2)}, u32[]{:S(2)}) collective-permute-start(f32[80,512]{1,0:T(8,128)} %get-tuple-element.58), channel_id=1, source_target_pairs={{0,4},{4,8},{8,12},{12,16},{16,20},{20,24},{24,28},{28,0},{1,5},{5... | collective-permute-start | bytes 491528 | tf_op jit(solution)/shard_map/ppermute | solution.py:549
  5.9 9.7 %collective-permute-start.1 = (f32[80,512]{1,0:T(8,128)}, f32[80,512]{1,0:T(8,128)S(1)}, u32[]{:S(2)}, u32[]{:S(2)}) collective-permute-start(f32[80,512]{1,0:T(8,128)} %get-tuple-element.59), channel_id=1, source_target_pairs={{4,0},{8,4},{12,8},{16,12},{20,16},{24,20},{28,24},{0,28},{5,1},{9... | collective-permute-start | bytes 491528 | tf_op jit(solution)/shard_map/ppermute | solution.py:549
  9.0 6.5 %collective-permute-start.4 = (f32[1,128]{1,0:T(1,128)S(1)}, f32[1,128]{1,0:T(1,128)S(1)}, u32[]{:S(2)}, u32[]{:S(2)}) collective-permute-start(f32[1,128]{1,0:T(1,128)S(1)} %get-tuple-element.66.order.counts), channel_id=1, source_target_pairs={{8,0},{12,4},{16,8},{20,12},{24,16},{28,20},{0,24},{4,28},{9,1},{1... | collective-permute-start | bytes 1544 | tf_op jit(solution)/shard_map/ppermute | solution.py:551
  10.9 7.5 %collective-permute-start.2 = (f32[5,32,512]{2,1,0:T(8,128)S(1)}, f32[5,32,512]{2,1,0:T(8,128)S(1)}, u32[]{:S(2)}, u32[]{:S(2)}) collective-permute-start(f32[5,32,512]{2,1,0:T(8,128)S(1)} %get-tuple-element.61), channel_id=1, source_target_pairs={{0,1},{1,0},{2,3},{3,2},{4,5},{5,4},{6,7},{7,6},{8,9},{9,8},{10,11... | collective-permute-start | bytes 983048 | tf_op jit(solution)/shard_map/ppermute | solution.py:550
  10.9 9.4 %collective-permute-start.3 = (f32[5,32,512]{2,1,0:T(8,128)S(1)}, f32[5,32,512]{2,1,0:T(8,128)S(1)}, u32[]{:S(2)}, u32[]{:S(2)}) collective-permute-start(f32[5,32,512]{2,1,0:T(8,128)S(1)} %get-tuple-element.62), channel_id=1, source_target_pairs={{0,3},{1,2},{2,1},{3,0},{4,7},{5,6},{6,5},{7,4},{8,11},{9,10},{10,... | collective-permute-start | bytes 983048 | tf_op jit(solution)/shard_map/ppermute | solution.py:550
  15.6 5.5 %collective-permute-start.5 = (f32[1,128]{1,0:T(1,128)S(1)}, f32[1,128]{1,0:T(1,128)S(1)}, u32[]{:S(2)}, u32[]{:S(2)}) collective-permute-start(f32[1,128]{1,0:T(1,128)S(1)} %shard_map.90.refs_0_.window), channel_id=1, source_target_pairs={{0,16},{4,20},{8,24},{12,28},{16,0},{20,4},{24,8},{28,12},{1,17},{... | collective-permute-start | bytes 1544 | tf_op jit(solution)/shard_map/ppermute | solution.py:567
  17.6 3.6 %collective-permute-start.6 = (f32[24,512]{1,0:T(8,128)S(1)}, f32[24,512]{1,0:T(8,128)S(1)}, u32[]{:S(2)}, u32[]{:S(2)}) collective-permute-start(f32[24,512]{1,0:T(8,128)S(1)} %get-tuple-element.69), channel_id=1, source_target_pairs={{0,1},{1,0},{2,3},{3,2},{4,5},{5,4},{6,7},{7,6},{8,9},{9,8},{10,11... | collective-permute-start | bytes 147464 | tf_op jit(solution)/shard_map/ppermute | solution.py:545
  17.7 4.2 %collective-permute-start.7 = (f32[24,512]{1,0:T(8,128)S(1)}, f32[24,512]{1,0:T(8,128)S(1)}, u32[]{:S(2)}, u32[]{:S(2)}) collective-permute-start(f32[24,512]{1,0:T(8,128)S(1)} %get-tuple-element.70), channel_id=1, source_target_pairs={{0,4},{1,2},{2,1},{3,7},{4,0},{5,6},{6,5},{7,3},{8,12},{9,10},{10,... | collective-permute-start | bytes 147464 | tf_op jit(solution)/shard_map/ppermute | solution.py:545
  21.2 1.1 %copy-start = (f32[4]{0:T(128)S(1)}, f32[4]{0:T(128)}, u32[]{:S(2)}) copy-start(f32[4]{0:T(128)} %lw.1) | copy-start | bytes 52
  23.7 5.0 %collective-permute-start.9 = (f32[2,32,512]{2,1,0:T(8,128)S(1)}, f32[2,32,512]{2,1,0:T(8,128)S(1)}, u32[]{:S(2)}, u32[]{:S(2)}) collective-permute-start(f32[2,32,512]{2,1,0:T(8,128)S(1)} %get-tuple-element.78), channel_id=1, source_target_pairs={{0,4},{1,2},{2,1},{3,7},{4,0},{5,6},{6,5},{7,3},{8,12},{9,10},{10,... | collective-permute-start | bytes 393224 | tf_op jit(solution)/shard_map/ppermute | solution.py:545
  24.5 4.3 %collective-permute-start.8 = (f32[2,32,512]{2,1,0:T(8,128)S(1)}, f32[2,32,512]{2,1,0:T(8,128)S(1)}, u32[]{:S(2)}, u32[]{:S(2)}) collective-permute-start(f32[2,32,512]{2,1,0:T(8,128)S(1)} %get-tuple-element.77.order), channel_id=1, source_target_pairs={{0,1},{1,0},{2,3},{3,2},{4,5},{5,4},{6,7},{7,6},{8,9},{9,8},{10,11... | collective-permute-start | bytes 393224 | tf_op jit(solution)/shard_map/ppermute | solution.py:545
